TPU v7x, 512 devices: a whole 4x4x16 slice. The times are simulated.
512 devices in a mesh: freq: 8 (over x, core), tile: 64 (over z, y).
Axes of the slice: x: 4, y: 4, z: 16, core: 2. Of those that a mesh axis runs over, the one named last changes fastest.
Arguments:
- model_start: float32 [8, 16384, 128], P('freq', 'tile'), may hold values from -6 to 6
- data: bfloat16 [8, 16384, 128], P('freq', 'tile'), may hold values from -6 to 6
- col_factors: bfloat16 [8, 512, 2, 112, 256], P('freq', 'tile'), may hold values from -0.375 to 0.375
- row_factors: bfloat16 [8, 512, 2, 112, 256], P('freq', 'tile'), may hold values from -0.1875 to 0.1875
- ranks: int32 [8, 64, 8], P('freq'), may hold values from 16 to 112
- gate_window: int32 [64, 2], replicated, may hold values from 0 to 2047, as said below
- step_sizes: float32 [8], P('freq'), may hold values from 0.2 to 0.6
Outputs:
- model_final: float32 [8, 16384, 128], P('freq', 'tile')
Inputs may be any that keep to these rules, and one draw needn't show every extreme that they name: `gate_window`: each row is (start, end) with 256 <= end - start <= 1024.
All inputs are finite; a program needn't handle non-finite values.
Results may differ from a plain program's by a relative error of at most 0.0085.
Values may be sent and summed in bfloat16 or wider, within the bound.
No kernel may reach another device: no remote copies, remote signals or barrier semaphores. Data moves between devices by JAX's collectives and lax.ppermute only.
A program may use at most 64 MiB of HBM per device.

v0:
```python
import math

import jax
import jax.numpy as jnp
from jax import lax
from jax.sharding import PartitionSpec as P

NT = 2048
ITERS = 2


def shifted(value, axis, steps):
    count = lax.axis_size(axis)
    leading, last = (max(0, -steps), min(count, count - steps))
    return lax.ppermute(value, axis, [(source, source + steps) for source in range(leading, last)])


def from_everyone(x, axis):
    length = lax.axis_size(axis)
    return lax.all_to_all(jnp.broadcast_to(x[None], (length, *x.shape)), axis, 0, 0, tiled=True)


def in_order(tiles, dim):
    dims = list(tiles.shape[1:])
    dims[dim] *= tiles.shape[0]
    return jnp.moveaxis(tiles, 0, dim).reshape(dims)


def gather_directly(x, axis, dim):
    tiles = from_everyone(x, axis)
    return in_order(tiles, dim)


def rotate(z):
    half = z.shape[-1] // 2
    return jnp.concatenate([-z[..., half:], z[..., :half]], axis=-1)


def gate_matrix(window, count):
    start = window[:, 0].astype(jnp.float32)
    span = (window[:, 1] - window[:, 0]).astype(jnp.float32)
    freqs = jnp.arange(count, dtype=jnp.float32)
    delta = freqs[:, None] - freqs[None, :]
    theta = 2.0 * math.pi * delta / NT
    safe = jnp.where(delta == 0.0, 1.0, jnp.sin(theta / 2.0))
    magnitude = jnp.where(
        (delta == 0.0)[:, :, None],
        span[None, None, :] / NT,
        jnp.sin(theta[:, :, None] * span[None, None, :] / 2.0) / (NT * safe[:, :, None]),
    )
    phase = theta[:, :, None] * (start[None, None, :] + (span[None, None, :] - 1.0) / 2.0)
    return (magnitude * jnp.cos(phase), magnitude * jnp.sin(phase))


def left_dot(factor, values):
    return lax.dot_general(
        factor, values, (((0,), (0,)), ((), ())), preferred_element_type=jnp.float32
    )


def complex_mix(coeff_re, coeff_im, values):
    width = values.shape[-1] // 2
    vals_re = values[..., :width]
    vals_im = values[..., width:]
    out_re = jnp.sum(coeff_re[:, None, :] * vals_re - coeff_im[:, None, :] * vals_im, axis=0)
    out_im = jnp.sum(coeff_re[:, None, :] * vals_im + coeff_im[:, None, :] * vals_re, axis=0)
    return jnp.concatenate([out_re, out_im], axis=-1)


def forward_send(block, amount):
    return shifted(block, "tile", amount)


def adjoint_send(block, amount):
    return shifted(block, "tile", amount)


def deliver_each(pieces, moves, sender):
    result = []
    for index, amount in enumerate(moves):
        if amount == 0:
            result.append(pieces[index])
        else:
            result.append(sender(pieces[index], amount))
    return result


def on_device(model_start, data, col_factors, row_factors, ranks, gate_window, step_sizes):
    ntile = lax.axis_size("tile")
    nfreq = lax.axis_size("freq")
    myself = lax.axis_index("tile")
    my_freq = lax.axis_index("freq")
    slots = ranks.shape[2]
    levels = col_factors.shape[3]
    tile_rows = col_factors.shape[4]
    center = slots // 2
    moves = [index - center for index in range(slots)]
    backward = [-amount for amount in moves]
    factors_v = col_factors[0]
    factors_u = row_factors[0]
    v_real = factors_v[:, 0].reshape(slots * levels, tile_rows)
    v_imag = factors_v[:, 1].reshape(slots * levels, tile_rows)
    u_real = factors_u[:, 0].reshape(slots * levels, tile_rows)
    u_imag = factors_u[:, 1].reshape(slots * levels, tile_rows)
    rank_table = ranks[0]
    devices = jnp.arange(ntile, dtype=jnp.int32)
    anchors = myself - (jnp.arange(slots, dtype=jnp.int32) - center)
    holder = devices[:, None] == anchors[None, :]
    row_ranks = jnp.sum(jnp.where(holder, rank_table, 0), axis=0)
    my_ranks = lax.dynamic_index_in_dim(rank_table, myself, 0, keepdims=False)
    level_ids = jnp.arange(levels, dtype=jnp.int32)
    col_mask = (level_ids[None, :] < my_ranks[:, None]).astype(jnp.float32)
    row_mask = (level_ids[None, :] < row_ranks[:, None]).astype(jnp.float32)
    gate_re, gate_im = gate_matrix(gate_window, nfreq)
    stepping = step_sizes[0]
    model = model_start[0]
    observed = data[0].astype(jnp.float32)
    width = model.shape[-1]
    for step in range(ITERS):
        model_bf = model.astype(jnp.bfloat16)
        coef = jnp.dot(v_real, model_bf, preferred_element_type=jnp.float32) + jnp.dot(
            v_imag, rotate(model_bf), preferred_element_type=jnp.float32
        )
        coef = (coef.reshape(slots, levels, width) * col_mask[:, :, None]).astype(jnp.bfloat16)
        outgoing = [coef[index] for index in range(slots)]
        arrived = deliver_each(outgoing, moves, forward_send)
        placed = jnp.stack(arrived).reshape(slots * levels, width)
        image = left_dot(u_real, placed) + left_dot(u_imag, rotate(placed))
        resid = (image - observed).astype(jnp.bfloat16)
        return_trip = jnp.dot(u_real, resid, preferred_element_type=jnp.float32) - jnp.dot(
            u_imag, rotate(resid), preferred_element_type=jnp.float32
        )
        return_trip = (return_trip.reshape(slots, levels, width) * row_mask[:, :, None]).astype(
            jnp.bfloat16
        )
        sending = [return_trip[index] for index in range(slots)]
        landed = deliver_each(sending, backward, adjoint_send)
        gathered = jnp.stack(landed).reshape(slots * levels, width)
        grad = left_dot(v_real, gathered) - left_dot(v_imag, rotate(gathered))
        updated = model - stepping * grad
        row_re = lax.dynamic_index_in_dim(gate_re, my_freq, 0, keepdims=False)
        row_im = lax.dynamic_index_in_dim(gate_im, my_freq, 0, keepdims=False)
        model = complex_mix(row_re, row_im, gather_directly(updated[None], "freq", 0))
    return model[None]


def solution(mesh):
    return jax.shard_map(
        on_device,
        mesh=mesh,
        in_specs=(
            P("freq", "tile", None),
            P("freq", "tile", None),
            P("freq", "tile", None, None, None),
            P("freq", "tile", None, None, None),
            P("freq", None, None),
            P(),
            P("freq"),
        ),
        out_specs=P("freq", "tile", None),
        check_vma=False,
    )
```

profile of v0, /device:TPU:368, one launch (start us, length us, event | category | flops | bytes accessed | tf_op | source)
XLA Modules:
  0.0 181.9 jit_solution(14817962775073350224)
XLA Ops:
  6.1 3.6 %collective-permute-start.1 = (bf16[112,128]{1,0:T(8,128)(2,1)S(1)}, bf16[112,128]{1,0:T(8,128)(2,1)S(1)}, u32[]{:S(2)}, u32[]{:S(2)}) collective-permute-start(bf16[112,128]{1,0:T(8,128)(2,1)S(1)} %get-tuple-element.53), channel_id=1, source_target_pairs={{3,0},{4,1},{5,2},{6,3},{7,4},{8,5},{9,6},{10,7},{11,8},{12,9},{13... | collective-permute-start | bytes 86024 | tf_op jit(solution)/shard_map/ppermute | solution.py:15
  15.5 3.5 %collective-permute-done.2 = bf16[112,128]{1,0:T(8,128)(2,1)S(1)} collective-permute-done((bf16[112,128]{1,0:T(8,128)(2,1)S(1)}, bf16[112,128]{1,0:T(8,128)(2,1)S(1)}, u32[]{:S(2)}, u32[]{:S(2)}) %collective-permute-start.2) | collective-permute-done | bytes 28704 | tf_op jit(solution)/shard_map/ppermute | solution.py:15
  19.1 6.3 %collective-permute-start.4 = (bf16[112,128]{1,0:T(8,128)(2,1)S(1)}, bf16[112,128]{1,0:T(8,128)(2,1)S(1)}, u32[]{:S(2)}, u32[]{:S(2)}) collective-permute-start(bf16[112,128]{1,0:T(8,128)(2,1)S(1)} %get-tuple-element.49), channel_id=1, source_target_pairs={{0,1},{1,2},{2,3},{3,4},{4,5},{5,6},{6,7},{7,8},{8,9},{9,10},{10,1... | collective-permute-start | bytes 86024 | tf_op jit(solution)/shard_map/ppermute | solution.py:15
  27.6 4.5 %collective-permute-start.6 = (bf16[112,128]{1,0:T(8,128)(2,1)S(1)}, bf16[112,128]{1,0:T(8,128)(2,1)S(1)}, u32[]{:S(2)}, u32[]{:S(2)}) collective-permute-start(bf16[112,128]{1,0:T(8,128)(2,1)S(1)} %get-tuple-element.47), channel_id=1, source_target_pairs={{0,3},{1,4},{2,5},{3,6},{4,7},{5,8},{6,9},{7,10},{8,11},{9,12},{10... | collective-permute-start | bytes 86024 | tf_op jit(solution)/shard_map/ppermute | solution.py:15
  36.1 4.1 %collective-permute-start.7 = (bf16[112,128]{1,0:T(8,128)(2,1)S(1)}, bf16[112,128]{1,0:T(8,128)(2,1)S(1)}, u32[]{:S(2)}, u32[]{:S(2)}) collective-permute-start(bf16[112,128]{1,0:T(8,128)(2,1)S(1)} %get-tuple-element.44), channel_id=1, source_target_pairs={{0,4},{1,5},{2,6},{3,7},{4,8},{5,9},{6,10},{7,11},{8,12},{9,13},{1... | collective-permute-start | bytes 86024 | tf_op jit(solution)/shard_map/ppermute | solution.py:15
  40.2 3.5 %collective-permute-start.8 = (bf16[112,128]{1,0:T(8,128)(2,1)S(1)}, bf16[112,128]{1,0:T(8,128)(2,1)S(1)}, u32[]{:S(2)}, u32[]{:S(2)}) collective-permute-start(bf16[112,128]{1,0:T(8,128)(2,1)S(1)} %get-tuple-element.43), channel_id=1, source_target_pairs={{0,3},{1,4},{2,5},{3,6},{4,7},{5,8},{6,9},{7,10},{8,11},{9,12},{10... | collective-permute-start | bytes 86024 | tf_op jit(solution)/shard_map/ppermute | solution.py:15
  43.7 3.4 %collective-permute-start.9 = (bf16[112,128]{1,0:T(8,128)(2,1)S(1)}, bf16[112,128]{1,0:T(8,128)(2,1)S(1)}, u32[]{:S(2)}, u32[]{:S(2)}) collective-permute-start(bf16[112,128]{1,0:T(8,128)(2,1)S(1)} %get-tuple-element.42), channel_id=1, source_target_pairs={{0,2},{1,3},{2,4},{3,5},{4,6},{5,7},{6,8},{7,9},{8,10},{9,11},{10,... | collective-permute-start | bytes 86024 | tf_op jit(solution)/shard_map/ppermute | solution.py:15
  47.1 3.7 %collective-permute-start.10 = (bf16[112,128]{1,0:T(8,128)(2,1)S(1)}, bf16[112,128]{1,0:T(8,128)(2,1)S(1)}, u32[]{:S(2)}, u32[]{:S(2)}) collective-permute-start(bf16[112,128]{1,0:T(8,128)(2,1)S(1)} %get-tuple-element.41), channel_id=1, source_target_pairs={{0,1},{1,2},{2,3},{3,4},{4,5},{5,6},{6,7},{7,8},{8,9},{9,10},{10,1... | collective-permute-start | bytes 86024 | tf_op jit(solution)/shard_map/ppermute | solution.py:15
  56.5 6.3 %collective-permute-start.12 = (bf16[112,128]{1,0:T(8,128)(2,1)S(1)}, bf16[112,128]{1,0:T(8,128)(2,1)S(1)}, u32[]{:S(2)}, u32[]{:S(2)}) collective-permute-start(bf16[112,128]{1,0:T(8,128)(2,1)S(1)} %get-tuple-element.38), channel_id=1, source_target_pairs={{2,0},{3,1},{4,2},{5,3},{6,4},{7,5},{8,6},{9,7},{10,8},{11,9},{12,... | collective-permute-start | bytes 86024 | tf_op jit(solution)/shard_map/ppermute | solution.py:15
  62.9 4.6 %collective-permute-start.13 = (bf16[112,128]{1,0:T(8,128)(2,1)S(1)}, bf16[112,128]{1,0:T(8,128)(2,1)S(1)}, u32[]{:S(2)}, u32[]{:S(2)}) collective-permute-start(bf16[112,128]{1,0:T(8,128)(2,1)S(1)} %get-tuple-element.37), channel_id=1, source_target_pairs={{3,0},{4,1},{5,2},{6,3},{7,4},{8,5},{9,6},{10,7},{11,8},{12,9},{13... | collective-permute-start | bytes 86024 | tf_op jit(solution)/shard_map/ppermute | solution.py:15
  67.6 3.2 %collective-permute-done.13 = bf16[112,128]{1,0:T(8,128)(2,1)S(1)} collective-permute-done((bf16[112,128]{1,0:T(8,128)(2,1)S(1)}, bf16[112,128]{1,0:T(8,128)(2,1)S(1)}, u32[]{:S(2)}, u32[]{:S(2)}) %collective-permute-start.13) | collective-permute-done | bytes 28704 | tf_op jit(solution)/shard_map/ppermute | solution.py:15
  72.7 4.3 %all-to-all-start = ((f32[8,1,256,128]{3,2,1,0:T(8,128)}), f32[8,1,256,128]{3,2,1,0:T(8,128)S(1)}, u32[]{:S(2)}, u32[]{:S(2)}) async-start(f32[8,1,256,128]{3,2,1,0:T(8,128)} %broadcast_in_dim.34), calls=%async_computation | async-start | bytes 2097152 | tf_op jit(solution)/shard_map/all_to_all | solution.py:20
  78.0 15.0 %all-to-all-done = f32[8,1,256,128]{3,2,1,0:T(8,128)S(1)} async-done(((f32[8,1,256,128]{3,2,1,0:T(8,128)}), f32[8,1,256,128]{3,2,1,0:T(8,128)S(1)}, u32[]{:S(2)}, u32[]{:S(2)}) %all-to-all-start) | async-done | bytes 1048608 | tf_op jit(solution)/shard_map/all_to_all | solution.py:20
  101.9 3.7 %collective-permute-start.17 = (bf16[112,128]{1,0:T(8,128)(2,1)S(1)}, bf16[112,128]{1,0:T(8,128)(2,1)S(1)}, u32[]{:S(2)}, u32[]{:S(2)}) collective-permute-start(bf16[112,128]{1,0:T(8,128)(2,1)S(1)} %get-tuple-element.31), channel_id=1, source_target_pairs={{1,0},{2,1},{3,2},{4,3},{5,4},{6,5},{7,6},{8,7},{9,8},{10,9},{11,1... | collective-permute-start | bytes 86024 | tf_op jit(solution)/shard_map/ppermute | solution.py:15
  105.7 3.7 %collective-permute-done.16 = bf16[112,128]{1,0:T(8,128)(2,1)S(1)} collective-permute-done((bf16[112,128]{1,0:T(8,128)(2,1)S(1)}, bf16[112,128]{1,0:T(8,128)(2,1)S(1)}, u32[]{:S(2)}, u32[]{:S(2)}) %collective-permute-start.16) | collective-permute-done | bytes 28704 | tf_op jit(solution)/shard_map/ppermute | solution.py:15
  109.4 6.3 %collective-permute-start.18 = (bf16[112,128]{1,0:T(8,128)(2,1)S(1)}, bf16[112,128]{1,0:T(8,128)(2,1)S(1)}, u32[]{:S(2)}, u32[]{:S(2)}) collective-permute-start(bf16[112,128]{1,0:T(8,128)(2,1)S(1)} %get-tuple-element.29), channel_id=1, source_target_pairs={{0,1},{1,2},{2,3},{3,4},{4,5},{5,6},{6,7},{7,8},{8,9},{9,10},{10,1... | collective-permute-start | bytes 86024 | tf_op jit(solution)/shard_map/ppermute | solution.py:15
  117.7 5.5 %collective-permute-start.20 = (bf16[112,128]{1,0:T(8,128)(2,1)S(1)}, bf16[112,128]{1,0:T(8,128)(2,1)S(1)}, u32[]{:S(2)}, u32[]{:S(2)}) collective-permute-start(bf16[112,128]{1,0:T(8,128)(2,1)S(1)} %get-tuple-element.27), channel_id=1, source_target_pairs={{0,3},{1,4},{2,5},{3,6},{4,7},{5,8},{6,9},{7,10},{8,11},{9,12},{10... | collective-permute-start | bytes 86024 | tf_op jit(solution)/shard_map/ppermute | solution.py:15
  126.5 4.8 %collective-permute-start.21 = (bf16[112,128]{1,0:T(8,128)(2,1)S(1)}, bf16[112,128]{1,0:T(8,128)(2,1)S(1)}, u32[]{:S(2)}, u32[]{:S(2)}) collective-permute-start(bf16[112,128]{1,0:T(8,128)(2,1)S(1)} %get-tuple-element.24), channel_id=1, source_target_pairs={{0,4},{1,5},{2,6},{3,7},{4,8},{5,9},{6,10},{7,11},{8,12},{9,13},{1... | collective-permute-start | bytes 86024 | tf_op jit(solution)/shard_map/ppermute | solution.py:15
  131.3 3.5 %collective-permute-start.22 = (bf16[112,128]{1,0:T(8,128)(2,1)S(1)}, bf16[112,128]{1,0:T(8,128)(2,1)S(1)}, u32[]{:S(2)}, u32[]{:S(2)}) collective-permute-start(bf16[112,128]{1,0:T(8,128)(2,1)S(1)} %get-tuple-element.23), channel_id=1, source_target_pairs={{0,3},{1,4},{2,5},{3,6},{4,7},{5,8},{6,9},{7,10},{8,11},{9,12},{10... | collective-permute-start | bytes 86024 | tf_op jit(solution)/shard_map/ppermute | solution.py:15
  134.8 3.6 %collective-permute-start.23 = (bf16[112,128]{1,0:T(8,128)(2,1)S(1)}, bf16[112,128]{1,0:T(8,128)(2,1)S(1)}, u32[]{:S(2)}, u32[]{:S(2)}) collective-permute-start(bf16[112,128]{1,0:T(8,128)(2,1)S(1)} %get-tuple-element.22), channel_id=1, source_target_pairs={{0,2},{1,3},{2,4},{3,5},{4,6},{5,7},{6,8},{7,9},{8,10},{9,11},{10,... | collective-permute-start | bytes 86024 | tf_op jit(solution)/shard_map/ppermute | solution.py:15
  138.4 3.7 %collective-permute-start.24 = (bf16[112,128]{1,0:T(8,128)(2,1)S(1)}, bf16[112,128]{1,0:T(8,128)(2,1)S(1)}, u32[]{:S(2)}, u32[]{:S(2)}) collective-permute-start(bf16[112,128]{1,0:T(8,128)(2,1)S(1)} %get-tuple-element.21), channel_id=1, source_target_pairs={{0,1},{1,2},{2,3},{3,4},{4,5},{5,6},{6,7},{7,8},{8,9},{9,10},{10,1... | collective-permute-start | bytes 86024 | tf_op jit(solution)/shard_map/ppermute | solution.py:15
  147.0 6.3 %collective-permute-start.26 = (bf16[112,128]{1,0:T(8,128)(2,1)S(1)}, bf16[112,128]{1,0:T(8,128)(2,1)S(1)}, u32[]{:S(2)}, u32[]{:S(2)}) collective-permute-start(bf16[112,128]{1,0:T(8,128)(2,1)S(1)} %get-tuple-element.18), channel_id=1, source_target_pairs={{2,0},{3,1},{4,2},{5,3},{6,4},{7,5},{8,6},{9,7},{10,8},{11,9},{12,... | collective-permute-start | bytes 86024 | tf_op jit(solution)/shard_map/ppermute | solution.py:15
  153.3 4.6 %collective-permute-start.27 = (bf16[112,128]{1,0:T(8,128)(2,1)S(1)}, bf16[112,128]{1,0:T(8,128)(2,1)S(1)}, u32[]{:S(2)}, u32[]{:S(2)}) collective-permute-start(bf16[112,128]{1,0:T(8,128)(2,1)S(1)} %get-tuple-element.17), channel_id=1, source_target_pairs={{3,0},{4,1},{5,2},{6,3},{7,4},{8,5},{9,6},{10,7},{11,8},{12,9},{13... | collective-permute-start | bytes 86024 | tf_op jit(solution)/shard_map/ppermute | solution.py:15
  162.2 18.5 %all_to_all.10 = f32[8,1,256,128]{3,2,1,0:T(8,128)S(1)} all-to-all(f32[8,1,256,128]{3,2,1,0:T(8,128)S(1)} %broadcast_in_dim.35), channel_id=1, replica_groups=mesh['freq'=8,'tile'=64] {'freq'}, dimensions={0} | all-to-all | bytes 2097152 | tf_op jit(solution)/shard_map/all_to_all | solution.py:20
  (138 shorter events, 50.0 us)
Async XLA Ops:
  3.1 12.4 %collective-permute-start = (bf16[112,128]{1,0:T(8,128)(2,1)S(1)}, bf16[112,128]{1,0:T(8,128)(2,1)S(1)}, u32[]{:S(2)}, u32[]{:S(2)}) collective-permute-start(bf16[112,128]{1,0:T(8,128)(2,1)S(1)} %get-tuple-element.54), channel_id=1, source_target_pairs={{4,0},{5,1},{6,2},{7,3},{8,4},{9,5},{10,6},{11,7},{12,8},{13,9},{1... | collective-permute-start | bytes 86024 | tf_op jit(solution)/shard_map/ppermute | solution.py:15
  6.1 9.4 %collective-permute-start.1 = (bf16[112,128]{1,0:T(8,128)(2,1)S(1)}, bf16[112,128]{1,0:T(8,128)(2,1)S(1)}, u32[]{:S(2)}, u32[]{:S(2)}) collective-permute-start(bf16[112,128]{1,0:T(8,128)(2,1)S(1)} %get-tuple-element.53), channel_id=1, source_target_pairs={{3,0},{4,1},{5,2},{6,3},{7,4},{8,5},{9,6},{10,7},{11,8},{12,9},{13... | collective-permute-start | bytes 86024 | tf_op jit(solution)/shard_map/ppermute | solution.py:15
  9.7 9.4 %collective-permute-start.2 = (bf16[112,128]{1,0:T(8,128)(2,1)S(1)}, bf16[112,128]{1,0:T(8,128)(2,1)S(1)}, u32[]{:S(2)}, u32[]{:S(2)}) collective-permute-start(bf16[112,128]{1,0:T(8,128)(2,1)S(1)} %get-tuple-element.52), channel_id=1, source_target_pairs={{2,0},{3,1},{4,2},{5,3},{6,4},{7,5},{8,6},{9,7},{10,8},{11,9},{12,... | collective-permute-start | bytes 86024 | tf_op jit(solution)/shard_map/ppermute | solution.py:15
  19.1 12.9 %collective-permute-start.4 = (bf16[112,128]{1,0:T(8,128)(2,1)S(1)}, bf16[112,128]{1,0:T(8,128)(2,1)S(1)}, u32[]{:S(2)}, u32[]{:S(2)}) collective-permute-start(bf16[112,128]{1,0:T(8,128)(2,1)S(1)} %get-tuple-element.49), channel_id=1, source_target_pairs={{0,1},{1,2},{2,3},{3,4},{4,5},{5,6},{6,7},{7,8},{8,9},{9,10},{10,1... | collective-permute-start | bytes 86024 | tf_op jit(solution)/shard_map/ppermute | solution.py:15
  25.6 7.3 %collective-permute-start.5 = (bf16[112,128]{1,0:T(8,128)(2,1)S(1)}, bf16[112,128]{1,0:T(8,128)(2,1)S(1)}, u32[]{:S(2)}, u32[]{:S(2)}) collective-permute-start(bf16[112,128]{1,0:T(8,128)(2,1)S(1)} %get-tuple-element.48), channel_id=1, source_target_pairs={{0,2},{1,3},{2,4},{3,5},{4,6},{5,7},{6,8},{7,9},{8,10},{9,11},{10,... | collective-permute-start | bytes 86024 | tf_op jit(solution)/shard_map/ppermute | solution.py:15
  36.1 14.7 %collective-permute-start.7 = (bf16[112,128]{1,0:T(8,128)(2,1)S(1)}, bf16[112,128]{1,0:T(8,128)(2,1)S(1)}, u32[]{:S(2)}, u32[]{:S(2)}) collective-permute-start(bf16[112,128]{1,0:T(8,128)(2,1)S(1)} %get-tuple-element.44), channel_id=1, source_target_pairs={{0,4},{1,5},{2,6},{3,7},{4,8},{5,9},{6,10},{7,11},{8,12},{9,13},{1... | collective-permute-start | bytes 86024 | tf_op jit(solution)/shard_map/ppermute | solution.py:15
  40.2 10.6 %collective-permute-start.8 = (bf16[112,128]{1,0:T(8,128)(2,1)S(1)}, bf16[112,128]{1,0:T(8,128)(2,1)S(1)}, u32[]{:S(2)}, u32[]{:S(2)}) collective-permute-start(bf16[112,128]{1,0:T(8,128)(2,1)S(1)} %get-tuple-element.43), channel_id=1, source_target_pairs={{0,3},{1,4},{2,5},{3,6},{4,7},{5,8},{6,9},{7,10},{8,11},{9,12},{10... | collective-permute-start | bytes 86024 | tf_op jit(solution)/shard_map/ppermute | solution.py:15
  43.7 7.3 %collective-permute-start.9 = (bf16[112,128]{1,0:T(8,128)(2,1)S(1)}, bf16[112,128]{1,0:T(8,128)(2,1)S(1)}, u32[]{:S(2)}, u32[]{:S(2)}) collective-permute-start(bf16[112,128]{1,0:T(8,128)(2,1)S(1)} %get-tuple-element.42), channel_id=1, source_target_pairs={{0,2},{1,3},{2,4},{3,5},{4,6},{5,7},{6,8},{7,9},{8,10},{9,11},{10,... | collective-permute-start | bytes 86024 | tf_op jit(solution)/shard_map/ppermute | solution.py:15
  52.9 14.6 %collective-permute-start.11 = (bf16[112,128]{1,0:T(8,128)(2,1)S(1)}, bf16[112,128]{1,0:T(8,128)(2,1)S(1)}, u32[]{:S(2)}, u32[]{:S(2)}) collective-permute-start(bf16[112,128]{1,0:T(8,128)(2,1)S(1)} %get-tuple-element.39), channel_id=1, source_target_pairs={{1,0},{2,1},{3,2},{4,3},{5,4},{6,5},{7,6},{8,7},{9,8},{10,9},{11,1... | collective-permute-start | bytes 86024 | tf_op jit(solution)/shard_map/ppermute | solution.py:15
  56.5 11.0 %collective-permute-start.12 = (bf16[112,128]{1,0:T(8,128)(2,1)S(1)}, bf16[112,128]{1,0:T(8,128)(2,1)S(1)}, u32[]{:S(2)}, u32[]{:S(2)}) collective-permute-start(bf16[112,128]{1,0:T(8,128)(2,1)S(1)} %get-tuple-element.38), channel_id=1, source_target_pairs={{2,0},{3,1},{4,2},{5,3},{6,4},{7,5},{8,6},{9,7},{10,8},{11,9},{12,... | collective-permute-start | bytes 86024 | tf_op jit(solution)/shard_map/ppermute | solution.py:15
  62.9 7.9 %collective-permute-start.13 = (bf16[112,128]{1,0:T(8,128)(2,1)S(1)}, bf16[112,128]{1,0:T(8,128)(2,1)S(1)}, u32[]{:S(2)}, u32[]{:S(2)}) collective-permute-start(bf16[112,128]{1,0:T(8,128)(2,1)S(1)} %get-tuple-element.37), channel_id=1, source_target_pairs={{3,0},{4,1},{5,2},{6,3},{7,4},{8,5},{9,6},{10,7},{11,8},{12,9},{13... | collective-permute-start | bytes 86024 | tf_op jit(solution)/shard_map/ppermute | solution.py:15
  72.7 20.3 %all-to-all-start = ((f32[8,1,256,128]{3,2,1,0:T(8,128)}), f32[8,1,256,128]{3,2,1,0:T(8,128)S(1)}, u32[]{:S(2)}, u32[]{:S(2)}) async-start(f32[8,1,256,128]{3,2,1,0:T(8,128)} %broadcast_in_dim.34), calls=%async_computation | async-start | bytes 2097152 | tf_op jit(solution)/shard_map/all_to_all | solution.py:20
  94.6 11.0 %collective-permute-start.14 = (bf16[112,128]{1,0:T(8,128)(2,1)S(1)}, bf16[112,128]{1,0:T(8,128)(2,1)S(1)}, u32[]{:S(2)}, u32[]{:S(2)}) collective-permute-start(bf16[112,128]{1,0:T(8,128)(2,1)S(1)} %get-tuple-element.34), channel_id=1, source_target_pairs={{4,0},{5,1},{6,2},{7,3},{8,4},{9,5},{10,6},{11,7},{12,8},{13,9},{1... | collective-permute-start | bytes 86024 | tf_op jit(solution)/shard_map/ppermute | solution.py:15
  97.3 8.3 %collective-permute-start.15 = (bf16[112,128]{1,0:T(8,128)(2,1)S(1)}, bf16[112,128]{1,0:T(8,128)(2,1)S(1)}, u32[]{:S(2)}, u32[]{:S(2)}) collective-permute-start(bf16[112,128]{1,0:T(8,128)(2,1)S(1)} %get-tuple-element.33), channel_id=1, source_target_pairs={{3,0},{4,1},{5,2},{6,3},{7,4},{8,5},{9,6},{10,7},{11,8},{12,9},{13... | collective-permute-start | bytes 86024 | tf_op jit(solution)/shard_map/ppermute | solution.py:15
  100.0 9.4 %collective-permute-start.16 = (bf16[112,128]{1,0:T(8,128)(2,1)S(1)}, bf16[112,128]{1,0:T(8,128)(2,1)S(1)}, u32[]{:S(2)}, u32[]{:S(2)}) collective-permute-start(bf16[112,128]{1,0:T(8,128)(2,1)S(1)} %get-tuple-element.32), channel_id=1, source_target_pairs={{2,0},{3,1},{4,2},{5,3},{6,4},{7,5},{8,6},{9,7},{10,8},{11,9},{12,... | collective-permute-start | bytes 86024 | tf_op jit(solution)/shard_map/ppermute | solution.py:15
  101.9 7.5 %collective-permute-start.17 = (bf16[112,128]{1,0:T(8,128)(2,1)S(1)}, bf16[112,128]{1,0:T(8,128)(2,1)S(1)}, u32[]{:S(2)}, u32[]{:S(2)}) collective-permute-start(bf16[112,128]{1,0:T(8,128)(2,1)S(1)} %get-tuple-element.31), channel_id=1, source_target_pairs={{1,0},{2,1},{3,2},{4,3},{5,4},{6,5},{7,6},{8,7},{9,8},{10,9},{11,1... | collective-permute-start | bytes 86024 | tf_op jit(solution)/shard_map/ppermute | solution.py:15
  109.4 13.8 %collective-permute-start.18 = (bf16[112,128]{1,0:T(8,128)(2,1)S(1)}, bf16[112,128]{1,0:T(8,128)(2,1)S(1)}, u32[]{:S(2)}, u32[]{:S(2)}) collective-permute-start(bf16[112,128]{1,0:T(8,128)(2,1)S(1)} %get-tuple-element.29), channel_id=1, source_target_pairs={{0,1},{1,2},{2,3},{3,4},{4,5},{5,6},{6,7},{7,8},{8,9},{9,10},{10,1... | collective-permute-start | bytes 86024 | tf_op jit(solution)/shard_map/ppermute | solution.py:15
  115.7 7.5 %collective-permute-start.19 = (bf16[112,128]{1,0:T(8,128)(2,1)S(1)}, bf16[112,128]{1,0:T(8,128)(2,1)S(1)}, u32[]{:S(2)}, u32[]{:S(2)}) collective-permute-start(bf16[112,128]{1,0:T(8,128)(2,1)S(1)} %get-tuple-element.28), channel_id=1, source_target_pairs={{0,2},{1,3},{2,4},{3,5},{4,6},{5,7},{6,8},{7,9},{8,10},{9,11},{10,... | collective-permute-start | bytes 86024 | tf_op jit(solution)/shard_map/ppermute | solution.py:15
  126.5 15.6 %collective-permute-start.21 = (bf16[112,128]{1,0:T(8,128)(2,1)S(1)}, bf16[112,128]{1,0:T(8,128)(2,1)S(1)}, u32[]{:S(2)}, u32[]{:S(2)}) collective-permute-start(bf16[112,128]{1,0:T(8,128)(2,1)S(1)} %get-tuple-element.24), channel_id=1, source_target_pairs={{0,4},{1,5},{2,6},{3,7},{4,8},{5,9},{6,10},{7,11},{8,12},{9,13},{1... | collective-permute-start | bytes 86024 | tf_op jit(solution)/shard_map/ppermute | solution.py:15
  131.3 10.8 %collective-permute-start.22 = (bf16[112,128]{1,0:T(8,128)(2,1)S(1)}, bf16[112,128]{1,0:T(8,128)(2,1)S(1)}, u32[]{:S(2)}, u32[]{:S(2)}) collective-permute-start(bf16[112,128]{1,0:T(8,128)(2,1)S(1)} %get-tuple-element.23), channel_id=1, source_target_pairs={{0,3},{1,4},{2,5},{3,6},{4,7},{5,8},{6,9},{7,10},{8,11},{9,12},{10... | collective-permute-start | bytes 86024 | tf_op jit(solution)/shard_map/ppermute | solution.py:15
  134.8 7.4 %collective-permute-start.23 = (bf16[112,128]{1,0:T(8,128)(2,1)S(1)}, bf16[112,128]{1,0:T(8,128)(2,1)S(1)}, u32[]{:S(2)}, u32[]{:S(2)}) collective-permute-start(bf16[112,128]{1,0:T(8,128)(2,1)S(1)} %get-tuple-element.22), channel_id=1, source_target_pairs={{0,2},{1,3},{2,4},{3,5},{4,6},{5,7},{6,8},{7,9},{8,10},{9,11},{10,... | collective-permute-start | bytes 86024 | tf_op jit(solution)/shard_map/ppermute | solution.py:15
  144.2 13.8 %collective-permute-start.25 = (bf16[112,128]{1,0:T(8,128)(2,1)S(1)}, bf16[112,128]{1,0:T(8,128)(2,1)S(1)}, u32[]{:S(2)}, u32[]{:S(2)}) collective-permute-start(bf16[112,128]{1,0:T(8,128)(2,1)S(1)} %get-tuple-element.19), channel_id=1, source_target_pairs={{1,0},{2,1},{3,2},{4,3},{5,4},{6,5},{7,6},{8,7},{9,8},{10,9},{11,1... | collective-permute-start | bytes 86024 | tf_op jit(solution)/shard_map/ppermute | solution.py:15
  147.0 11.0 %collective-permute-start.26 = (bf16[112,128]{1,0:T(8,128)(2,1)S(1)}, bf16[112,128]{1,0:T(8,128)(2,1)S(1)}, u32[]{:S(2)}, u32[]{:S(2)}) collective-permute-start(bf16[112,128]{1,0:T(8,128)(2,1)S(1)} %get-tuple-element.18), channel_id=1, source_target_pairs={{2,0},{3,1},{4,2},{5,3},{6,4},{7,5},{8,6},{9,7},{10,8},{11,9},{12,... | collective-permute-start | bytes 86024 | tf_op jit(solution)/shard_map/ppermute | solution.py:15
  153.3 7.9 %collective-permute-start.27 = (bf16[112,128]{1,0:T(8,128)(2,1)S(1)}, bf16[112,128]{1,0:T(8,128)(2,1)S(1)}, u32[]{:S(2)}, u32[]{:S(2)}) collective-permute-start(bf16[112,128]{1,0:T(8,128)(2,1)S(1)} %get-tuple-element.17), channel_id=1, source_target_pairs={{3,0},{4,1},{5,2},{6,3},{7,4},{8,5},{9,6},{10,7},{11,8},{12,9},{13... | collective-permute-start | bytes 86024 | tf_op jit(solution)/shard_map/ppermute | solution.py:15
  (10 other events, 53.7 us)
where the time goes:
time: 183 us; the launch traced here: 182 us
  starting transfers between devices  112 us (61%)
  waiting for transfers between devices  36.3 us (20%)
  blocking collectives  18.5 us (10%)
  local copies, waits for them, and re-layouts  5.42 us (3%)
  matrix products  4.86 us (3%)
  other arithmetic  3.59 us (2%)
    ppermute x28, starting transfers between devices, shifted(): lax.ppermute(value, axis, [(source, source + steps) for source in range(l...  107 us
    ppermute x28, waiting for transfers between devices, shifted(): lax.ppermute(value, axis, [(source, source + steps) for source in range(l...  21.3 us
    all_to_all x1, blocking collectives, from_everyone(): lax.all_to_all(jnp.broadcast_to(x[None], (length, *x.shape)), axis, 0, 0,...  18.5 us
    all_to_all x1, waiting for transfers between devices, from_everyone(): lax.all_to_all(jnp.broadcast_to(x[None], (length, *x.shape)), axis, 0, 0,...  15 us
    all_to_all x1, starting transfers between devices, from_everyone(): lax.all_to_all(jnp.broadcast_to(x[None], (length, *x.shape)), axis, 0, 0,...  4.3 us
  transfers between devices with their start and end apart: 29, of which 11 were waited for; matrix products, arithmetic and copies ran while one was open for 1% of the time, Pallas kernels for 0%

commit v1 on v0

v1 whole, which is shorter than its diff:
```python
import math

import jax
import jax.numpy as jnp
from jax import lax
from jax.sharding import PartitionSpec as P

NT = 2048
ITERS = 2
WIDE = 4


def rotate(z):
    half = z.shape[-1] // 2
    return jnp.concatenate([-z[..., half:], z[..., :half]], axis=-1)


def gate_matrix(window, count):
    start = window[:, 0].astype(jnp.float32)
    span = (window[:, 1] - window[:, 0]).astype(jnp.float32)
    freqs = jnp.arange(count, dtype=jnp.float32)
    delta = freqs[:, None] - freqs[None, :]
    theta = 2.0 * math.pi * delta / NT
    safe = jnp.where(delta == 0.0, 1.0, jnp.sin(theta / 2.0))
    magnitude = jnp.where(
        (delta == 0.0)[:, :, None],
        span[None, None, :] / NT,
        jnp.sin(theta[:, :, None] * span[None, None, :] / 2.0) / (NT * safe[:, :, None]),
    )
    phase = theta[:, :, None] * (start[None, None, :] + (span[None, None, :] - 1.0) / 2.0)
    return (magnitude * jnp.cos(phase), magnitude * jnp.sin(phase))


def left_dot(factor, values):
    return lax.dot_general(
        factor, values, (((0,), (0,)), ((), ())), preferred_element_type=jnp.float32
    )


def complex_mix(coeff_re, coeff_im, values):
    values = values.astype(jnp.float32)
    width = values.shape[-1] // 2
    vals_re = values[..., :width]
    vals_im = values[..., width:]
    out_re = jnp.sum(coeff_re[:, None, :] * vals_re - coeff_im[:, None, :] * vals_im, axis=0)
    out_im = jnp.sum(coeff_re[:, None, :] * vals_im + coeff_im[:, None, :] * vals_re, axis=0)
    return jnp.concatenate([out_re, out_im], axis=-1)


def on_device(model_start, data, col_factors, row_factors, ranks, gate_window, step_sizes):
    ntile = lax.axis_size("tile")
    nfreq = lax.axis_size("freq")
    myself = lax.axis_index("tile")
    my_freq = lax.axis_index("freq")
    slots = ranks.shape[2]
    levels = col_factors.shape[3]
    half = slots // 2
    rows_z = ntile // WIDE
    col = myself % WIDE
    odd = (myself // WIDE) % 2 == 1
    groups = [[slots * k + i for i in range(slots)] for k in range(ntile // slots)]
    swaps = [
        (z * WIDE + y, (z + 1 if z % 2 else z - 1) * WIDE + y)
        for z in range(1, rows_z - 1)
        for y in range(WIDE)
    ]

    def swap(value):
        return lax.ppermute(value, "tile", swaps)

    def spread(own, forwarded):
        send = jnp.stack([own, jnp.concatenate([forwarded, forwarded])], axis=1)
        got = lax.all_to_all(send, "tile", 0, 0, tiled=True, axis_index_groups=groups)
        return got[:, 0], got[:, 1]

    def by_parity(same, cross):
        return jnp.where(
            odd, jnp.concatenate([cross, same]), jnp.concatenate([same, cross])
        )

    def cross_half(pieces):
        return jnp.where(odd, pieces[:half], pieces[half:])

    def same_half(pieces):
        return jnp.where(odd, pieces[half:], pieces[:half])

    def in_order(table, start_same, start_cross):
        twice = jnp.concatenate([table, table])
        same = lax.dynamic_slice_in_dim(table, start_same, half, 0)
        cross = lax.dynamic_slice_in_dim(twice, start_cross, half, 0)
        return by_parity(same, cross)

    others = jnp.arange(half, dtype=jnp.int32)
    direct_in = jnp.where(odd, col < others, col >= others)
    direct_out = jnp.where(odd, others >= col, others < col)
    none = jnp.zeros((half,), bool)
    relay_in = by_parity(none, jnp.logical_not(direct_in))[:, None, None]
    relay_out = by_parity(none, jnp.logical_not(direct_out))[:, None, None]

    v = in_order(col_factors[0], 4 - col, 8 - col)
    u = in_order(row_factors[0][::-1], 3 - col, 7 - col)
    v_real, v_imag = (v[:, i].reshape(slots * levels, -1) for i in range(2))
    u_real, u_imag = (u[:, i].reshape(slots * levels, -1) for i in range(2))

    rank_table = ranks[0]
    my_ranks = lax.dynamic_index_in_dim(rank_table, myself, 0, keepdims=False)
    anchors = myself - (jnp.arange(slots, dtype=jnp.int32) - half)
    holder = jnp.arange(ntile, dtype=jnp.int32)[:, None] == anchors[None, :]
    row_ranks = jnp.sum(jnp.where(holder, rank_table, 0), axis=0)
    level_ids = jnp.arange(levels, dtype=jnp.int32)
    col_mask = (level_ids[None, :] < in_order(my_ranks, 4 - col, 8 - col)[:, None])[..., None]
    row_mask = (
        level_ids[None, :] < in_order(row_ranks[::-1], 3 - col, 7 - col)[:, None]
    )[..., None]

    gate_re, gate_im = gate_matrix(gate_window, nfreq)
    row_re = lax.dynamic_index_in_dim(gate_re, my_freq, 0, keepdims=False)
    row_im = lax.dynamic_index_in_dim(gate_im, my_freq, 0, keepdims=False)
    stepping = step_sizes[0]
    model = model_start[0]
    observed = data[0].astype(jnp.float32)
    width = model.shape[-1]
    for step in range(ITERS):
        model_bf = model.astype(jnp.bfloat16)
        coef = jnp.dot(v_real, model_bf, preferred_element_type=jnp.float32) + jnp.dot(
            v_imag, rotate(model_bf), preferred_element_type=jnp.float32
        )
        coef = jnp.where(col_mask, coef.reshape(slots, levels, width), 0.0).astype(jnp.bfloat16)
        direct, relayed = spread(coef, swap(cross_half(coef)))
        relayed = same_half(relayed)
        placed = jnp.where(relay_in, jnp.concatenate([relayed, relayed]), direct)
        placed = placed.reshape(slots * levels, width)
        image = left_dot(u_real, placed) + left_dot(u_imag, rotate(placed))
        resid = (image - observed).astype(jnp.bfloat16)
        back = jnp.dot(u_real, resid, preferred_element_type=jnp.float32) - jnp.dot(
            u_imag, rotate(resid), preferred_element_type=jnp.float32
        )
        back = jnp.where(row_mask, back.reshape(slots, levels, width), 0.0).astype(jnp.bfloat16)
        direct, relayed = spread(back, cross_half(back))
        relayed = swap(same_half(relayed))
        landed = jnp.where(relay_out, jnp.concatenate([relayed, relayed]), direct)
        landed = landed.reshape(slots * levels, width)
        grad = left_dot(v_real, landed) - left_dot(v_imag, rotate(landed))
        updated = (model - stepping * grad).astype(jnp.bfloat16)
        everyone = lax.all_gather(updated, "freq", axis=0, tiled=False)
        model = complex_mix(row_re, row_im, everyone)
    return model[None]


def solution(mesh):
    return jax.shard_map(
        on_device,
        mesh=mesh,
        in_specs=(
            P("freq", "tile", None),
            P("freq", "tile", None),
            P("freq", "tile", None, None, None),
            P("freq", "tile", None, None, None),
            P("freq", None, None),
            P(),
            P("freq"),
        ),
        out_specs=P("freq", "tile", None),
        check_vma=False,
    )
```

time: 183 us -> 124 us (0.68)
  the two profiles are of different devices: /device:TPU:368 before, /device:TPU:129 now
where the time goes in v1:
time: 124 us; the launch traced here: 123 us
  blocking collectives  55.5 us (45%)
  waiting for transfers between devices  30.7 us (25%)
  starting transfers between devices  17.4 us (14%)
  other arithmetic  8.02 us (6%)
  local copies, waits for them, and re-layouts  5.21 us (4%)
  matrix products  5.15 us (4%)
  between operations  1.35 us (1%)
    all_gather x2, blocking collectives, on_device(): everyone = lax.all_gather(updated, 'freq', axis=0, tiled=False)  34.6 us
    all_to_all x2, blocking collectives, spread(): lax.all_to_all(send, 'tile', 0, 0, tiled=True, axis_index_groups=groups)  20.9 us
    ppermute x4, waiting for transfers between devices, swap(): return lax.ppermute(value, 'tile', swaps)  18.9 us
    all_to_all x2, waiting for transfers between devices, spread(): lax.all_to_all(send, 'tile', 0, 0, tiled=True, axis_index_groups=groups)  11.9 us
    all_to_all x2, starting transfers between devices, spread(): lax.all_to_all(send, 'tile', 0, 0, tiled=True, axis_index_groups=groups)  9.38 us
    ppermute x4, starting transfers between devices, swap(): return lax.ppermute(value, 'tile', swaps)  7.99 us
    dot_general x8, matrix products, left_dot(): lax.dot_general(factor, values, (((0,), (0,)), ((), ())), preferred_eleme...  2.82 us
  transfers between devices with their start and end apart: 6, of which 6 were waited for; matrix products, arithmetic and copies ran while one was open for 2% of the time, Pallas kernels for 0%

profile of v1, /device:TPU:129, one launch (start us, length us, event | category | flops | bytes accessed | tf_op | source)
XLA Modules:
  0.0 123.4 jit_solution(10845633486219269881)
XLA Ops:
  0.0 1.1 dynamic-slice_bitcast_fusion
  1.7 0.8 copy-done.1
  4.8 1.9 %collective-permute-start = (bf16[4,112,128]{2,1,0:T(8,128)(2,1)S(1)}, bf16[4,112,128]{2,1,0:T(8,128)(2,1)S(1)}, u32[]{:S(2)}, u32[]{:S(2)}) collective-permute-start(bf16[4,112,128]{2,1,0:T(8,128)(2,1)S(1)} %slice_select_fusion.3), channel_id=1, source_target_pairs={{4,8},{5,9},{6,10},{7,11},{8,4},{9,5},{10,6},{11,7},{12,16},{13,17... | collective-permute-start | bytes 344072 | tf_op jit(solution)/shard_map/ppermute | solution.py:69
  6.9 5.0 %collective-permute-done = bf16[4,112,128]{2,1,0:T(8,128)(2,1)S(1)} collective-permute-done((bf16[4,112,128]{2,1,0:T(8,128)(2,1)S(1)}, bf16[4,112,128]{2,1,0:T(8,128)(2,1)S(1)}, u32[]{:S(2)}, u32[]{:S(2)}) %collective-permute-start) | collective-permute-done | bytes 114720 | tf_op jit(solution)/shard_map/ppermute | solution.py:69
  11.9 0.8 pad_maximum_fusion
  12.7 4.7 %all-to-all-start = ((bf16[8,2,112,128]{3,2,1,0:T(8,128)(2,1)}), bf16[8,2,112,128]{3,2,1,0:T(8,128)(2,1)S(1)}, u32[]{:S(2)}, u32[]{:S(2)}) async-start(bf16[8,2,112,128]{3,2,1,0:T(8,128)(2,1)} %pad_maximum_fusion), calls=%async_computation | async-start | bytes 917504 | tf_op jit(solution)/shard_map/all_to_all | solution.py:73
  17.8 0.5 copy-done.3
  19.1 5.3 %all-to-all-done = bf16[8,2,112,128]{3,2,1,0:T(8,128)(2,1)S(1)} async-done(((bf16[8,2,112,128]{3,2,1,0:T(8,128)(2,1)}), bf16[8,2,112,128]{3,2,1,0:T(8,128)(2,1)S(1)}, u32[]{:S(2)}, u32[]{:S(2)}) %all-to-all-start) | async-done | bytes 458784 | tf_op jit(solution)/shard_map/all_to_all | solution.py:73
  26.6 0.8 copy.13
  27.4 4.6 %all-to-all-start.1 = ((bf16[8,2,112,128]{3,2,1,0:T(8,128)(2,1)}), bf16[8,2,112,128]{3,2,1,0:T(8,128)(2,1)S(1)}, u32[]{:S(2)}, u32[]{:S(2)}) async-start(bf16[8,2,112,128]{3,2,1,0:T(8,128)(2,1)} %copy.13), calls=%async_computation.1 | async-start | bytes 917504 | tf_op jit(solution)/shard_map/all_to_all | solution.py:73
  32.4 6.6 %all-to-all-done.1 = bf16[8,2,112,128]{3,2,1,0:T(8,128)(2,1)S(1)} async-done(((bf16[8,2,112,128]{3,2,1,0:T(8,128)(2,1)}), bf16[8,2,112,128]{3,2,1,0:T(8,128)(2,1)S(1)}, u32[]{:S(2)}, u32[]{:S(2)}) %all-to-all-start.1) | async-done | bytes 458784 | tf_op jit(solution)/shard_map/all_to_all | solution.py:73
  39.0 2.2 %collective-permute-start.1 = (bf16[4,112,128]{2,1,0:T(8,128)(2,1)S(1)}, bf16[4,112,128]{2,1,0:T(8,128)(2,1)S(1)}, u32[]{:S(2)}, u32[]{:S(2)}) collective-permute-start(bf16[4,112,128]{2,1,0:T(8,128)(2,1)S(1)} %fusion.32), channel_id=1, source_target_pairs={{4,8},{5,9},{6,10},{7,11},{8,4},{9,5},{10,6},{11,7},{12,16},{13,17... | collective-permute-start | bytes 344072 | tf_op jit(solution)/shard_map/ppermute | solution.py:69
  42.2 3.6 %collective-permute-done.1 = bf16[4,112,128]{2,1,0:T(8,128)(2,1)S(1)} collective-permute-done((bf16[4,112,128]{2,1,0:T(8,128)(2,1)S(1)}, bf16[4,112,128]{2,1,0:T(8,128)(2,1)S(1)}, u32[]{:S(2)}, u32[]{:S(2)}) %collective-permute-start.1) | collective-permute-done | bytes 114720 | tf_op jit(solution)/shard_map/ppermute | solution.py:69
  47.0 17.5 %all-gather = bf16[2048,128]{1,0:T(8,128)(2,1)S(1)} all-gather(bf16[256,128]{1,0:T(8,128)(2,1)S(1)} %fusion.7), channel_id=2, replica_groups=mesh['freq'=8,'tile'=64] {'freq'}, dimensions={0}, use_global_device_ids=true | all-gather | bytes 589824 | tf_op jit(solution)/shard_map/all_gather | solution.py:145
  64.6 0.4 subtract_reduce_fusion.1
  66.0 1.9 %collective-permute-start.2 = (bf16[4,112,128]{2,1,0:T(8,128)(2,1)S(1)}, bf16[4,112,128]{2,1,0:T(8,128)(2,1)S(1)}, u32[]{:S(2)}, u32[]{:S(2)}) collective-permute-start(bf16[4,112,128]{2,1,0:T(8,128)(2,1)S(1)} %slice_select_fusion.1), channel_id=1, source_target_pairs={{4,8},{5,9},{6,10},{7,11},{8,4},{9,5},{10,6},{11,7},{12,16},{13,17... | collective-permute-start | bytes 344072 | tf_op jit(solution)/shard_map/ppermute | solution.py:69
  68.2 5.5 %collective-permute-done.2 = bf16[4,112,128]{2,1,0:T(8,128)(2,1)S(1)} collective-permute-done((bf16[4,112,128]{2,1,0:T(8,128)(2,1)S(1)}, bf16[4,112,128]{2,1,0:T(8,128)(2,1)S(1)}, u32[]{:S(2)}, u32[]{:S(2)}) %collective-permute-start.2) | collective-permute-done | bytes 114720 | tf_op jit(solution)/shard_map/ppermute | solution.py:69
  73.8 10.7 %all_to_all.20 = bf16[8,2,112,128]{3,2,1,0:T(8,128)(2,1)S(1)} all-to-all(bf16[8,2,112,128]{3,2,1,0:T(8,128)(2,1)S(1)} %copy.17), channel_id=1, replica_groups={{0,1,2,3,4,5,6,7},{8,9,10,11,12,13,14,15},{16,17,18,19,20,21,22,23},{24..., dimensions={0} | all-to-all | bytes 917504 | tf_op jit(solution)/shard_map/all_to_all | solution.py:73
  86.7 10.2 %all_to_all.21 = bf16[8,2,112,128]{3,2,1,0:T(8,128)(2,1)S(1)} all-to-all(bf16[8,2,112,128]{3,2,1,0:T(8,128)(2,1)S(1)} %copy.21), channel_id=1, replica_groups={{0,1,2,3,4,5,6,7},{8,9,10,11,12,13,14,15},{16,17,18,19,20,21,22,23},{24..., dimensions={0} | all-to-all | bytes 917504 | tf_op jit(solution)/shard_map/all_to_all | solution.py:73
  97.0 1.9 %collective-permute-start.3 = (bf16[4,112,128]{2,1,0:T(8,128)(2,1)S(1)}, bf16[4,112,128]{2,1,0:T(8,128)(2,1)S(1)}, u32[]{:S(2)}, u32[]{:S(2)}) collective-permute-start(bf16[4,112,128]{2,1,0:T(8,128)(2,1)S(1)} %fusion.28), channel_id=1, source_target_pairs={{4,8},{5,9},{6,10},{7,11},{8,4},{9,5},{10,6},{11,7},{12,16},{13,17... | collective-permute-start | bytes 344072 | tf_op jit(solution)/shard_map/ppermute | solution.py:69
  99.0 4.8 %collective-permute-done.3 = bf16[4,112,128]{2,1,0:T(8,128)(2,1)S(1)} collective-permute-done((bf16[4,112,128]{2,1,0:T(8,128)(2,1)S(1)}, bf16[4,112,128]{2,1,0:T(8,128)(2,1)S(1)}, u32[]{:S(2)}, u32[]{:S(2)}) %collective-permute-start.3) | collective-permute-done | bytes 114720 | tf_op jit(solution)/shard_map/ppermute | solution.py:69
  105.0 17.1 %all-gather.1 = bf16[2048,128]{1,0:T(8,128)(2,1)S(1)} all-gather(bf16[256,128]{1,0:T(8,128)(2,1)S(1)} %fusion.9), channel_id=3, replica_groups=mesh['freq'=8,'tile'=64] {'freq'}, dimensions={0}, use_global_device_ids=true | all-gather | bytes 589824 | tf_op jit(solution)/shard_map/all_gather | solution.py:145
  122.2 0.4 subtract_reduce_fusion
  122.6 0.8 maximum_bitcast_fusion.4
  (114 shorter events, 12.7 us)
Async XLA Ops:
  0.0 1.3 %copy-start = (bf16[1,8,2,112,256]{4,3,2,1,0:T(8,128)(2,1)S(1)}, bf16[1,8,2,112,256]{4,3,2,1,0:T(8,128)(2,1)}, u32[]{:S(2)}) copy-start(bf16[1,8,2,112,256]{4,3,2,1,0:T(8,128)(2,1)} %param.9) | copy-start | bytes 2752516
  1.6 0.9 copy-start.1
  2.6 0.7 copy-start.4
  4.8 7.1 %collective-permute-start = (bf16[4,112,128]{2,1,0:T(8,128)(2,1)S(1)}, bf16[4,112,128]{2,1,0:T(8,128)(2,1)S(1)}, u32[]{:S(2)}, u32[]{:S(2)}) collective-permute-start(bf16[4,112,128]{2,1,0:T(8,128)(2,1)S(1)} %slice_select_fusion.3), channel_id=1, source_target_pairs={{4,8},{5,9},{6,10},{7,11},{8,4},{9,5},{10,6},{11,7},{12,16},{13,17... | collective-permute-start | bytes 344072 | tf_op jit(solution)/shard_map/ppermute | solution.py:69
  6.9 10.8 %copy-start.2 = (bf16[1,8,2,112,256]{4,3,2,1,0:T(8,128)(2,1)S(1)}, bf16[1,8,2,112,256]{4,3,2,1,0:T(8,128)(2,1)}, u32[]{:S(2)}) copy-start(bf16[1,8,2,112,256]{4,3,2,1,0:T(8,128)(2,1)} %param.10) | copy-start | bytes 2752516
  12.7 11.7 %all-to-all-start = ((bf16[8,2,112,128]{3,2,1,0:T(8,128)(2,1)}), bf16[8,2,112,128]{3,2,1,0:T(8,128)(2,1)S(1)}, u32[]{:S(2)}, u32[]{:S(2)}) async-start(bf16[8,2,112,128]{3,2,1,0:T(8,128)(2,1)} %pad_maximum_fusion), calls=%async_computation | async-start | bytes 917504 | tf_op jit(solution)/shard_map/all_to_all | solution.py:73
  17.5 0.8 copy-start.3
  26.6 5.5 %copy-start.5 = (s32[64,2]{0,1:T(2,128)S(1)}, s32[64,2]{0,1:T(2,128)}, u32[]{:S(2)}) copy-start(s32[64,2]{0,1:T(2,128)} %param.12) | copy-start | bytes 1540
  27.4 11.6 %all-to-all-start.1 = ((bf16[8,2,112,128]{3,2,1,0:T(8,128)(2,1)}), bf16[8,2,112,128]{3,2,1,0:T(8,128)(2,1)S(1)}, u32[]{:S(2)}, u32[]{:S(2)}) async-start(bf16[8,2,112,128]{3,2,1,0:T(8,128)(2,1)} %copy.13), calls=%async_computation.1 | async-start | bytes 917504 | tf_op jit(solution)/shard_map/all_to_all | solution.py:73
  39.0 6.7 %collective-permute-start.1 = (bf16[4,112,128]{2,1,0:T(8,128)(2,1)S(1)}, bf16[4,112,128]{2,1,0:T(8,128)(2,1)S(1)}, u32[]{:S(2)}, u32[]{:S(2)}) collective-permute-start(bf16[4,112,128]{2,1,0:T(8,128)(2,1)S(1)} %fusion.32), channel_id=1, source_target_pairs={{4,8},{5,9},{6,10},{7,11},{8,4},{9,5},{10,6},{11,7},{12,16},{13,17... | collective-permute-start | bytes 344072 | tf_op jit(solution)/shard_map/ppermute | solution.py:69
  66.0 7.7 %collective-permute-start.2 = (bf16[4,112,128]{2,1,0:T(8,128)(2,1)S(1)}, bf16[4,112,128]{2,1,0:T(8,128)(2,1)S(1)}, u32[]{:S(2)}, u32[]{:S(2)}) collective-permute-start(bf16[4,112,128]{2,1,0:T(8,128)(2,1)S(1)} %slice_select_fusion.1), channel_id=1, source_target_pairs={{4,8},{5,9},{6,10},{7,11},{8,4},{9,5},{10,6},{11,7},{12,16},{13,17... | collective-permute-start | bytes 344072 | tf_op jit(solution)/shard_map/ppermute | solution.py:69
  97.0 6.7 %collective-permute-start.3 = (bf16[4,112,128]{2,1,0:T(8,128)(2,1)S(1)}, bf16[4,112,128]{2,1,0:T(8,128)(2,1)S(1)}, u32[]{:S(2)}, u32[]{:S(2)}) collective-permute-start(bf16[4,112,128]{2,1,0:T(8,128)(2,1)S(1)} %fusion.28), channel_id=1, source_target_pairs={{4,8},{5,9},{6,10},{7,11},{8,4},{9,5},{10,6},{11,7},{12,16},{13,17... | collective-permute-start | bytes 344072 | tf_op jit(solution)/shard_map/ppermute | solution.py:69

commit v2 on v1

--- a/solution.py
+++ b/solution.py
@@ -38,12 +38,13 @@
 
 
 def complex_mix(coeff_re, coeff_im, values):
-    values = values.astype(jnp.float32)
     width = values.shape[-1] // 2
     vals_re = values[..., :width]
     vals_im = values[..., width:]
-    out_re = jnp.sum(coeff_re[:, None, :] * vals_re - coeff_im[:, None, :] * vals_im, axis=0)
-    out_im = jnp.sum(coeff_re[:, None, :] * vals_im + coeff_im[:, None, :] * vals_re, axis=0)
+    g_re = coeff_re[:, :, None, :]
+    g_im = coeff_im[:, :, None, :]
+    out_re = jnp.sum(g_re * vals_re - g_im * vals_im, axis=1)
+    out_im = jnp.sum(g_re * vals_im + g_im * vals_re, axis=1)
     return jnp.concatenate([out_re, out_im], axis=-1)
 
 
@@ -65,13 +66,30 @@
         for y in range(WIDE)
     ]
 
+    half_freq = [
+        [
+            f * ntile + (z % rows_z) * WIDE + y
+            for f in range(nfreq)
+            for z in (2 * k - 1, 2 * k)
+        ]
+        for k in range(rows_z // 2)
+        for y in range(WIDE)
+    ]
+
     def swap(value):
         return lax.ppermute(value, "tile", swaps)
 
-    def spread(own, forwarded):
-        send = jnp.stack([own, jnp.concatenate([forwarded, forwarded])], axis=1)
+    def spread(own, relayed):
+        send = jnp.stack([own, jnp.concatenate([relayed, relayed])], axis=1)
         got = lax.all_to_all(send, "tile", 0, 0, tiled=True, axis_index_groups=groups)
-        return got[:, 0], got[:, 1]
+        return got[:, 0], same_half(got[:, 1])
+
+    def among_pair(pieces):
+        flat = pieces.reshape(2 * nfreq, -1, pieces.shape[-1])
+        got = lax.all_to_all(
+            flat, ("freq", "tile"), 0, 0, tiled=True, axis_index_groups=half_freq
+        )
+        return got.reshape(pieces.shape)
 
     def by_parity(same, cross):
         return jnp.where(
@@ -95,7 +113,7 @@
     direct_out = jnp.where(odd, others >= col, others < col)
     none = jnp.zeros((half,), bool)
     relay_in = by_parity(none, jnp.logical_not(direct_in))[:, None, None]
-    relay_out = by_parity(none, jnp.logical_not(direct_out))[:, None, None]
+    drop_out = by_parity(none, jnp.logical_not(direct_out))[:, None, None]
 
     v = in_order(col_factors[0], 4 - col, 8 - col)
     u = in_order(row_factors[0][::-1], 3 - col, 7 - col)
@@ -114,20 +132,33 @@
     )[..., None]
 
     gate_re, gate_im = gate_matrix(gate_window, nfreq)
-    row_re = lax.dynamic_index_in_dim(gate_re, my_freq, 0, keepdims=False)
-    row_im = lax.dynamic_index_in_dim(gate_im, my_freq, 0, keepdims=False)
     stepping = step_sizes[0]
     model = model_start[0]
     observed = data[0].astype(jnp.float32)
     width = model.shape[-1]
+    part = model.shape[0] // nfreq
+
+    def multiply(real, imag, values):
+        return jnp.dot(real, values, preferred_element_type=jnp.float32) + jnp.dot(
+            imag, rotate(values), preferred_element_type=jnp.float32
+        )
+
+    partner = None
     for step in range(ITERS):
         model_bf = model.astype(jnp.bfloat16)
-        coef = jnp.dot(v_real, model_bf, preferred_element_type=jnp.float32) + jnp.dot(
-            v_imag, rotate(model_bf), preferred_element_type=jnp.float32
-        )
+        coef = multiply(v_real, v_imag, model_bf)
         coef = jnp.where(col_mask, coef.reshape(slots, levels, width), 0.0).astype(jnp.bfloat16)
-        direct, relayed = spread(coef, swap(cross_half(coef)))
-        relayed = same_half(relayed)
+        if step == 0:
+            beyond = cross_half(coef)
+            kept = jnp.where(cross_half(col_mask)[:, None], cross_half(v), 0)
+            beyond, kept = lax.optimization_barrier((beyond, kept))
+            far = swap(beyond)
+            w = swap(kept)
+            w_real, w_imag = (w[:, i].reshape(half * levels, -1) for i in range(2))
+        else:
+            far = multiply(w_real, w_imag, partner).astype(jnp.bfloat16)
+            far = far.reshape(half, levels, width)
+        direct, relayed = spread(coef, far)
         placed = jnp.where(relay_in, jnp.concatenate([relayed, relayed]), direct)
         placed = placed.reshape(slots * levels, width)
         image = left_dot(u_real, placed) + left_dot(u_imag, rotate(placed))
@@ -137,13 +168,26 @@
         )
         back = jnp.where(row_mask, back.reshape(slots, levels, width), 0.0).astype(jnp.bfloat16)
         direct, relayed = spread(back, cross_half(back))
-        relayed = swap(same_half(relayed))
-        landed = jnp.where(relay_out, jnp.concatenate([relayed, relayed]), direct)
-        landed = landed.reshape(slots * levels, width)
+        landed = jnp.where(drop_out, 0, direct).reshape(slots * levels, width)
+        handed = jnp.where(direct_out[:, None, None], relayed, 0).reshape(half * levels, width)
         grad = left_dot(v_real, landed) - left_dot(v_imag, rotate(landed))
-        updated = (model - stepping * grad).astype(jnp.bfloat16)
-        everyone = lax.all_gather(updated, "freq", axis=0, tiled=False)
-        model = complex_mix(row_re, row_im, everyone)
+        share = left_dot(w_real, handed) - left_dot(w_imag, rotate(handed))
+        mine = (model - stepping * grad).astype(jnp.bfloat16).reshape(nfreq, part, width)
+        theirs = (-stepping * share).astype(jnp.bfloat16).reshape(nfreq, part, width)
+        both = jnp.where(
+            odd, jnp.stack([mine, theirs], axis=1), jnp.stack([theirs, mine], axis=1)
+        )
+        z = jnp.sum(among_pair(both).astype(jnp.float32), axis=1)
+        mixed = complex_mix(gate_re, gate_im, z).astype(jnp.bfloat16)
+        if step == ITERS - 1:
+            model = lax.all_to_all(mixed, "freq", 0, 0, tiled=True)
+            model = model.astype(jnp.float32).reshape(nfreq * part, width)
+        else:
+            pair = among_pair(jnp.stack([mixed, mixed], axis=1))
+            low = pair[:, 0].reshape(nfreq * part, width)
+            high = pair[:, 1].reshape(nfreq * part, width)
+            model = jnp.where(odd, low, high).astype(jnp.float32)
+            partner = jnp.where(odd, high, low)
     return model[None]
 
 

time: 124 us -> 136 us (1.097)
  the two profiles are of different devices: /device:TPU:129 before, /device:TPU:32 now
where the time goes in v2:
time: 136 us; the launch traced here: 135 us
  blocking collectives  57.9 us (43%)
  starting transfers between devices  24.9 us (18%)
  waiting for transfers between devices  22.7 us (17%)
  other arithmetic  10.6 us (8%)
  matrix products  8.76 us (6%)
  local copies, waits for them, and re-layouts  8.53 us (6%)
  between operations  1.45 us (1%)
    all_to_all x2, blocking collectives, spread(): lax.all_to_all(send, 'tile', 0, 0, tiled=True, axis_index_groups=groups)  25.3 us
    all_to_all x2, blocking collectives, among_pair(): lax.all_to_all(flat, ('freq', 'tile'), 0, 0, tiled=True, axis_index_group...  24.6 us
    ppermute x2, waiting for transfers between devices, swap(): return lax.ppermute(value, 'tile', swaps)  10.8 us
    all_to_all x2, starting transfers between devices, spread(): lax.all_to_all(send, 'tile', 0, 0, tiled=True, axis_index_groups=groups)  10.5 us
    ppermute x2, starting transfers between devices, swap(): return lax.ppermute(value, 'tile', swaps)  8.85 us
    all_to_all x1, blocking collectives, on_device(): model = lax.all_to_all(mixed, 'freq', 0, 0, tiled=True)  8.04 us
    all_to_all x1, waiting for transfers between devices, among_pair(): lax.all_to_all(flat, ('freq', 'tile'), 0, 0, tiled=True, axis_index_group...  6.25 us
    dot_general x12, matrix products, left_dot(): lax.dot_general(factor, values, (((0,), (0,)), ((), ())), preferred_eleme...  5.95 us
  transfers between devices with their start and end apart: 5, of which 4 were waited for; matrix products, arithmetic and copies ran while one was open for 3% of the time, Pallas kernels for 0%

profile of v2, /device:TPU:32, one launch (start us, length us, event | category | flops | bytes accessed | tf_op | source)
XLA Modules:
  0.0 134.8 jit_solution(10645326677484112861)
XLA Ops:
  0.0 1.1 copy_bitcast_fusion.2
  3.9 1.2 maximum_select_fusion
  5.1 0.9 fusion.19
  6.9 3.8 %collective-permute-start = (bf16[4,112,128]{2,1,0:T(8,128)(2,1)S(1)}, bf16[4,112,128]{2,1,0:T(8,128)(2,1)S(1)}, u32[]{:S(2)}, u32[]{:S(2)}) collective-permute-start(bf16[4,112,128]{2,1,0:T(8,128)(2,1)S(1)} %slice_select_fusion.3), channel_id=1, source_target_pairs={{4,8},{5,9},{6,10},{7,11},{8,4},{9,5},{10,6},{11,7},{12,16},{13,17... | collective-permute-start | bytes 344072 | tf_op jit(solution)/shard_map/ppermute | solution.py:80
  10.9 2.9 %collective-permute-done = bf16[4,112,128]{2,1,0:T(8,128)(2,1)S(1)} collective-permute-done((bf16[4,112,128]{2,1,0:T(8,128)(2,1)S(1)}, bf16[4,112,128]{2,1,0:T(8,128)(2,1)S(1)}, u32[]{:S(2)}, u32[]{:S(2)}) %collective-permute-start) | collective-permute-done | bytes 114720 | tf_op jit(solution)/shard_map/ppermute | solution.py:80
  13.9 0.8 pad_maximum_fusion
  14.7 5.9 %all-to-all-start = ((bf16[8,2,112,128]{3,2,1,0:T(8,128)(2,1)}), bf16[8,2,112,128]{3,2,1,0:T(8,128)(2,1)S(1)}, u32[]{:S(2)}, u32[]{:S(2)}) async-start(bf16[8,2,112,128]{3,2,1,0:T(8,128)(2,1)} %pad_maximum_fusion), calls=%async_computation | async-start | bytes 917504 | tf_op jit(solution)/shard_map/all_to_all | solution.py:84
  21.1 1.2 fusion.113
  22.3 5.6 %all-to-all-done = bf16[8,2,112,128]{3,2,1,0:T(8,128)(2,1)S(1)} async-done(((bf16[8,2,112,128]{3,2,1,0:T(8,128)(2,1)}), bf16[8,2,112,128]{3,2,1,0:T(8,128)(2,1)S(1)}, u32[]{:S(2)}, u32[]{:S(2)}) %all-to-all-start) | async-done | bytes 458784 | tf_op jit(solution)/shard_map/all_to_all | solution.py:84
  30.1 0.8 copy.56
  30.9 4.5 %all-to-all-start.1 = ((bf16[8,2,112,128]{3,2,1,0:T(8,128)(2,1)}), bf16[8,2,112,128]{3,2,1,0:T(8,128)(2,1)S(1)}, u32[]{:S(2)}, u32[]{:S(2)}) async-start(bf16[8,2,112,128]{3,2,1,0:T(8,128)(2,1)} %copy.56), calls=%async_computation.1 | async-start | bytes 917504 | tf_op jit(solution)/shard_map/all_to_all | solution.py:84
  35.4 5.0 %collective-permute-start.1 = (bf16[4,2,112,256]{3,2,0,1:T(8,128)(2,1)}, bf16[4,2,112,256]{3,2,0,1:T(8,128)(2,1)}, u32[]{:S(2)}, u32[]{:S(2)}) collective-permute-start(bf16[4,2,112,256]{3,2,0,1:T(8,128)(2,1)} %fusion.19), channel_id=1, source_target_pairs={{4,8},{5,9},{6,10},{7,11},{8,4},{9,5},{10,6},{11,7},{12,16},{13,17... | collective-permute-start | bytes 1376264 | tf_op jit(solution)/shard_map/ppermute | solution.py:80
  42.1 7.9 %collective-permute-done.1 = bf16[4,2,112,256]{3,2,0,1:T(8,128)(2,1)} collective-permute-done((bf16[4,2,112,256]{3,2,0,1:T(8,128)(2,1)}, bf16[4,2,112,256]{3,2,0,1:T(8,128)(2,1)}, u32[]{:S(2)}, u32[]{:S(2)}) %collective-permute-start.1) | collective-permute-done | bytes 458784 | tf_op jit(solution)/shard_map/ppermute | solution.py:80
  50.0 1.8 %fusion.115 = (bf16[4,1,112,256]{3,2,0,1:T(8,128)(2,1)}, bf16[4,1,112,256]{3,2,0,1:T(8,128)(2,1)S(1)}) fusion(bf16[4,2,112,256]{3,2,0,1:T(8,128)(2,1)} %collective-permute-done.1), kind=kLoop, calls=%fused_computation.227 | loop fusion | bytes 917504 | tf_op jit(solution)/shard_map/slice | solution.py:157
  53.7 1.2 fusion.12
  55.0 0.7 maximum_select_fusion.2
  55.7 5.6 %all-to-all-start.2 = ((bf16[16,32,128]{2,1,0:T(8,128)(2,1)}), bf16[16,32,128]{2,1,0:T(8,128)(2,1)S(1)}, u32[]{:S(2)}, u32[]{:S(2)}) async-start(bf16[16,32,128]{2,1,0:T(8,128)(2,1)} %bitcast.41), calls=%async_computation.2 | async-start | bytes 262144 | tf_op jit(solution)/shard_map/all_to_all | solution.py:89
  61.6 6.3 %all-to-all-done.2 = bf16[16,32,128]{2,1,0:T(8,128)(2,1)S(1)} async-done(((bf16[16,32,128]{2,1,0:T(8,128)(2,1)}), bf16[16,32,128]{2,1,0:T(8,128)(2,1)S(1)}, u32[]{:S(2)}, u32[]{:S(2)}) %all-to-all-start.2) | async-done | bytes 131104 | tf_op jit(solution)/shard_map/all_to_all | solution.py:89
  68.5 9.2 %all_to_all.40 = bf16[16,32,128]{2,1,0:T(8,128)(2,1)S(1)} all-to-all(bf16[16,32,128]{2,1,0:T(8,128)(2,1)S(1)} %bitcast.260), channel_id=1, replica_groups={{60,0,124,64,188,128,252,192,316,256,380,320,444,384,508,448},{61,1,125..., dimensions={0} | all-to-all | bytes 262144 | tf_op jit(solution)/shard_map/all_to_all | solution.py:89
  79.5 14.0 %all_to_all.41 = bf16[8,2,112,128]{3,2,1,0:T(8,128)(2,1)S(1)} all-to-all(bf16[8,2,112,128]{3,2,1,0:T(8,128)(2,1)S(1)} %copy.64), channel_id=1, replica_groups={{0,1,2,3,4,5,6,7},{8,9,10,11,12,13,14,15},{16,17,18,19,20,21,22,23},{24..., dimensions={0} | all-to-all | bytes 917504 | tf_op jit(solution)/shard_map/all_to_all | solution.py:84
  95.8 11.2 %all_to_all.42 = bf16[8,2,112,128]{3,2,1,0:T(8,128)(2,1)S(1)} all-to-all(bf16[8,2,112,128]{3,2,1,0:T(8,128)(2,1)S(1)} %copy.68), channel_id=1, replica_groups={{0,1,2,3,4,5,6,7},{8,9,10,11,12,13,14,15},{16,17,18,19,20,21,22,23},{24..., dimensions={0} | all-to-all | bytes 917504 | tf_op jit(solution)/shard_map/all_to_all | solution.py:84
  108.8 1.2 fusion.11
  110.1 15.4 %all_to_all.43 = bf16[16,32,128]{2,1,0:T(8,128)(2,1)S(1)} all-to-all(bf16[16,32,128]{2,1,0:T(8,128)(2,1)S(1)} %bitcast.259), channel_id=1, replica_groups={{60,0,124,64,188,128,252,192,316,256,380,320,444,384,508,448},{61,1,125..., dimensions={0} | all-to-all | bytes 262144 | tf_op jit(solution)/shard_map/all_to_all | solution.py:89
  126.1 8.0 %all_to_all.44 = bf16[8,32,128]{2,1,0:T(8,128)(2,1)S(1)} all-to-all(bf16[8,32,128]{2,1,0:T(8,128)(2,1)S(1)} %pad_maximum_fusion.6), channel_id=1, replica_groups=mesh['freq'=8,'tile'=64] {'freq'}, dimensions={0} | all-to-all | bytes 131072 | tf_op jit(solution)/shard_map/all_to_all | solution.py:183
  (138 shorter events, 16.8 us)
Async XLA Ops:
  0.0 1.3 copy-start
  1.3 0.7 copy-start.6
  1.3 1.9 %copy-start.1 = (f32[1,256,128]{2,1,0:T(8,128)S(1)}, f32[1,256,128]{2,1,0:T(8,128)}, u32[]{:S(2)}) copy-start(f32[1,256,128]{2,1,0:T(8,128)} %param.7) | copy-start | bytes 393220
  1.3 2.0 %copy-start.3 = (bf16[1,8,2,112,256]{4,3,2,1,0:T(8,128)(2,1)S(1)}, bf16[1,8,2,112,256]{4,3,2,1,0:T(8,128)(2,1)}, u32[]{:S(2)}) copy-start(bf16[1,8,2,112,256]{4,3,2,1,0:T(8,128)(2,1)} %param.10) | copy-start | bytes 2752516
  6.9 7.0 %collective-permute-start = (bf16[4,112,128]{2,1,0:T(8,128)(2,1)S(1)}, bf16[4,112,128]{2,1,0:T(8,128)(2,1)S(1)}, u32[]{:S(2)}, u32[]{:S(2)}) collective-permute-start(bf16[4,112,128]{2,1,0:T(8,128)(2,1)S(1)} %slice_select_fusion.3), channel_id=1, source_target_pairs={{4,8},{5,9},{6,10},{7,11},{8,4},{9,5},{10,6},{11,7},{12,16},{13,17... | collective-permute-start | bytes 344072 | tf_op jit(solution)/shard_map/ppermute | solution.py:80
  13.9 7.0 %copy-start.5 = (bf16[1,256,128]{2,1,0:T(8,128)(2,1)S(1)}, bf16[1,256,128]{2,1,0:T(8,128)(2,1)}, u32[]{:S(2)}) copy-start(bf16[1,256,128]{2,1,0:T(8,128)(2,1)} %param.8) | copy-start | bytes 196612
  14.7 13.2 %all-to-all-start = ((bf16[8,2,112,128]{3,2,1,0:T(8,128)(2,1)}), bf16[8,2,112,128]{3,2,1,0:T(8,128)(2,1)S(1)}, u32[]{:S(2)}, u32[]{:S(2)}) async-start(bf16[8,2,112,128]{3,2,1,0:T(8,128)(2,1)} %pad_maximum_fusion), calls=%async_computation | async-start | bytes 917504 | tf_op jit(solution)/shard_map/all_to_all | solution.py:84
  30.1 12.0 %copy-start.7 = (s32[64,2]{0,1:T(2,128)S(1)}, s32[64,2]{0,1:T(2,128)}, u32[]{:S(2)}) copy-start(s32[64,2]{0,1:T(2,128)} %param.12) | copy-start | bytes 1540
  30.9 20.9 %all-to-all-start.1 = ((bf16[8,2,112,128]{3,2,1,0:T(8,128)(2,1)}), bf16[8,2,112,128]{3,2,1,0:T(8,128)(2,1)S(1)}, u32[]{:S(2)}, u32[]{:S(2)}) async-start(bf16[8,2,112,128]{3,2,1,0:T(8,128)(2,1)} %copy.56), calls=%async_computation.1 | async-start | bytes 917504 | tf_op jit(solution)/shard_map/all_to_all | solution.py:84
  35.4 14.6 %collective-permute-start.1 = (bf16[4,2,112,256]{3,2,0,1:T(8,128)(2,1)}, bf16[4,2,112,256]{3,2,0,1:T(8,128)(2,1)}, u32[]{:S(2)}, u32[]{:S(2)}) collective-permute-start(bf16[4,2,112,256]{3,2,0,1:T(8,128)(2,1)} %fusion.19), channel_id=1, source_target_pairs={{4,8},{5,9},{6,10},{7,11},{8,4},{9,5},{10,6},{11,7},{12,16},{13,17... | collective-permute-start | bytes 1376264 | tf_op jit(solution)/shard_map/ppermute | solution.py:80
  41.4 0.6 copy-start.8
  52.1 0.7 copy-start.9
  52.4 0.9 copy-start.2
  55.7 12.2 %all-to-all-start.2 = ((bf16[16,32,128]{2,1,0:T(8,128)(2,1)}), bf16[16,32,128]{2,1,0:T(8,128)(2,1)S(1)}, u32[]{:S(2)}, u32[]{:S(2)}) async-start(bf16[16,32,128]{2,1,0:T(8,128)(2,1)} %bitcast.41), calls=%async_computation.2 | async-start | bytes 262144 | tf_op jit(solution)/shard_map/all_to_all | solution.py:89
  77.7 0.9 copy-start.4
  107.4 0.7 copy-start.10

commit v3 on v1

v3 whole, which is shorter than its diff:
```python
import functools
import math

import jax
import jax.numpy as jnp
from jax import lax
from jax.experimental import pallas as pl
from jax.experimental.pallas import tpu as pltpu
from jax.sharding import PartitionSpec as P

NT = 2048
ITERS = 2
WIDE = 4
VMEM_BYTES = 24 * 2**20
COL, ODD, OWN, FAR, ROW, SCALARS = 0, 1, 2, 10, 14, 24


def gate_matrix(window, count):
    start = window[:, 0].astype(jnp.float32)
    span = (window[:, 1] - window[:, 0]).astype(jnp.float32)
    freqs = jnp.arange(count, dtype=jnp.float32)
    delta = freqs[:, None] - freqs[None, :]
    theta = 2.0 * math.pi * delta / NT
    safe = jnp.where(delta == 0.0, 1.0, jnp.sin(theta / 2.0))
    magnitude = jnp.where(
        (delta == 0.0)[:, :, None],
        span[None, None, :] / NT,
        jnp.sin(theta[:, :, None] * span[None, None, :] / 2.0) / (NT * safe[:, :, None]),
    )
    phase = theta[:, :, None] * (start[None, None, :] + (span[None, None, :] - 1.0) / 2.0)
    return (magnitude * jnp.cos(phase), magnitude * jnp.sin(phase))


def turn(z):
    width = z.shape[-1]
    lane = lax.broadcasted_iota(jnp.int32, z.shape, z.ndim - 1)
    rolled = pltpu.roll(z, width // 2, z.ndim - 1)
    return jnp.where(lane < width // 2, -rolled, rolled)


def turn_bf(z):
    return turn(z.astype(jnp.float32)).astype(jnp.bfloat16)


def dot(a, b):
    return jnp.dot(a, b, preferred_element_type=jnp.float32)


def left_dot(a, b):
    return lax.dot_general(a, b, (((0,), (0,)), ((), ())), preferred_element_type=jnp.float32)


def keep(value, rank):
    row = lax.broadcasted_iota(jnp.int32, value.shape, 0)
    return jnp.where(row < rank, value.astype(jnp.float32), 0.0).astype(jnp.bfloat16)


def side_of(ref, side):
    return jnp.concatenate([ref[j, side] for j in range(ref.shape[0])], axis=0)


def far_factor(far_ref, index, which, levels):
    start = (2 * index + which) * levels
    return far_ref[start : start + levels, :]


def outward(col, s, odd):
    column = (col + s) & 3
    way = (col + s) >> 2
    same = way == 1
    near = jnp.where(odd == 1, way == 0, way == 2)
    return column, same, near


def coef_kernel(scal, v_ref, far_ref, x_ref, out_ref, *, first):
    slots, _, levels, rows = v_ref.shape
    half = slots // 2
    col, odd = scal[COL], scal[ODD]
    if first:
        x = x_ref[...].astype(jnp.bfloat16)
        packed = far_ref[half * 2 * levels :, :]
        width = x.shape[-1]
        x_far = jnp.concatenate([packed[:, :width], packed[:, width:]], axis=0)
    else:
        x = side_of(x_ref, 1 - odd)
        x_far = side_of(x_ref, odd)
    x_turn, far_turn = turn_bf(x), turn_bf(x_far)
    for s in range(slots):
        column, same, _ = outward(col, s, odd)
        place = column + half * jnp.where(same, odd, 1 - odd)
        out_ref[place, 0] = keep(dot(v_ref[s, 0], x) + dot(v_ref[s, 1], x_turn), scal[OWN + s])
    for i in range(half):
        column = (col + i) & 3
        piece = dot(far_factor(far_ref, i, 0, levels), x_far)
        piece += dot(far_factor(far_ref, i, 1, levels), far_turn)
        piece = keep(piece, scal[FAR + i])
        out_ref[column, 1] = piece
        out_ref[column + half, 1] = piece


def resid_kernel(scal, got_ref, u_ref, data_ref, out_ref):
    slots = u_ref.shape[0]
    half = slots // 2
    col, odd = scal[COL], scal[ODD]
    real = jnp.zeros(data_ref.shape, jnp.float32)
    imag = jnp.zeros(data_ref.shape, jnp.float32)
    for s in range(slots):
        column = (col + slots - s) & 3
        way = (col + slots - s) >> 2
        near = jnp.where(odd == 1, way == 0, way == 2)
        relay = jnp.logical_not(jnp.logical_or(near, way == 1)).astype(jnp.int32)
        piece = got_ref[column + half * jnp.where(near, 1 - odd, odd), relay]
        real += left_dot(u_ref[s, 0], piece)
        imag += left_dot(u_ref[s, 1], piece)
    image = real + turn(imag)
    resid = (image - data_ref[...].astype(jnp.float32)).astype(jnp.bfloat16)
    resid_turn = turn_bf(resid)
    for s in range(slots):
        column = (col + slots - s) & 3
        same = ((col + slots - s) >> 2) == 1
        piece = keep(dot(u_ref[s, 0], resid) - dot(u_ref[s, 1], resid_turn), scal[ROW + s])
        out_ref[column + half * jnp.where(same, odd, 1 - odd), 0] = piece

        @pl.when(jnp.logical_not(same))
        def _():
            out_ref[column, 1] = piece
            out_ref[column + half, 1] = piece


def grad_kernel(scal, size_ref, got_ref, v_ref, far_ref, x_ref, out_ref, *, first):
    slots, _, levels, _ = v_ref.shape
    half = slots // 2
    col, odd = scal[COL], scal[ODD]
    parts, _, part, width = out_ref.shape
    shape = (parts * part, width)
    real = jnp.zeros(shape, jnp.float32)
    imag = jnp.zeros(shape, jnp.float32)
    for s in range(slots):
        column, same, near = outward(col, s, odd)
        piece = got_ref[column + half * jnp.where(same, odd, 1 - odd), 0]
        piece = keep(piece, jnp.where(jnp.logical_or(same, near), levels, 0))
        real += left_dot(v_ref[s, 0], piece)
        imag += left_dot(v_ref[s, 1], piece)
    far_real = jnp.zeros(shape, jnp.float32)
    far_imag = jnp.zeros(shape, jnp.float32)
    for i in range(half):
        column = (col + i) & 3
        valid = (col + i < half).astype(jnp.int32) == odd
        piece = keep(got_ref[column + half * odd, 1], jnp.where(valid, levels, 0))
        far_real += left_dot(far_factor(far_ref, i, 0, levels), piece)
        far_imag += left_dot(far_factor(far_ref, i, 1, levels), piece)
    x = x_ref[...] if first else side_of(x_ref, 1 - odd).astype(jnp.float32)
    size = size_ref[0]
    mine = (x - size * (real - turn(imag))).astype(jnp.bfloat16)
    theirs = (-size * (far_real - turn(far_imag))).astype(jnp.bfloat16)
    for j in range(parts):
        out_ref[j, 1 - odd] = mine[j * part : (j + 1) * part]
        out_ref[j, odd] = theirs[j * part : (j + 1) * part]


def mix_kernel(re_ref, im_ref, got_ref, out_ref):
    count = got_ref.shape[0]
    z, z_turn = [], []
    for g in range(count):
        total = got_ref[g, 0].astype(jnp.float32) + got_ref[g, 1].astype(jnp.float32)
        z.append(total)
        z_turn.append(turn(total))
    for f in range(count):
        total = jnp.zeros_like(z[0])
        for g in range(count):
            total += re_ref[f, g : g + 1, :] * z[g] + im_ref[f, g : g + 1, :] * z_turn[g]
        total = total.astype(jnp.bfloat16)
        for side in range(out_ref.shape[1]):
            out_ref[f, side] = total


def kernel_call(body, shape, scalars, *operands):
    smem = pl.BlockSpec(memory_space=pltpu.SMEM)
    vmem = pl.BlockSpec(memory_space=pltpu.VMEM)
    return pl.pallas_call(
        body,
        out_shape=jax.ShapeDtypeStruct(shape, jnp.bfloat16),
        in_specs=[smem] * len(scalars) + [vmem] * len(operands),
        out_specs=vmem,
        compiler_params=pltpu.CompilerParams(vmem_limit_bytes=VMEM_BYTES),
    )(*scalars, *operands)


def on_device(model_start, data, col_factors, row_factors, ranks, gate_window, step_sizes):
    ntile = lax.axis_size("tile")
    nfreq = lax.axis_size("freq")
    myself = lax.axis_index("tile")
    slots = ranks.shape[2]
    levels = col_factors.shape[3]
    half = slots // 2
    rows_z = ntile // WIDE
    col = myself % WIDE
    odd = (myself // WIDE) % 2
    groups = [[slots * k + i for i in range(slots)] for k in range(ntile // slots)]
    swaps = [
        (z * WIDE + y, (z + 1 if z % 2 else z - 1) * WIDE + y)
        for z in range(1, rows_z - 1)
        for y in range(WIDE)
    ]
    pairs = [
        [
            f * ntile + (z % rows_z) * WIDE + y
            for f in range(nfreq)
            for z in (2 * k - 1, 2 * k)
        ]
        for k in range(rows_z // 2)
        for y in range(WIDE)
    ]

    def spread(pieces):
        return lax.all_to_all(pieces, "tile", 0, 0, tiled=True, axis_index_groups=groups)

    def among_pair(pieces):
        flat = pieces.reshape(2 * nfreq, -1, pieces.shape[-1])
        got = lax.all_to_all(
            flat, ("freq", "tile"), 0, 0, tiled=True, axis_index_groups=pairs
        )
        return got.reshape(pieces.shape)

    model = model_start[0]
    rows, width = model.shape
    part = rows // nfreq
    v, u, observed = col_factors[0], row_factors[0], data[0]

    beyond = lax.dynamic_slice_in_dim(v, half * odd, half, 0).reshape(-1, rows)
    start = model.astype(jnp.bfloat16)
    start = jnp.concatenate([start[: rows // 2], start[rows // 2 :]], axis=1)
    far = lax.ppermute(jnp.concatenate([beyond, start], axis=0), "tile", swaps)

    table = ranks[0]
    slot_ids = jnp.arange(slots, dtype=jnp.int32)
    opposite = jnp.clip(myself + jnp.where(odd == 1, WIDE, -WIDE), 0, ntile - 1)
    far_ranks = lax.dynamic_slice(table, (opposite, half * (1 - odd)), (1, half))[0]
    own_ranks = lax.dynamic_index_in_dim(table, myself, 0, keepdims=False)
    anchors = jnp.clip(myself + half - slot_ids, 0, ntile - 1)
    holder = jnp.arange(ntile, dtype=jnp.int32)[:, None] == anchors[None, :]
    row_ranks = jnp.sum(jnp.where(holder, table, 0), axis=0)
    scal = jnp.concatenate([jnp.stack([col, odd]), own_ranks, far_ranks, row_ranks])
    scal = jnp.pad(scal, (0, SCALARS - scal.shape[0]))

    gate_re, gate_im = gate_matrix(gate_window, nfreq)
    gate_re = jnp.concatenate([gate_re, gate_re], axis=-1)
    gate_im = jnp.concatenate([gate_im, gate_im], axis=-1)

    tiles = (slots, 2, levels, width)
    for step in range(ITERS):
        first = step == 0
        coef = kernel_call(
            functools.partial(coef_kernel, first=first), tiles, [scal], v, far, model
        )
        back = kernel_call(resid_kernel, tiles, [scal], spread(coef), u, observed)
        z = kernel_call(
            functools.partial(grad_kernel, first=first),
            (nfreq, 2, part, width),
            [scal, step_sizes],
            spread(back),
            v,
            far,
            model,
        )
        z = among_pair(z)
        if step == ITERS - 1:
            mixed = kernel_call(mix_kernel, (nfreq, 1, part, width), [], gate_re, gate_im, z)
            model = lax.all_to_all(mixed[:, 0], "freq", 0, 0, tiled=True)
        else:
            mixed = kernel_call(mix_kernel, z.shape, [], gate_re, gate_im, z)
            model = among_pair(mixed)
    return model.reshape(1, rows, width).astype(jnp.float32)


def solution(mesh):
    return jax.shard_map(
        on_device,
        mesh=mesh,
        in_specs=(
            P("freq", "tile", None),
            P("freq", "tile", None),
            P("freq", "tile", None, None, None),
            P("freq", "tile", None, None, None),
            P("freq", None, None),
            P(),
            P("freq"),
        ),
        out_specs=P("freq", "tile", None),
        check_vma=False,
    )
```

time: 124 us -> 128 us (1.032)
  the two profiles are of different devices: /device:TPU:129 before, /device:TPU:1 now
where the time goes in v3:
time: 128 us; the launch traced here: 127 us
  blocking collectives  79.2 us (62%)
  starting transfers between devices  20 us (16%)
  Pallas kernels  11.5 us (9%)
  waiting for transfers between devices  10.5 us (8%)
  local copies, waits for them, and re-layouts  2.95 us (2%)
  other arithmetic  2.27 us (2%)
    all_to_all x3, blocking collectives, spread(): lax.all_to_all(pieces, 'tile', 0, 0, tiled=True, axis_index_groups=groups)  48.9 us
    all_to_all x2, blocking collectives, among_pair(): lax.all_to_all(flat, ('freq', 'tile'), 0, 0, tiled=True, axis_index_group...  22.8 us
    all_to_all x1, starting transfers between devices, among_pair(): lax.all_to_all(flat, ('freq', 'tile'), 0, 0, tiled=True, axis_index_group...  15.8 us
    pallas_call x8, Pallas kernels, kernel_call(): pl.pallas_call(body, out_shape=jax.ShapeDtypeStruct(shape, jnp.bfloat16),...  11.5 us
    all_to_all x1, blocking collectives, on_device(): model = lax.all_to_all(mixed[:, 0], 'freq', 0, 0, tiled=True)  7.61 us
    all_to_all x1, waiting for transfers between devices, spread(): lax.all_to_all(pieces, 'tile', 0, 0, tiled=True, axis_index_groups=groups)  5.5 us
    all_to_all x1, waiting for transfers between devices, among_pair(): lax.all_to_all(flat, ('freq', 'tile'), 0, 0, tiled=True, axis_index_group...  4.99 us
    all_to_all x1, starting transfers between devices, spread(): lax.all_to_all(pieces, 'tile', 0, 0, tiled=True, axis_index_groups=groups)  3.47 us
  transfers between devices with their start and end apart: 3, of which 2 were waited for; matrix products, arithmetic and copies ran while one was open for 1% of the time, Pallas kernels for 0%

profile of v3, /device:TPU:1, one launch (start us, length us, event | category | flops | bytes accessed | tf_op | source)
XLA Modules:
  0.0 127.3 jit_solution(12191050916075675587)
XLA Ops:
  0.0 0.9 bitcast_convert_fusion.1
  0.9 1.1 constant_dynamic-slice_fusion
  2.1 0.7 collective-permute-start
  2.9 0.7 copy-done.4
  4.2 1.1 shard_map.73
  5.4 26.5 %all_to_all.40.got_ref = bf16[8,2,112,128]{3,2,1,0:T(8,128)(2,1)S(1)} all-to-all(bf16[8,2,112,128]{3,2,1,0:T(8,128)(2,1)S(1)} %shard_map.73), channel_id=1, replica_groups={{0,1,2,3,4,5,6,7},{8,9,10,11,12,13,14,15},{16,17,18,19,20,21,22,23},{24..., dimensions={0} | all-to-all | bytes 917504 | tf_op jit(solution)/shard_map/all_to_all | solution.py:216
  31.9 3.3 %shard_map.74 = bf16[8,2,112,128]{3,2,1,0:T(8,128)(2,1)} custom-call(s32[24]{0:T(128)S(1)} %pad.4.scal, bf16[8,2,112,128]{3,2,1,0:T(8,128)(2,1)S(1)} %all_to_all.40.got_ref, bf16[8,2,112,256]{3,2,1,0:T(8,128)(2,1)S(1)} %bitcast.32, bf16[256,128]{1,0:T(8,128)(2,1)S(1)} %bitcast.42), custom_call_target="tpu_custom_call" | custom-call | tf_op jit(solution)/shard_map/pallas_call | solution.py:180
  35.2 3.5 %all-to-all-start.1 = ((bf16[8,2,112,128]{3,2,1,0:T(8,128)(2,1)}), bf16[8,2,112,128]{3,2,1,0:T(8,128)(2,1)S(1)}, u32[]{:S(2)}, u32[]{:S(2)}) async-start(bf16[8,2,112,128]{3,2,1,0:T(8,128)(2,1)} %shard_map.74), calls=%async_computation.1 | async-start | bytes 917504 | tf_op jit(solution)/shard_map/all_to_all | solution.py:216
  39.3 0.7 copy-done.5
  40.0 5.5 %all-to-all-done.1.got_ref = bf16[8,2,112,128]{3,2,1,0:T(8,128)(2,1)S(1)} async-done(((bf16[8,2,112,128]{3,2,1,0:T(8,128)(2,1)}), bf16[8,2,112,128]{3,2,1,0:T(8,128)(2,1)S(1)}, u32[]{:S(2)}, u32[]{:S(2)}) %all-to-all-start.1) | async-done | bytes 458784 | tf_op jit(solution)/shard_map/all_to_all | solution.py:216
  45.5 1.9 %shard_map.75 = bf16[8,2,32,128]{3,2,1,0:T(8,128)(2,1)} custom-call(s32[24]{0:T(128)S(1)} %pad.4.scal, f32[1]{0:T(128)S(6)} %copy.8.size_ref, bf16[8,2,112,128]{3,2,1,0:T(8,128)(2,1)S(1)} %all-to-all-done.1.got_ref, bf16[8,2,112,256]{3,2,1,0:T(8,128)(2,1)S(1)} %bitcast.29, bf16[1024,256]{1,0:T(8,128)(2,1)S(1)} %collective-permute-done.far_ref, ...), custom_call_target="tpu_custom_call" | custom-call | tf_op jit(solution)/shard_map/pallas_call | solution.py:180
  47.4 15.8 %all-to-all-start.2 = ((bf16[16,32,128]{2,1,0:T(8,128)(2,1)}), bf16[16,32,128]{2,1,0:T(8,128)(2,1)S(1)}, u32[]{:S(2)}, u32[]{:S(2)}) async-start(bf16[16,32,128]{2,1,0:T(8,128)(2,1)} %bitcast.10), calls=%async_computation.2 | async-start | bytes 262144 | tf_op jit(solution)/shard_map/all_to_all | solution.py:220
  63.2 0.3 fusion.1
  63.6 5.0 %all-to-all-done.2 = bf16[16,32,128]{2,1,0:T(8,128)(2,1)S(1)} async-done(((bf16[16,32,128]{2,1,0:T(8,128)(2,1)}), bf16[16,32,128]{2,1,0:T(8,128)(2,1)S(1)}, u32[]{:S(2)}, u32[]{:S(2)}) %all-to-all-start.2) | async-done | bytes 131104 | tf_op jit(solution)/shard_map/all_to_all | solution.py:220
  68.6 0.2 shard_map.76
  68.8 10.4 %all_to_all.41 = bf16[16,32,128]{2,1,0:T(8,128)(2,1)S(1)} all-to-all(bf16[16,32,128]{2,1,0:T(8,128)(2,1)S(1)} %bitcast.40), channel_id=1, replica_groups={{60,0,124,64,188,128,252,192,316,256,380,320,444,384,508,448},{61,1,125..., dimensions={0} | all-to-all | bytes 262144 | tf_op jit(solution)/shard_map/all_to_all | solution.py:220
  79.2 1.1 shard_map.77
  80.4 10.6 %all_to_all.42.got_ref = bf16[8,2,112,128]{3,2,1,0:T(8,128)(2,1)S(1)} all-to-all(bf16[8,2,112,128]{3,2,1,0:T(8,128)(2,1)S(1)} %shard_map.77), channel_id=1, replica_groups={{0,1,2,3,4,5,6,7},{8,9,10,11,12,13,14,15},{16,17,18,19,20,21,22,23},{24..., dimensions={0} | all-to-all | bytes 917504 | tf_op jit(solution)/shard_map/all_to_all | solution.py:216
  91.0 2.5 %shard_map.78 = bf16[8,2,112,128]{3,2,1,0:T(8,128)(2,1)S(1)} custom-call(s32[24]{0:T(128)S(1)} %pad.4.scal, bf16[8,2,112,128]{3,2,1,0:T(8,128)(2,1)S(1)} %all_to_all.42.got_ref, bf16[8,2,112,256]{3,2,1,0:T(8,128)(2,1)S(1)} %bitcast.33, bf16[256,128]{1,0:T(8,128)(2,1)S(1)} %bitcast.43), custom_call_target="tpu_custom_call" | custom-call | tf_op jit(solution)/shard_map/pallas_call | solution.py:180
  93.5 11.7 %all_to_all.43.got_ref = bf16[8,2,112,128]{3,2,1,0:T(8,128)(2,1)S(1)} all-to-all(bf16[8,2,112,128]{3,2,1,0:T(8,128)(2,1)S(1)} %shard_map.78), channel_id=1, replica_groups={{0,1,2,3,4,5,6,7},{8,9,10,11,12,13,14,15},{16,17,18,19,20,21,22,23},{24..., dimensions={0} | all-to-all | bytes 917504 | tf_op jit(solution)/shard_map/all_to_all | solution.py:216
  105.3 1.2 shard_map.79
  106.5 12.3 %all_to_all.44 = bf16[16,32,128]{2,1,0:T(8,128)(2,1)S(1)} all-to-all(bf16[16,32,128]{2,1,0:T(8,128)(2,1)S(1)} %bitcast.41), channel_id=1, replica_groups={{60,0,124,64,188,128,252,192,316,256,380,320,444,384,508,448},{61,1,125..., dimensions={0} | all-to-all | bytes 262144 | tf_op jit(solution)/shard_map/all_to_all | solution.py:220
  119.0 7.6 %all_to_all.45 = bf16[8,32,128]{2,1,0:T(8,128)(2,1)S(1)} all-to-all(bf16[8,32,128]{2,1,0:T(8,128)(2,1)S(1)} %bitcast.44), channel_id=1, replica_groups=mesh['freq'=8,'tile'=64] {'freq'}, dimensions={0} | all-to-all | bytes 131072 | tf_op jit(solution)/shard_map/all_to_all | solution.py:269
  126.6 0.7 bitcast_convert_fusion
  (26 shorter events, 1.1 us)
Async XLA Ops:
  0.9 3.3 %copy-start = (bf16[1,8,2,112,256]{4,3,2,1,0:T(8,128)(2,1)S(1)}, bf16[1,8,2,112,256]{4,3,2,1,0:T(8,128)(2,1)}, u32[]{:S(2)}) copy-start(bf16[1,8,2,112,256]{4,3,2,1,0:T(8,128)(2,1)} %param.9) | copy-start | bytes 2752516
  2.1 2.1 %copy-start.2 = (f32[1,256,128]{2,1,0:T(8,128)S(1)}, f32[1,256,128]{2,1,0:T(8,128)}, u32[]{:S(2)}) copy-start(f32[1,256,128]{2,1,0:T(8,128)} %param.7) | copy-start | bytes 393220
  2.1 2.1 %collective-permute-start = (bf16[1024,256]{1,0:T(8,128)(2,1)S(1)}, bf16[1024,256]{1,0:T(8,128)(2,1)S(1)}, u32[]{:S(2)}, u32[]{:S(2)}) collective-permute-start(bf16[1024,256]{1,0:T(8,128)(2,1)S(1)} %maximum_maximum_fusion), channel_id=1, source_target_pairs={{4,8},{5,9},{6,10},{7,11},{8,4},{9,5},{10,6},{11,7},{12,16},{13,17... | collective-permute-start | bytes 1572872 | tf_op jit(solution)/shard_map/ppermute | solution.py:233
  2.9 0.7 copy-start.4
  4.2 27.6 %copy-start.3 = (bf16[1,256,128]{2,1,0:T(8,128)(2,1)S(1)}, bf16[1,256,128]{2,1,0:T(8,128)(2,1)}, u32[]{:S(2)}) copy-start(bf16[1,256,128]{2,1,0:T(8,128)(2,1)} %param.8) | copy-start | bytes 196612
  5.3 26.5 %copy-start.1 = (bf16[1,8,2,112,256]{4,3,2,1,0:T(8,128)(2,1)S(1)}, bf16[1,8,2,112,256]{4,3,2,1,0:T(8,128)(2,1)}, u32[]{:S(2)}) copy-start(bf16[1,8,2,112,256]{4,3,2,1,0:T(8,128)(2,1)} %param.10) | copy-start | bytes 2752516
  35.2 10.3 %all-to-all-start.1 = ((bf16[8,2,112,128]{3,2,1,0:T(8,128)(2,1)}), bf16[8,2,112,128]{3,2,1,0:T(8,128)(2,1)S(1)}, u32[]{:S(2)}, u32[]{:S(2)}) async-start(bf16[8,2,112,128]{3,2,1,0:T(8,128)(2,1)} %shard_map.74), calls=%async_computation.1 | async-start | bytes 917504 | tf_op jit(solution)/shard_map/all_to_all | solution.py:216
  39.3 0.7 copy-start.5
  47.4 21.3 %all-to-all-start.2 = ((bf16[16,32,128]{2,1,0:T(8,128)(2,1)}), bf16[16,32,128]{2,1,0:T(8,128)(2,1)S(1)}, u32[]{:S(2)}, u32[]{:S(2)}) async-start(bf16[16,32,128]{2,1,0:T(8,128)(2,1)} %bitcast.10), calls=%async_computation.2 | async-start | bytes 262144 | tf_op jit(solution)/shard_map/all_to_all | solution.py:220

commit v4 on v3

--- a/solution.py
+++ b/solution.py
@@ -59,9 +59,9 @@
     return jnp.concatenate([ref[j, side] for j in range(ref.shape[0])], axis=0)
 
 
-def far_factor(far_ref, index, which, levels):
-    start = (2 * index + which) * levels
-    return far_ref[start : start + levels, :]
+def far_factor(far_refs, index, which):
+    each = far_refs[0].shape[0]
+    return far_refs[index // each][index % each, which]
 
 
 def outward(col, s, odd):
@@ -72,33 +72,53 @@
     return column, same, near
 
 
-def coef_kernel(scal, v_ref, far_ref, x_ref, out_ref, *, first):
-    slots, _, levels, rows = v_ref.shape
+def beyond_kernel(scal, v_ref, x_ref, out_ref):
+    half = out_ref.shape[0]
+    x = x_ref[...].astype(jnp.bfloat16)
+    x_turn = turn_bf(x)
+    for i in range(half):
+        s = half * scal[ODD] + i
+        out_ref[i] = (dot(v_ref[s, 0], x) + dot(v_ref[s, 1], x_turn)).astype(jnp.bfloat16)
+
+
+def own_coefs(scal, v_ref, x, out_ref):
+    slots = v_ref.shape[0]
     half = slots // 2
     col, odd = scal[COL], scal[ODD]
-    if first:
-        x = x_ref[...].astype(jnp.bfloat16)
-        packed = far_ref[half * 2 * levels :, :]
-        width = x.shape[-1]
-        x_far = jnp.concatenate([packed[:, :width], packed[:, width:]], axis=0)
-    else:
-        x = side_of(x_ref, 1 - odd)
-        x_far = side_of(x_ref, odd)
-    x_turn, far_turn = turn_bf(x), turn_bf(x_far)
+    x_turn = turn_bf(x)
     for s in range(slots):
         column, same, _ = outward(col, s, odd)
         place = column + half * jnp.where(same, odd, 1 - odd)
         out_ref[place, 0] = keep(dot(v_ref[s, 0], x) + dot(v_ref[s, 1], x_turn), scal[OWN + s])
+
+
+def first_coef_kernel(scal, v_ref, x_ref, relay_ref, out_ref):
+    half = relay_ref.shape[0]
+    own_coefs(scal, v_ref, x_ref[...].astype(jnp.bfloat16), out_ref)
     for i in range(half):
-        column = (col + i) & 3
-        piece = dot(far_factor(far_ref, i, 0, levels), x_far)
-        piece += dot(far_factor(far_ref, i, 1, levels), far_turn)
+        column = (scal[COL] + i) & 3
+        piece = keep(relay_ref[i], scal[FAR + i])
+        out_ref[column, 1] = piece
+        out_ref[column + half, 1] = piece
+
+
+def coef_kernel(scal, v_ref, near_far_ref, last_far_ref, x_ref, out_ref):
+    half = v_ref.shape[0] // 2
+    odd = scal[ODD]
+    far_refs = (near_far_ref, last_far_ref)
+    x_far = side_of(x_ref, odd)
+    far_turn = turn_bf(x_far)
+    own_coefs(scal, v_ref, side_of(x_ref, 1 - odd), out_ref)
+    for i in range(half):
+        column = (scal[COL] + i) & 3
+        piece = dot(far_factor(far_refs, i, 0), x_far) + dot(far_factor(far_refs, i, 1), far_turn)
         piece = keep(piece, scal[FAR + i])
         out_ref[column, 1] = piece
         out_ref[column + half, 1] = piece
 
 
-def resid_kernel(scal, got_ref, u_ref, data_ref, out_ref):
+def resid_kernel(scal, got_ref, u_ref, data_ref, *rest):
+    out_ref = rest[-1]
     slots = u_ref.shape[0]
     half = slots // 2
     col, odd = scal[COL], scal[ODD]
@@ -127,7 +147,10 @@
             out_ref[column + half, 1] = piece
 
 
-def grad_kernel(scal, size_ref, got_ref, v_ref, far_ref, x_ref, out_ref, *, first):
+def grad_kernel(
+    scal, size_ref, got_ref, v_ref, near_far_ref, last_far_ref, x_ref, out_ref, *, first
+):
+    far_refs = (near_far_ref, last_far_ref)
     slots, _, levels, _ = v_ref.shape
     half = slots // 2
     col, odd = scal[COL], scal[ODD]
@@ -147,8 +170,8 @@
         column = (col + i) & 3
         valid = (col + i < half).astype(jnp.int32) == odd
         piece = keep(got_ref[column + half * odd, 1], jnp.where(valid, levels, 0))
-        far_real += left_dot(far_factor(far_ref, i, 0, levels), piece)
-        far_imag += left_dot(far_factor(far_ref, i, 1, levels), piece)
+        far_real += left_dot(far_factor(far_refs, i, 0), piece)
+        far_imag += left_dot(far_factor(far_refs, i, 1), piece)
     x = x_ref[...] if first else side_of(x_ref, 1 - odd).astype(jnp.float32)
     size = size_ref[0]
     mine = (x - size * (real - turn(imag))).astype(jnp.bfloat16)
@@ -227,10 +250,15 @@
     part = rows // nfreq
     v, u, observed = col_factors[0], row_factors[0], data[0]
 
-    beyond = lax.dynamic_slice_in_dim(v, half * odd, half, 0).reshape(-1, rows)
-    start = model.astype(jnp.bfloat16)
-    start = jnp.concatenate([start[: rows // 2], start[rows // 2 :]], axis=1)
-    far = lax.ppermute(jnp.concatenate([beyond, start], axis=0), "tile", swaps)
+    where = jnp.stack([col, odd])
+    relay = kernel_call(beyond_kernel, (half, levels, width), [where], v, model)
+    relay = lax.ppermute(relay, "tile", swaps)
+    fars = [
+        lax.ppermute(
+            lax.dynamic_slice_in_dim(v, half * odd + i, half // 2, 0), "tile", swaps
+        )
+        for i in (0, half // 2)
+    ]
 
     table = ranks[0]
     slot_ids = jnp.arange(slots, dtype=jnp.int32)
@@ -240,7 +268,7 @@
     anchors = jnp.clip(myself + half - slot_ids, 0, ntile - 1)
     holder = jnp.arange(ntile, dtype=jnp.int32)[:, None] == anchors[None, :]
     row_ranks = jnp.sum(jnp.where(holder, table, 0), axis=0)
-    scal = jnp.concatenate([jnp.stack([col, odd]), own_ranks, far_ranks, row_ranks])
+    scal = jnp.concatenate([where, own_ranks, far_ranks, row_ranks])
     scal = jnp.pad(scal, (0, SCALARS - scal.shape[0]))
 
     gate_re, gate_im = gate_matrix(gate_window, nfreq)
@@ -250,17 +278,19 @@
     tiles = (slots, 2, levels, width)
     for step in range(ITERS):
         first = step == 0
-        coef = kernel_call(
-            functools.partial(coef_kernel, first=first), tiles, [scal], v, far, model
-        )
-        back = kernel_call(resid_kernel, tiles, [scal], spread(coef), u, observed)
+        if first:
+            coef = kernel_call(first_coef_kernel, tiles, [scal], v, model, relay)
+            back = kernel_call(resid_kernel, tiles, [scal], spread(coef), u, observed, fars[0])
+        else:
+            coef = kernel_call(coef_kernel, tiles, [scal], v, *fars, model)
+            back = kernel_call(resid_kernel, tiles, [scal], spread(coef), u, observed)
         z = kernel_call(
             functools.partial(grad_kernel, first=first),
             (nfreq, 2, part, width),
             [scal, step_sizes],
             spread(back),
             v,
-            far,
+            *fars,
             model,
         )
         z = among_pair(z)

time: 128 us -> 125 us (0.977)
  the two profiles are of different devices: /device:TPU:1 before, /device:TPU:32 now
where the time goes in v4:
time: 125 us; the launch traced here: 124 us
  blocking collectives  58.8 us (47%)
  starting transfers between devices  31 us (25%)
  waiting for transfers between devices  15.8 us (13%)
  Pallas kernels  13.1 us (10%)
  local copies, waits for them, and re-layouts  3.25 us (3%)
  other arithmetic  1.4 us (1%)
    all_to_all x2, blocking collectives, spread(): lax.all_to_all(pieces, 'tile', 0, 0, tiled=True, axis_index_groups=groups)  26.5 us
    all_to_all x2, blocking collectives, among_pair(): lax.all_to_all(flat, ('freq', 'tile'), 0, 0, tiled=True, axis_index_group...  24.3 us
    pallas_call x9, Pallas kernels, kernel_call(): pl.pallas_call(body, out_shape=jax.ShapeDtypeStruct(shape, jnp.bfloat16),...  13.1 us
    all_to_all x2, starting transfers between devices, spread(): lax.all_to_all(pieces, 'tile', 0, 0, tiled=True, axis_index_groups=groups)  12 us
    ppermute x2, starting transfers between devices, on_device(): lax.ppermute(lax.dynamic_slice_in_dim(v, half * odd + i, half // 2, 0), '...  9.23 us
    all_to_all x1, blocking collectives, on_device(): model = lax.all_to_all(mixed[:, 0], 'freq', 0, 0, tiled=True)  8.04 us
    ppermute x2, waiting for transfers between devices, on_device(): lax.ppermute(lax.dynamic_slice_in_dim(v, half * odd + i, half // 2, 0), '...  7.93 us
    all_to_all x1, waiting for transfers between devices, among_pair(): lax.all_to_all(flat, ('freq', 'tile'), 0, 0, tiled=True, axis_index_group...  6.12 us
  transfers between devices with their start and end apart: 6, of which 4 were waited for; matrix products, arithmetic and copies ran while one was open for 1% of the time, Pallas kernels for 0%

profile of v4, /device:TPU:32, one launch (start us, length us, event | category | flops | bytes accessed | tf_op | source)
XLA Modules:
  0.0 124.3 jit_solution(3700130945797774943)
XLA Ops:
  0.1 1.2 copy-done
  1.3 0.9 copy-done.3
  2.2 0.9 shard_map.73
  3.0 3.8 %collective-permute-start.2 = (bf16[4,112,128]{2,1,0:T(8,128)(2,1)S(1)}, bf16[4,112,128]{2,1,0:T(8,128)(2,1)S(1)}, u32[]{:S(2)}, u32[]{:S(2)}) collective-permute-start(bf16[4,112,128]{2,1,0:T(8,128)(2,1)S(1)} %shard_map.73), channel_id=1, source_target_pairs={{4,8},{5,9},{6,10},{7,11},{8,4},{9,5},{10,6},{11,7},{12,16},{13,17... | collective-permute-start | bytes 344072 | tf_op jit(solution)/shard_map/ppermute | solution.py:255
  8.2 1.8 %collective-permute-done.2.relay_ref = bf16[4,112,128]{2,1,0:T(8,128)(2,1)S(1)} collective-permute-done((bf16[4,112,128]{2,1,0:T(8,128)(2,1)S(1)}, bf16[4,112,128]{2,1,0:T(8,128)(2,1)S(1)}, u32[]{:S(2)}, u32[]{:S(2)}) %collective-permute-start.2) | collective-permute-done | bytes 114720 | tf_op jit(solution)/shard_map/ppermute | solution.py:255
  10.0 1.8 %shard_map.74 = bf16[8,2,112,128]{3,2,1,0:T(8,128)(2,1)} custom-call(s32[24]{0:T(128)S(1)} %pad.4.scal, bf16[8,2,112,256]{3,2,1,0:T(8,128)(2,1)S(1)} %bitcast.31, f32[256,128]{1,0:T(8,128)S(1)} %bitcast.40, bf16[4,112,128]{2,1,0:T(8,128)(2,1)S(1)} %collective-permute-done.2.relay_ref), custom_call_target="tpu_custom_call" | custom-call | tf_op jit(solution)/shard_map/pallas_call | solution.py:203
  11.8 6.1 %all-to-all-start = ((bf16[8,2,112,128]{3,2,1,0:T(8,128)(2,1)}), bf16[8,2,112,128]{3,2,1,0:T(8,128)(2,1)S(1)}, u32[]{:S(2)}, u32[]{:S(2)}) async-start(bf16[8,2,112,128]{3,2,1,0:T(8,128)(2,1)} %shard_map.74), calls=%async_computation | async-start | bytes 917504 | tf_op jit(solution)/shard_map/all_to_all | solution.py:239
  17.9 4.9 %collective-permute-start = (bf16[2,2,112,256]{3,2,1,0:T(8,128)(2,1)S(1)}, bf16[2,2,112,256]{3,2,1,0:T(8,128)(2,1)S(1)}, u32[]{:S(2)}, u32[]{:S(2)}) collective-permute-start(bf16[2,2,112,256]{3,2,1,0:T(8,128)(2,1)S(1)} %get-tuple-element.8), channel_id=1, source_target_pairs={{4,8},{5,9},{6,10},{7,11},{8,4},{9,5},{10,6},{11,7},{12,16},{13,17... | collective-permute-start | bytes 688136 | tf_op jit(solution)/shard_map/ppermute | solution.py:257
  22.8 4.6 %collective-permute-done.rest_0_.near_far_ref = bf16[2,2,112,256]{3,2,1,0:T(8,128)(2,1)S(1)} collective-permute-done((bf16[2,2,112,256]{3,2,1,0:T(8,128)(2,1)S(1)}, bf16[2,2,112,256]{3,2,1,0:T(8,128)(2,1)S(1)}, u32[]{:S(2)}, u32[]{:S(2)}) %collective-permute-start) | collective-permute-done | bytes 229408 | tf_op jit(solution)/shard_map/ppermute | solution.py:257
  27.5 3.3 %shard_map.75 = bf16[8,2,112,128]{3,2,1,0:T(8,128)(2,1)} custom-call(s32[24]{0:T(128)S(1)} %pad.4.scal, bf16[8,2,112,128]{3,2,1,0:T(8,128)(2,1)S(1)} %all-to-all-done.got_ref, bf16[8,2,112,256]{3,2,1,0:T(8,128)(2,1)S(1)} %bitcast.35, bf16[256,128]{1,0:T(8,128)(2,1)S(1)} %bitcast.46, bf16[2,2,112,256]{3,2,1,0:T(8,128)(2,1)S(1)} %collective-permute-done.rest_0_.near_far_ref), custom_call_target="tpu_custom_call" | custom-call | tf_op jit(solution)/shard_map/pallas_call | solution.py:203
  30.8 6.0 %all-to-all-start.1 = ((bf16[8,2,112,128]{3,2,1,0:T(8,128)(2,1)}), bf16[8,2,112,128]{3,2,1,0:T(8,128)(2,1)S(1)}, u32[]{:S(2)}, u32[]{:S(2)}) async-start(bf16[8,2,112,128]{3,2,1,0:T(8,128)(2,1)} %shard_map.75), calls=%async_computation.1 | async-start | bytes 917504 | tf_op jit(solution)/shard_map/all_to_all | solution.py:239
  36.8 4.3 %collective-permute-start.1 = (bf16[2,2,112,256]{3,2,1,0:T(8,128)(2,1)S(1)}, bf16[2,2,112,256]{3,2,1,0:T(8,128)(2,1)S(1)}, u32[]{:S(2)}, u32[]{:S(2)}) collective-permute-start(bf16[2,2,112,256]{3,2,1,0:T(8,128)(2,1)S(1)} %get-tuple-element.7), channel_id=1, source_target_pairs={{4,8},{5,9},{6,10},{7,11},{8,4},{9,5},{10,6},{11,7},{12,16},{13,17... | collective-permute-start | bytes 688136 | tf_op jit(solution)/shard_map/ppermute | solution.py:257
  41.8 3.3 %collective-permute-done.1.last_far_ref = bf16[2,2,112,256]{3,2,1,0:T(8,128)(2,1)S(1)} collective-permute-done((bf16[2,2,112,256]{3,2,1,0:T(8,128)(2,1)S(1)}, bf16[2,2,112,256]{3,2,1,0:T(8,128)(2,1)S(1)}, u32[]{:S(2)}, u32[]{:S(2)}) %collective-permute-start.1) | collective-permute-done | bytes 229408 | tf_op jit(solution)/shard_map/ppermute | solution.py:257
  45.1 1.9 %shard_map.76 = bf16[8,2,32,128]{3,2,1,0:T(8,128)(2,1)} custom-call(s32[24]{0:T(128)S(1)} %pad.4.scal, f32[1]{0:T(128)S(6)} %copy.8.size_ref, bf16[8,2,112,128]{3,2,1,0:T(8,128)(2,1)S(1)} %all-to-all-done.1.got_ref, bf16[8,2,112,256]{3,2,1,0:T(8,128)(2,1)S(1)} %bitcast.32, bf16[2,2,112,256]{3,2,1,0:T(8,128)(2,1)S(1)} %collective-permute-done.rest_0_.near_far_ref, ...), custom_call_target="tpu_custom_call" | custom-call | tf_op jit(solution)/shard_map/pallas_call | solution.py:203
  47.0 6.0 %all-to-all-start.2 = ((bf16[16,32,128]{2,1,0:T(8,128)(2,1)}), bf16[16,32,128]{2,1,0:T(8,128)(2,1)S(1)}, u32[]{:S(2)}, u32[]{:S(2)}) async-start(bf16[16,32,128]{2,1,0:T(8,128)(2,1)} %bitcast.11), calls=%async_computation.2 | async-start | bytes 262144 | tf_op jit(solution)/shard_map/all_to_all | solution.py:243
  53.4 6.1 %all-to-all-done.2 = bf16[16,32,128]{2,1,0:T(8,128)(2,1)S(1)} async-done(((bf16[16,32,128]{2,1,0:T(8,128)(2,1)}), bf16[16,32,128]{2,1,0:T(8,128)(2,1)S(1)}, u32[]{:S(2)}, u32[]{:S(2)}) %all-to-all-start.2) | async-done | bytes 131104 | tf_op jit(solution)/shard_map/all_to_all | solution.py:243
  59.7 9.2 %all_to_all.40 = bf16[16,32,128]{2,1,0:T(8,128)(2,1)S(1)} all-to-all(bf16[16,32,128]{2,1,0:T(8,128)(2,1)S(1)} %bitcast.44), channel_id=1, replica_groups={{60,0,124,64,188,128,252,192,316,256,380,320,444,384,508,448},{61,1,125..., dimensions={0} | all-to-all | bytes 262144 | tf_op jit(solution)/shard_map/all_to_all | solution.py:243
  68.9 1.1 shard_map.78
  70.0 14.9 %all_to_all.41.got_ref = bf16[8,2,112,128]{3,2,1,0:T(8,128)(2,1)S(1)} all-to-all(bf16[8,2,112,128]{3,2,1,0:T(8,128)(2,1)S(1)} %shard_map.78), channel_id=1, replica_groups={{0,1,2,3,4,5,6,7},{8,9,10,11,12,13,14,15},{16,17,18,19,20,21,22,23},{24..., dimensions={0} | all-to-all | bytes 917504 | tf_op jit(solution)/shard_map/all_to_all | solution.py:239
  84.9 2.5 %shard_map.79 = bf16[8,2,112,128]{3,2,1,0:T(8,128)(2,1)S(1)} custom-call(s32[24]{0:T(128)S(1)} %pad.4.scal, bf16[8,2,112,128]{3,2,1,0:T(8,128)(2,1)S(1)} %all_to_all.41.got_ref, bf16[8,2,112,256]{3,2,1,0:T(8,128)(2,1)S(1)} %bitcast.36, bf16[256,128]{1,0:T(8,128)(2,1)S(1)} %bitcast.47), custom_call_target="tpu_custom_call" | custom-call | tf_op jit(solution)/shard_map/pallas_call | solution.py:203
  87.4 11.6 %all_to_all.42.got_ref = bf16[8,2,112,128]{3,2,1,0:T(8,128)(2,1)S(1)} all-to-all(bf16[8,2,112,128]{3,2,1,0:T(8,128)(2,1)S(1)} %shard_map.79), channel_id=1, replica_groups={{0,1,2,3,4,5,6,7},{8,9,10,11,12,13,14,15},{16,17,18,19,20,21,22,23},{24..., dimensions={0} | all-to-all | bytes 917504 | tf_op jit(solution)/shard_map/all_to_all | solution.py:239
  99.1 1.2 shard_map.80
  100.3 15.1 %all_to_all.43 = bf16[16,32,128]{2,1,0:T(8,128)(2,1)S(1)} all-to-all(bf16[16,32,128]{2,1,0:T(8,128)(2,1)S(1)} %bitcast.45), channel_id=1, replica_groups={{60,0,124,64,188,128,252,192,316,256,380,320,444,384,508,448},{61,1,125..., dimensions={0} | all-to-all | bytes 262144 | tf_op jit(solution)/shard_map/all_to_all | solution.py:243
  115.6 8.0 %all_to_all.44 = bf16[8,32,128]{2,1,0:T(8,128)(2,1)S(1)} all-to-all(bf16[8,32,128]{2,1,0:T(8,128)(2,1)S(1)} %bitcast.48), channel_id=1, replica_groups=mesh['freq'=8,'tile'=64] {'freq'}, dimensions={0} | all-to-all | bytes 131072 | tf_op jit(solution)/shard_map/all_to_all | solution.py:299
  (34 shorter events, 3.0 us)
Async XLA Ops:
  0.1 1.2 copy-start
  1.3 0.9 copy-start.3
  2.2 7.8 %copy-start.1 = (bf16[1,8,2,112,256]{4,3,2,1,0:T(8,128)(2,1)S(1)}, bf16[1,8,2,112,256]{4,3,2,1,0:T(8,128)(2,1)}, u32[]{:S(2)}) copy-start(bf16[1,8,2,112,256]{4,3,2,1,0:T(8,128)(2,1)} %param.9) | copy-start | bytes 2752516
  2.2 7.8 %copy-start.4 = (f32[1,256,128]{2,1,0:T(8,128)S(1)}, f32[1,256,128]{2,1,0:T(8,128)}, u32[]{:S(2)}) copy-start(f32[1,256,128]{2,1,0:T(8,128)} %param.7) | copy-start | bytes 393220
  3.0 7.0 %collective-permute-start.2 = (bf16[4,112,128]{2,1,0:T(8,128)(2,1)S(1)}, bf16[4,112,128]{2,1,0:T(8,128)(2,1)S(1)}, u32[]{:S(2)}, u32[]{:S(2)}) collective-permute-start(bf16[4,112,128]{2,1,0:T(8,128)(2,1)S(1)} %shard_map.73), channel_id=1, source_target_pairs={{4,8},{5,9},{6,10},{7,11},{8,4},{9,5},{10,6},{11,7},{12,16},{13,17... | collective-permute-start | bytes 344072 | tf_op jit(solution)/shard_map/ppermute | solution.py:255
  6.9 0.7 copy-start.6
  11.8 15.7 %copy-start.2 = (bf16[1,8,2,112,256]{4,3,2,1,0:T(8,128)(2,1)S(1)}, bf16[1,8,2,112,256]{4,3,2,1,0:T(8,128)(2,1)}, u32[]{:S(2)}) copy-start(bf16[1,8,2,112,256]{4,3,2,1,0:T(8,128)(2,1)} %param.10) | copy-start | bytes 2752516
  11.8 15.7 %all-to-all-start = ((bf16[8,2,112,128]{3,2,1,0:T(8,128)(2,1)}), bf16[8,2,112,128]{3,2,1,0:T(8,128)(2,1)S(1)}, u32[]{:S(2)}, u32[]{:S(2)}) async-start(bf16[8,2,112,128]{3,2,1,0:T(8,128)(2,1)} %shard_map.74), calls=%async_computation | async-start | bytes 917504 | tf_op jit(solution)/shard_map/all_to_all | solution.py:239
  17.9 9.6 %copy-start.5 = (bf16[1,256,128]{2,1,0:T(8,128)(2,1)S(1)}, bf16[1,256,128]{2,1,0:T(8,128)(2,1)}, u32[]{:S(2)}) copy-start(bf16[1,256,128]{2,1,0:T(8,128)(2,1)} %param.8) | copy-start | bytes 196612
  17.9 9.6 %collective-permute-start = (bf16[2,2,112,256]{3,2,1,0:T(8,128)(2,1)S(1)}, bf16[2,2,112,256]{3,2,1,0:T(8,128)(2,1)S(1)}, u32[]{:S(2)}, u32[]{:S(2)}) collective-permute-start(bf16[2,2,112,256]{3,2,1,0:T(8,128)(2,1)S(1)} %get-tuple-element.8), channel_id=1, source_target_pairs={{4,8},{5,9},{6,10},{7,11},{8,4},{9,5},{10,6},{11,7},{12,16},{13,17... | collective-permute-start | bytes 688136 | tf_op jit(solution)/shard_map/ppermute | solution.py:257
  30.8 14.2 %all-to-all-start.1 = ((bf16[8,2,112,128]{3,2,1,0:T(8,128)(2,1)}), bf16[8,2,112,128]{3,2,1,0:T(8,128)(2,1)S(1)}, u32[]{:S(2)}, u32[]{:S(2)}) async-start(bf16[8,2,112,128]{3,2,1,0:T(8,128)(2,1)} %shard_map.75), calls=%async_computation.1 | async-start | bytes 917504 | tf_op jit(solution)/shard_map/all_to_all | solution.py:239
  36.8 4.3 %copy-start.7 = (s32[64,2]{0,1:T(2,128)S(1)}, s32[64,2]{0,1:T(2,128)}, u32[]{:S(2)}) copy-start(s32[64,2]{0,1:T(2,128)} %param.12) | copy-start | bytes 1540
  36.8 8.3 %collective-permute-start.1 = (bf16[2,2,112,256]{3,2,1,0:T(8,128)(2,1)S(1)}, bf16[2,2,112,256]{3,2,1,0:T(8,128)(2,1)S(1)}, u32[]{:S(2)}, u32[]{:S(2)}) collective-permute-start(bf16[2,2,112,256]{3,2,1,0:T(8,128)(2,1)S(1)} %get-tuple-element.7), channel_id=1, source_target_pairs={{4,8},{5,9},{6,10},{7,11},{8,4},{9,5},{10,6},{11,7},{12,16},{13,17... | collective-permute-start | bytes 688136 | tf_op jit(solution)/shard_map/ppermute | solution.py:257
  47.0 12.6 %all-to-all-start.2 = ((bf16[16,32,128]{2,1,0:T(8,128)(2,1)}), bf16[16,32,128]{2,1,0:T(8,128)(2,1)S(1)}, u32[]{:S(2)}, u32[]{:S(2)}) async-start(bf16[16,32,128]{2,1,0:T(8,128)(2,1)} %bitcast.11), calls=%async_computation.2 | async-start | bytes 262144 | tf_op jit(solution)/shard_map/all_to_all | solution.py:243

commit v5 on v4

--- a/solution.py
+++ b/solution.py
@@ -72,13 +72,15 @@
     return column, same, near
 
 
-def beyond_kernel(scal, v_ref, x_ref, out_ref):
+def beyond_kernel(scal, v_ref, x_ref, out_ref, *far_refs):
     half = out_ref.shape[0]
+    each = far_refs[0].shape[0]
     x = x_ref[...].astype(jnp.bfloat16)
     x_turn = turn_bf(x)
     for i in range(half):
         s = half * scal[ODD] + i
         out_ref[i] = (dot(v_ref[s, 0], x) + dot(v_ref[s, 1], x_turn)).astype(jnp.bfloat16)
+        far_refs[i // each][i % each] = v_ref[s]
 
 
 def own_coefs(scal, v_ref, x, out_ref):
@@ -139,12 +141,9 @@
         column = (col + slots - s) & 3
         same = ((col + slots - s) >> 2) == 1
         piece = keep(dot(u_ref[s, 0], resid) - dot(u_ref[s, 1], resid_turn), scal[ROW + s])
-        out_ref[column + half * jnp.where(same, odd, 1 - odd), 0] = piece
-
-        @pl.when(jnp.logical_not(same))
-        def _():
-            out_ref[column, 1] = piece
-            out_ref[column + half, 1] = piece
+        place = column + half * jnp.where(same, odd, 1 - odd)
+        out_ref[place, 0] = piece
+        out_ref[(place + half) & (slots - 1), 1] = piece
 
 
 def grad_kernel(
@@ -200,11 +199,13 @@
 def kernel_call(body, shape, scalars, *operands):
     smem = pl.BlockSpec(memory_space=pltpu.SMEM)
     vmem = pl.BlockSpec(memory_space=pltpu.VMEM)
+    several = isinstance(shape, list)
+    outs = [jax.ShapeDtypeStruct(s, jnp.bfloat16) for s in (shape if several else [shape])]
     return pl.pallas_call(
         body,
-        out_shape=jax.ShapeDtypeStruct(shape, jnp.bfloat16),
+        out_shape=outs if several else outs[0],
         in_specs=[smem] * len(scalars) + [vmem] * len(operands),
-        out_specs=vmem,
+        out_specs=[vmem] * len(outs) if several else vmem,
         compiler_params=pltpu.CompilerParams(vmem_limit_bytes=VMEM_BYTES),
     )(*scalars, *operands)
 
@@ -251,14 +252,15 @@
     v, u, observed = col_factors[0], row_factors[0], data[0]
 
     where = jnp.stack([col, odd])
-    relay = kernel_call(beyond_kernel, (half, levels, width), [where], v, model)
+    relay, *fars = kernel_call(
+        beyond_kernel,
+        [(half, levels, width)] + [(half // 2, 2, levels, rows)] * 2,
+        [where],
+        v,
+        model,
+    )
     relay = lax.ppermute(relay, "tile", swaps)
-    fars = [
-        lax.ppermute(
-            lax.dynamic_slice_in_dim(v, half * odd + i, half // 2, 0), "tile", swaps
-        )
-        for i in (0, half // 2)
-    ]
+    fars = [lax.ppermute(far, "tile", swaps) for far in fars]
 
     table = ranks[0]
     slot_ids = jnp.arange(slots, dtype=jnp.int32)

time: 125 us -> 123 us (0.984)
  Pallas kernels: 13.1 us -> 11.1 us
    pallas_call x9, Pallas kernels: 13.1 us -> 11.1 us  [kernel_call(): pl.pallas_call(body, out_shape=outs if several else outs[0], in_specs=[sm...]
where the time goes in v5:
time: 123 us; the launch traced here: 122 us
  blocking collectives  58.8 us (48%)
  starting transfers between devices  31 us (25%)
  waiting for transfers between devices  15.8 us (13%)
  Pallas kernels  11.1 us (9%)
  local copies, waits for them, and re-layouts  3.23 us (3%)
  other arithmetic  1.4 us (1%)
    all_to_all x2, blocking collectives, spread(): lax.all_to_all(pieces, 'tile', 0, 0, tiled=True, axis_index_groups=groups)  26.5 us
    all_to_all x2, blocking collectives, among_pair(): lax.all_to_all(flat, ('freq', 'tile'), 0, 0, tiled=True, axis_index_group...  24.3 us
    all_to_all x2, starting transfers between devices, spread(): lax.all_to_all(pieces, 'tile', 0, 0, tiled=True, axis_index_groups=groups)  12 us
    pallas_call x9, Pallas kernels, kernel_call(): pl.pallas_call(body, out_shape=outs if several else outs[0], in_specs=[sm...  11.1 us
    ppermute x2, starting transfers between devices, on_device(): fars = [lax.ppermute(far, 'tile', swaps) for far in fars]  9.21 us
    all_to_all x1, blocking collectives, on_device(): model = lax.all_to_all(mixed[:, 0], 'freq', 0, 0, tiled=True)  8.04 us
    ppermute x2, waiting for transfers between devices, on_device(): fars = [lax.ppermute(far, 'tile', swaps) for far in fars]  7.92 us
    all_to_all x1, waiting for transfers between devices, among_pair(): lax.all_to_all(flat, ('freq', 'tile'), 0, 0, tiled=True, axis_index_group...  6.12 us
  transfers between devices with their start and end apart: 6, of which 4 were waited for; matrix products, arithmetic and copies ran while one was open for 1% of the time, Pallas kernels for 0%

profile of v5, /device:TPU:32, one launch (start us, length us, event | category | flops | bytes accessed | tf_op | source)
XLA Modules:
  0.0 122.3 jit_solution(13997534308280713066)
XLA Ops:
  0.1 1.2 copy-done
  1.3 0.9 copy-done.3
  2.2 0.9 shard_map.73
  3.0 3.8 %collective-permute-start.2 = (bf16[4,112,128]{2,1,0:T(8,128)(2,1)S(1)}, bf16[4,112,128]{2,1,0:T(8,128)(2,1)S(1)}, u32[]{:S(2)}, u32[]{:S(2)}) collective-permute-start(bf16[4,112,128]{2,1,0:T(8,128)(2,1)S(1)} %get-tuple-element.10), channel_id=1, source_target_pairs={{4,8},{5,9},{6,10},{7,11},{8,4},{9,5},{10,6},{11,7},{12,16},{13,17... | collective-permute-start | bytes 344072 | tf_op jit(solution)/shard_map/ppermute | solution.py:262
  8.2 1.8 %collective-permute-done.2.relay_ref = bf16[4,112,128]{2,1,0:T(8,128)(2,1)S(1)} collective-permute-done((bf16[4,112,128]{2,1,0:T(8,128)(2,1)S(1)}, bf16[4,112,128]{2,1,0:T(8,128)(2,1)S(1)}, u32[]{:S(2)}, u32[]{:S(2)}) %collective-permute-start.2) | collective-permute-done | bytes 114720 | tf_op jit(solution)/shard_map/ppermute | solution.py:262
  10.0 1.8 %shard_map.74 = bf16[8,2,112,128]{3,2,1,0:T(8,128)(2,1)} custom-call(s32[24]{0:T(128)S(1)} %pad.4.scal, bf16[8,2,112,256]{3,2,1,0:T(8,128)(2,1)S(1)} %bitcast.27, f32[256,128]{1,0:T(8,128)S(1)} %bitcast.36, bf16[4,112,128]{2,1,0:T(8,128)(2,1)S(1)} %collective-permute-done.2.relay_ref), custom_call_target="tpu_custom_call" | custom-call | tf_op jit(solution)/shard_map/pallas_call | solution.py:204
  11.8 6.1 %all-to-all-start = ((bf16[8,2,112,128]{3,2,1,0:T(8,128)(2,1)}), bf16[8,2,112,128]{3,2,1,0:T(8,128)(2,1)S(1)}, u32[]{:S(2)}, u32[]{:S(2)}) async-start(bf16[8,2,112,128]{3,2,1,0:T(8,128)(2,1)} %shard_map.74), calls=%async_computation | async-start | bytes 917504 | tf_op jit(solution)/shard_map/all_to_all | solution.py:240
  17.9 4.9 %collective-permute-start = (bf16[2,2,112,256]{3,2,1,0:T(8,128)(2,1)S(1)}, bf16[2,2,112,256]{3,2,1,0:T(8,128)(2,1)S(1)}, u32[]{:S(2)}, u32[]{:S(2)}) collective-permute-start(bf16[2,2,112,256]{3,2,1,0:T(8,128)(2,1)S(1)} %get-tuple-element.8), channel_id=1, source_target_pairs={{4,8},{5,9},{6,10},{7,11},{8,4},{9,5},{10,6},{11,7},{12,16},{13,17... | collective-permute-start | bytes 688136 | tf_op jit(solution)/shard_map/ppermute | solution.py:263
  22.8 4.6 %collective-permute-done.rest_0_.near_far_ref = bf16[2,2,112,256]{3,2,1,0:T(8,128)(2,1)S(1)} collective-permute-done((bf16[2,2,112,256]{3,2,1,0:T(8,128)(2,1)S(1)}, bf16[2,2,112,256]{3,2,1,0:T(8,128)(2,1)S(1)}, u32[]{:S(2)}, u32[]{:S(2)}) %collective-permute-start) | collective-permute-done | bytes 229408 | tf_op jit(solution)/shard_map/ppermute | solution.py:263
  27.4 2.3 %shard_map.75 = bf16[8,2,112,128]{3,2,1,0:T(8,128)(2,1)} custom-call(s32[24]{0:T(128)S(1)} %pad.4.scal, bf16[8,2,112,128]{3,2,1,0:T(8,128)(2,1)S(1)} %all-to-all-done.got_ref, bf16[8,2,112,256]{3,2,1,0:T(8,128)(2,1)S(1)} %bitcast.31, bf16[256,128]{1,0:T(8,128)(2,1)S(1)} %bitcast.42, bf16[2,2,112,256]{3,2,1,0:T(8,128)(2,1)S(1)} %collective-permute-done.rest_0_.near_far_ref), custom_call_target="tpu_custom_call" | custom-call | tf_op jit(solution)/shard_map/pallas_call | solution.py:204
  29.8 6.0 %all-to-all-start.1 = ((bf16[8,2,112,128]{3,2,1,0:T(8,128)(2,1)}), bf16[8,2,112,128]{3,2,1,0:T(8,128)(2,1)S(1)}, u32[]{:S(2)}, u32[]{:S(2)}) async-start(bf16[8,2,112,128]{3,2,1,0:T(8,128)(2,1)} %shard_map.75), calls=%async_computation.1 | async-start | bytes 917504 | tf_op jit(solution)/shard_map/all_to_all | solution.py:240
  35.7 4.3 %collective-permute-start.1 = (bf16[2,2,112,256]{3,2,1,0:T(8,128)(2,1)S(1)}, bf16[2,2,112,256]{3,2,1,0:T(8,128)(2,1)S(1)}, u32[]{:S(2)}, u32[]{:S(2)}) collective-permute-start(bf16[2,2,112,256]{3,2,1,0:T(8,128)(2,1)S(1)} %get-tuple-element.9), channel_id=1, source_target_pairs={{4,8},{5,9},{6,10},{7,11},{8,4},{9,5},{10,6},{11,7},{12,16},{13,17... | collective-permute-start | bytes 688136 | tf_op jit(solution)/shard_map/ppermute | solution.py:263
  40.7 3.3 %collective-permute-done.1.last_far_ref = bf16[2,2,112,256]{3,2,1,0:T(8,128)(2,1)S(1)} collective-permute-done((bf16[2,2,112,256]{3,2,1,0:T(8,128)(2,1)S(1)}, bf16[2,2,112,256]{3,2,1,0:T(8,128)(2,1)S(1)}, u32[]{:S(2)}, u32[]{:S(2)}) %collective-permute-start.1) | collective-permute-done | bytes 229408 | tf_op jit(solution)/shard_map/ppermute | solution.py:263
  44.0 1.9 %shard_map.76 = bf16[8,2,32,128]{3,2,1,0:T(8,128)(2,1)} custom-call(s32[24]{0:T(128)S(1)} %pad.4.scal, f32[1]{0:T(128)S(6)} %copy.8.size_ref, bf16[8,2,112,128]{3,2,1,0:T(8,128)(2,1)S(1)} %all-to-all-done.1.got_ref, bf16[8,2,112,256]{3,2,1,0:T(8,128)(2,1)S(1)} %bitcast.28, bf16[2,2,112,256]{3,2,1,0:T(8,128)(2,1)S(1)} %collective-permute-done.rest_0_.near_far_ref, ...), custom_call_target="tpu_custom_call" | custom-call | tf_op jit(solution)/shard_map/pallas_call | solution.py:204
  45.9 6.0 %all-to-all-start.2 = ((bf16[16,32,128]{2,1,0:T(8,128)(2,1)}), bf16[16,32,128]{2,1,0:T(8,128)(2,1)S(1)}, u32[]{:S(2)}, u32[]{:S(2)}) async-start(bf16[16,32,128]{2,1,0:T(8,128)(2,1)} %bitcast.9), calls=%async_computation.2 | async-start | bytes 262144 | tf_op jit(solution)/shard_map/all_to_all | solution.py:244
  52.3 6.1 %all-to-all-done.2 = bf16[16,32,128]{2,1,0:T(8,128)(2,1)S(1)} async-done(((bf16[16,32,128]{2,1,0:T(8,128)(2,1)}), bf16[16,32,128]{2,1,0:T(8,128)(2,1)S(1)}, u32[]{:S(2)}, u32[]{:S(2)}) %all-to-all-start.2) | async-done | bytes 131104 | tf_op jit(solution)/shard_map/all_to_all | solution.py:244
  58.7 9.2 %all_to_all.40 = bf16[16,32,128]{2,1,0:T(8,128)(2,1)S(1)} all-to-all(bf16[16,32,128]{2,1,0:T(8,128)(2,1)S(1)} %bitcast.40), channel_id=1, replica_groups={{60,0,124,64,188,128,252,192,316,256,380,320,444,384,508,448},{61,1,125..., dimensions={0} | all-to-all | bytes 262144 | tf_op jit(solution)/shard_map/all_to_all | solution.py:244
  67.9 1.1 shard_map.78
  69.0 14.9 %all_to_all.41.got_ref = bf16[8,2,112,128]{3,2,1,0:T(8,128)(2,1)S(1)} all-to-all(bf16[8,2,112,128]{3,2,1,0:T(8,128)(2,1)S(1)} %shard_map.78), channel_id=1, replica_groups={{0,1,2,3,4,5,6,7},{8,9,10,11,12,13,14,15},{16,17,18,19,20,21,22,23},{24..., dimensions={0} | all-to-all | bytes 917504 | tf_op jit(solution)/shard_map/all_to_all | solution.py:240
  83.9 1.5 %shard_map.79 = bf16[8,2,112,128]{3,2,1,0:T(8,128)(2,1)S(1)} custom-call(s32[24]{0:T(128)S(1)} %pad.4.scal, bf16[8,2,112,128]{3,2,1,0:T(8,128)(2,1)S(1)} %all_to_all.41.got_ref, bf16[8,2,112,256]{3,2,1,0:T(8,128)(2,1)S(1)} %bitcast.32, bf16[256,128]{1,0:T(8,128)(2,1)S(1)} %bitcast.43), custom_call_target="tpu_custom_call" | custom-call | tf_op jit(solution)/shard_map/pallas_call | solution.py:204
  85.4 11.6 %all_to_all.42.got_ref = bf16[8,2,112,128]{3,2,1,0:T(8,128)(2,1)S(1)} all-to-all(bf16[8,2,112,128]{3,2,1,0:T(8,128)(2,1)S(1)} %shard_map.79), channel_id=1, replica_groups={{0,1,2,3,4,5,6,7},{8,9,10,11,12,13,14,15},{16,17,18,19,20,21,22,23},{24..., dimensions={0} | all-to-all | bytes 917504 | tf_op jit(solution)/shard_map/all_to_all | solution.py:240
  97.1 1.2 %shard_map.80 = bf16[8,2,32,128]{3,2,1,0:T(8,128)(2,1)S(1)} custom-call(s32[24]{0:T(128)S(1)} %pad.4.scal, f32[1]{0:T(128)S(6)} %copy.8.size_ref, bf16[8,2,112,128]{3,2,1,0:T(8,128)(2,1)S(1)} %all_to_all.42.got_ref, bf16[8,2,112,256]{3,2,1,0:T(8,128)(2,1)S(1)} %bitcast.30, bf16[2,2,112,256]{3,2,1,0:T(8,128)(2,1)S(1)} %collective-permute-done.rest_0_.near_far_ref, ...), custom_call_target="tpu_custom_call" | custom-call | tf_op jit(solution)/shard_map/pallas_call | solution.py:204
  98.3 15.1 %all_to_all.43 = bf16[16,32,128]{2,1,0:T(8,128)(2,1)S(1)} all-to-all(bf16[16,32,128]{2,1,0:T(8,128)(2,1)S(1)} %bitcast.41), channel_id=1, replica_groups={{60,0,124,64,188,128,252,192,316,256,380,320,444,384,508,448},{61,1,125..., dimensions={0} | all-to-all | bytes 262144 | tf_op jit(solution)/shard_map/all_to_all | solution.py:244
  113.6 8.0 %all_to_all.44 = bf16[8,32,128]{2,1,0:T(8,128)(2,1)S(1)} all-to-all(bf16[8,32,128]{2,1,0:T(8,128)(2,1)S(1)} %bitcast.44), channel_id=1, replica_groups=mesh['freq'=8,'tile'=64] {'freq'}, dimensions={0} | all-to-all | bytes 131072 | tf_op jit(solution)/shard_map/all_to_all | solution.py:301
  (33 shorter events, 2.9 us)
Async XLA Ops:
  0.1 1.2 copy-start
  1.3 0.9 copy-start.3
  2.2 7.8 %copy-start.1 = (bf16[1,8,2,112,256]{4,3,2,1,0:T(8,128)(2,1)S(1)}, bf16[1,8,2,112,256]{4,3,2,1,0:T(8,128)(2,1)}, u32[]{:S(2)}) copy-start(bf16[1,8,2,112,256]{4,3,2,1,0:T(8,128)(2,1)} %param.9) | copy-start | bytes 2752516
  2.2 7.8 %copy-start.4 = (f32[1,256,128]{2,1,0:T(8,128)S(1)}, f32[1,256,128]{2,1,0:T(8,128)}, u32[]{:S(2)}) copy-start(f32[1,256,128]{2,1,0:T(8,128)} %param.7) | copy-start | bytes 393220
  3.0 7.0 %collective-permute-start.2 = (bf16[4,112,128]{2,1,0:T(8,128)(2,1)S(1)}, bf16[4,112,128]{2,1,0:T(8,128)(2,1)S(1)}, u32[]{:S(2)}, u32[]{:S(2)}) collective-permute-start(bf16[4,112,128]{2,1,0:T(8,128)(2,1)S(1)} %get-tuple-element.10), channel_id=1, source_target_pairs={{4,8},{5,9},{6,10},{7,11},{8,4},{9,5},{10,6},{11,7},{12,16},{13,17... | collective-permute-start | bytes 344072 | tf_op jit(solution)/shard_map/ppermute | solution.py:262
  6.9 0.7 copy-start.6
  8.2 19.2 %copy-start.2 = (bf16[1,8,2,112,256]{4,3,2,1,0:T(8,128)(2,1)S(1)}, bf16[1,8,2,112,256]{4,3,2,1,0:T(8,128)(2,1)}, u32[]{:S(2)}) copy-start(bf16[1,8,2,112,256]{4,3,2,1,0:T(8,128)(2,1)} %param.10) | copy-start | bytes 2752516
  11.8 15.6 %copy-start.5 = (bf16[1,256,128]{2,1,0:T(8,128)(2,1)S(1)}, bf16[1,256,128]{2,1,0:T(8,128)(2,1)}, u32[]{:S(2)}) copy-start(bf16[1,256,128]{2,1,0:T(8,128)(2,1)} %param.8) | copy-start | bytes 196612
  11.8 15.6 %all-to-all-start = ((bf16[8,2,112,128]{3,2,1,0:T(8,128)(2,1)}), bf16[8,2,112,128]{3,2,1,0:T(8,128)(2,1)S(1)}, u32[]{:S(2)}, u32[]{:S(2)}) async-start(bf16[8,2,112,128]{3,2,1,0:T(8,128)(2,1)} %shard_map.74), calls=%async_computation | async-start | bytes 917504 | tf_op jit(solution)/shard_map/all_to_all | solution.py:240
  17.9 9.6 %collective-permute-start = (bf16[2,2,112,256]{3,2,1,0:T(8,128)(2,1)S(1)}, bf16[2,2,112,256]{3,2,1,0:T(8,128)(2,1)S(1)}, u32[]{:S(2)}, u32[]{:S(2)}) collective-permute-start(bf16[2,2,112,256]{3,2,1,0:T(8,128)(2,1)S(1)} %get-tuple-element.8), channel_id=1, source_target_pairs={{4,8},{5,9},{6,10},{7,11},{8,4},{9,5},{10,6},{11,7},{12,16},{13,17... | collective-permute-start | bytes 688136 | tf_op jit(solution)/shard_map/ppermute | solution.py:263
  29.8 14.3 %all-to-all-start.1 = ((bf16[8,2,112,128]{3,2,1,0:T(8,128)(2,1)}), bf16[8,2,112,128]{3,2,1,0:T(8,128)(2,1)S(1)}, u32[]{:S(2)}, u32[]{:S(2)}) async-start(bf16[8,2,112,128]{3,2,1,0:T(8,128)(2,1)} %shard_map.75), calls=%async_computation.1 | async-start | bytes 917504 | tf_op jit(solution)/shard_map/all_to_all | solution.py:240
  35.7 4.3 %copy-start.7 = (s32[64,2]{0,1:T(2,128)S(1)}, s32[64,2]{0,1:T(2,128)}, u32[]{:S(2)}) copy-start(s32[64,2]{0,1:T(2,128)} %param.12) | copy-start | bytes 1540
  35.7 8.3 %collective-permute-start.1 = (bf16[2,2,112,256]{3,2,1,0:T(8,128)(2,1)S(1)}, bf16[2,2,112,256]{3,2,1,0:T(8,128)(2,1)S(1)}, u32[]{:S(2)}, u32[]{:S(2)}) collective-permute-start(bf16[2,2,112,256]{3,2,1,0:T(8,128)(2,1)S(1)} %get-tuple-element.9), channel_id=1, source_target_pairs={{4,8},{5,9},{6,10},{7,11},{8,4},{9,5},{10,6},{11,7},{12,16},{13,17... | collective-permute-start | bytes 688136 | tf_op jit(solution)/shard_map/ppermute | solution.py:263
  45.9 12.6 %all-to-all-start.2 = ((bf16[16,32,128]{2,1,0:T(8,128)(2,1)}), bf16[16,32,128]{2,1,0:T(8,128)(2,1)S(1)}, u32[]{:S(2)}, u32[]{:S(2)}) async-start(bf16[16,32,128]{2,1,0:T(8,128)(2,1)} %bitcast.9), calls=%async_computation.2 | async-start | bytes 262144 | tf_op jit(solution)/shard_map/all_to_all | solution.py:244

commit v6 on v5

--- a/solution.py
+++ b/solution.py
@@ -12,6 +12,7 @@
 ITERS = 2
 WIDE = 4
 VMEM_BYTES = 24 * 2**20
+FIRST_VMEM_BYTES = 62 * 2**20
 COL, ODD, OWN, FAR, ROW, SCALARS = 0, 1, 2, 10, 14, 24
 
 
@@ -72,15 +73,23 @@
     return column, same, near
 
 
-def beyond_kernel(scal, v_ref, x_ref, out_ref, *far_refs):
+def beyond_kernel(scal, v_ref, x_ref, out_ref, low_ref, high_ref, x_here, arrived):
     half = out_ref.shape[0]
-    each = far_refs[0].shape[0]
-    x = x_ref[...].astype(jnp.bfloat16)
+    each = half // 2
+    copies = [pltpu.make_async_copy(x_ref, x_here, arrived.at[half])]
+    for i in range(half):
+        there = (low_ref, high_ref)[i // each].at[i % each]
+        copies.append(pltpu.make_async_copy(v_ref.at[half * scal[ODD] + i], there, arrived.at[i]))
+    for copy in copies:
+        copy.start()
+    copies[0].wait()
+    x = x_here[...].astype(jnp.bfloat16)
     x_turn = turn_bf(x)
     for i in range(half):
-        s = half * scal[ODD] + i
-        out_ref[i] = (dot(v_ref[s, 0], x) + dot(v_ref[s, 1], x_turn)).astype(jnp.bfloat16)
-        far_refs[i // each][i % each] = v_ref[s]
+        copies[1 + i].wait()
+        tile = (low_ref, high_ref)[i // each]
+        piece = dot(tile[i % each, 0], x) + dot(tile[i % each, 1], x_turn)
+        out_ref[i] = piece.astype(jnp.bfloat16)
 
 
 def own_coefs(scal, v_ref, x, out_ref):
@@ -199,13 +208,11 @@
 def kernel_call(body, shape, scalars, *operands):
     smem = pl.BlockSpec(memory_space=pltpu.SMEM)
     vmem = pl.BlockSpec(memory_space=pltpu.VMEM)
-    several = isinstance(shape, list)
-    outs = [jax.ShapeDtypeStruct(s, jnp.bfloat16) for s in (shape if several else [shape])]
     return pl.pallas_call(
         body,
-        out_shape=outs if several else outs[0],
+        out_shape=jax.ShapeDtypeStruct(shape, jnp.bfloat16),
         in_specs=[smem] * len(scalars) + [vmem] * len(operands),
-        out_specs=[vmem] * len(outs) if several else vmem,
+        out_specs=vmem,
         compiler_params=pltpu.CompilerParams(vmem_limit_bytes=VMEM_BYTES),
     )(*scalars, *operands)
 
@@ -252,13 +259,22 @@
     v, u, observed = col_factors[0], row_factors[0], data[0]
 
     where = jnp.stack([col, odd])
-    relay, *fars = kernel_call(
+    vmem = pl.BlockSpec(memory_space=pltpu.VMEM)
+    hbm = pl.BlockSpec(memory_space=pltpu.HBM)
+    relay, *fars = pl.pallas_call(
         beyond_kernel,
-        [(half, levels, width)] + [(half // 2, 2, levels, rows)] * 2,
-        [where],
-        v,
-        model,
-    )
+        out_shape=[
+            jax.ShapeDtypeStruct(shape, jnp.bfloat16)
+            for shape in [(half, levels, width)] + [(half // 2, 2, levels, rows)] * 2
+        ],
+        in_specs=[pl.BlockSpec(memory_space=pltpu.SMEM), hbm, hbm],
+        out_specs=[vmem] * 3,
+        scratch_shapes=[
+            pltpu.VMEM((rows, width), jnp.float32),
+            pltpu.SemaphoreType.DMA((half + 1,)),
+        ],
+        compiler_params=pltpu.CompilerParams(vmem_limit_bytes=FIRST_VMEM_BYTES),
+    )(where, v, model)
     relay = lax.ppermute(relay, "tile", swaps)
     fars = [lax.ppermute(far, "tile", swaps) for far in fars]
 
@@ -277,6 +293,7 @@
     gate_re = jnp.concatenate([gate_re, gate_re], axis=-1)
     gate_im = jnp.concatenate([gate_im, gate_im], axis=-1)
 
+    relay, scal, gate_re, gate_im = lax.optimization_barrier((relay, scal, gate_re, gate_im))
     tiles = (slots, 2, levels, width)
     for step in range(ITERS):
         first = step == 0

time: 123 us -> 123 us (level)
  blocking collectives: 58.8 us -> 71 us
  waiting for transfers between devices: 15.8 us -> 9.48 us
  starting transfers between devices: 31 us -> 25.2 us
  local copies, waits for them, and re-layouts: 3.23 us -> 1.13 us
  Pallas kernels: 11.1 us -> 12.6 us
    all_to_all x2 -> x3, blocking collectives: 24.3 us -> 36.4 us  [among_pair(): lax.all_to_all(flat, ('freq', 'tile'), 0, 0, tiled=True, axis_index_group...]
    all_to_all x1 -> x0, waiting for transfers between devices: 6.12 us -> none  [among_pair(): lax.all_to_all(flat, ('freq', 'tile'), 0, 0, tiled=True, axis_index_group...]
    all_to_all x1 -> x0, starting transfers between devices: 5.96 us -> none  [among_pair(): lax.all_to_all(flat, ('freq', 'tile'), 0, 0, tiled=True, axis_index_group...]
    unnamed x16, local copies, waits for them, and re-layouts: 2.78 us -> 0.68 us
    pallas_call x9, Pallas kernels: 11.1 us -> 12.6 us  [the longest x8 9.55 us: kernel_call(): pl.pallas_call(body, out_shape=jax.ShapeDtypeStruct(shape, jnp.bfloat16),...]
  transfers between devices with their start and end apart: 6 -> 5, of which waited for: 4 -> 3; matrix products, arithmetic and copies ran while one was open for 1% -> 1% of each run, Pallas kernels for 0% -> 0%
where the time goes in v6:
time: 123 us; the launch traced here: 122 us
  blocking collectives  71 us (58%)
  starting transfers between devices  25.2 us (20%)
  Pallas kernels  12.6 us (10%)
  waiting for transfers between devices  9.48 us (8%)
  other arithmetic  1.94 us (2%)
    all_to_all x3, blocking collectives, among_pair(): lax.all_to_all(flat, ('freq', 'tile'), 0, 0, tiled=True, axis_index_group...  36.4 us
    all_to_all x2, blocking collectives, spread(): lax.all_to_all(pieces, 'tile', 0, 0, tiled=True, axis_index_groups=groups)  26.5 us
    all_to_all x2, starting transfers between devices, spread(): lax.all_to_all(pieces, 'tile', 0, 0, tiled=True, axis_index_groups=groups)  12.2 us
    pallas_call x8, Pallas kernels, kernel_call(): pl.pallas_call(body, out_shape=jax.ShapeDtypeStruct(shape, jnp.bfloat16),...  9.55 us
    ppermute x2, starting transfers between devices, on_device(): fars = [lax.ppermute(far, 'tile', swaps) for far in fars]  9.24 us
    all_to_all x1, blocking collectives, on_device(): model = lax.all_to_all(mixed[:, 0], 'freq', 0, 0, tiled=True)  8.04 us
    ppermute x2, waiting for transfers between devices, on_device(): fars = [lax.ppermute(far, 'tile', swaps) for far in fars]  7.99 us
    ppermute x1, starting transfers between devices, on_device(): relay = lax.ppermute(relay, 'tile', swaps)  3.82 us
  transfers between devices with their start and end apart: 5, of which 3 were waited for; matrix products, arithmetic and copies ran while one was open for 1% of the time, Pallas kernels for 0%

profile of v6, /device:TPU:32, one launch (start us, length us, event | category | flops | bytes accessed | tf_op | source)
XLA Modules:
  0.0 122.2 jit_solution(13156275983925927002)
XLA Ops:
  0.0 0.6 pad_add_fusion.scal
  0.6 3.0 %shard_map.73 = (bf16[4,112,128]{2,1,0:T(8,128)(2,1)}, bf16[2,2,112,256]{3,2,1,0:T(8,128)(2,1)}, bf16[2,2,112,256]{3,2,1,0:T(8,128)(2,1)}) custom-call(s32[2]{0:T(128)} %pad_add_fusion.scal, bf16[8,2,112,256]{3,2,1,0:T(8,128)(2,1)} %bitcast.26, f32[256,128]{1,0:T(8,128)} %bitcast.35), custom_call_target="tpu_custom_call" | custom-call | tf_op jit(solution)/shard_map/pallas_call | solution.py:264
  3.6 3.8 %collective-permute-start = (bf16[4,112,128]{2,1,0:T(8,128)(2,1)}, bf16[4,112,128]{2,1,0:T(8,128)(2,1)S(1)}, u32[]{:S(2)}, u32[]{:S(2)}) collective-permute-start(bf16[4,112,128]{2,1,0:T(8,128)(2,1)} %get-tuple-element.12), channel_id=1, source_target_pairs={{4,8},{5,9},{6,10},{7,11},{8,4},{9,5},{10,6},{11,7},{12,16},{13,17... | collective-permute-start | bytes 344072 | tf_op jit(solution)/shard_map/ppermute | solution.py:278
  7.6 0.6 copy-done.5
  9.3 1.5 %collective-permute-done.relay_ref = bf16[4,112,128]{2,1,0:T(8,128)(2,1)S(1)} collective-permute-done((bf16[4,112,128]{2,1,0:T(8,128)(2,1)}, bf16[4,112,128]{2,1,0:T(8,128)(2,1)S(1)}, u32[]{:S(2)}, u32[]{:S(2)}) %collective-permute-start) | collective-permute-done | bytes 114720 | tf_op jit(solution)/shard_map/ppermute | solution.py:278
  10.8 1.8 %shard_map.74 = bf16[8,2,112,128]{3,2,1,0:T(8,128)(2,1)} custom-call(s32[24]{0:T(128)S(1)} %pad.4.scal, bf16[8,2,112,256]{3,2,1,0:T(8,128)(2,1)S(1)} %bitcast.27, f32[256,128]{1,0:T(8,128)S(1)} %bitcast.36, bf16[4,112,128]{2,1,0:T(8,128)(2,1)S(1)} %collective-permute-done.relay_ref), custom_call_target="tpu_custom_call" | custom-call | tf_op jit(solution)/shard_map/pallas_call | solution.py:211
  12.6 6.1 %all-to-all-start = ((bf16[8,2,112,128]{3,2,1,0:T(8,128)(2,1)}), bf16[8,2,112,128]{3,2,1,0:T(8,128)(2,1)S(1)}, u32[]{:S(2)}, u32[]{:S(2)}) async-start(bf16[8,2,112,128]{3,2,1,0:T(8,128)(2,1)} %shard_map.74), calls=%async_computation | async-start | bytes 917504 | tf_op jit(solution)/shard_map/all_to_all | solution.py:247
  18.7 4.9 %collective-permute-start.1 = (bf16[2,2,112,256]{3,2,1,0:T(8,128)(2,1)S(1)}, bf16[2,2,112,256]{3,2,1,0:T(8,128)(2,1)S(1)}, u32[]{:S(2)}, u32[]{:S(2)}) collective-permute-start(bf16[2,2,112,256]{3,2,1,0:T(8,128)(2,1)S(1)} %copy-done.7), channel_id=1, source_target_pairs={{4,8},{5,9},{6,10},{7,11},{8,4},{9,5},{10,6},{11,7},{12,16},{13,17... | collective-permute-start | bytes 688136 | tf_op jit(solution)/shard_map/ppermute | solution.py:279
  23.6 4.7 %collective-permute-done.1.rest_0_.near_far_ref = bf16[2,2,112,256]{3,2,1,0:T(8,128)(2,1)S(1)} collective-permute-done((bf16[2,2,112,256]{3,2,1,0:T(8,128)(2,1)S(1)}, bf16[2,2,112,256]{3,2,1,0:T(8,128)(2,1)S(1)}, u32[]{:S(2)}, u32[]{:S(2)}) %collective-permute-start.1) | collective-permute-done | bytes 229408 | tf_op jit(solution)/shard_map/ppermute | solution.py:279
  28.3 2.3 %shard_map.75 = bf16[8,2,112,128]{3,2,1,0:T(8,128)(2,1)} custom-call(s32[24]{0:T(128)S(1)} %pad.4.scal, bf16[8,2,112,128]{3,2,1,0:T(8,128)(2,1)S(1)} %all-to-all-done.got_ref, bf16[8,2,112,256]{3,2,1,0:T(8,128)(2,1)S(1)} %bitcast.31, bf16[256,128]{1,0:T(8,128)(2,1)S(1)} %bitcast.43, bf16[2,2,112,256]{3,2,1,0:T(8,128)(2,1)S(1)} %collective-permute-done.1.rest_0_.near_far_ref), custom_call_target="tpu_custom_call" | custom-call | tf_op jit(solution)/shard_map/pallas_call | solution.py:211
  30.6 6.1 %all-to-all-start.1 = ((bf16[8,2,112,128]{3,2,1,0:T(8,128)(2,1)}), bf16[8,2,112,128]{3,2,1,0:T(8,128)(2,1)S(1)}, u32[]{:S(2)}, u32[]{:S(2)}) async-start(bf16[8,2,112,128]{3,2,1,0:T(8,128)(2,1)} %shard_map.75), calls=%async_computation.1 | async-start | bytes 917504 | tf_op jit(solution)/shard_map/all_to_all | solution.py:247
  36.7 4.3 %collective-permute-start.2 = (bf16[2,2,112,256]{3,2,1,0:T(8,128)(2,1)S(1)}, bf16[2,2,112,256]{3,2,1,0:T(8,128)(2,1)S(1)}, u32[]{:S(2)}, u32[]{:S(2)}) collective-permute-start(bf16[2,2,112,256]{3,2,1,0:T(8,128)(2,1)S(1)} %copy-done.6), channel_id=1, source_target_pairs={{4,8},{5,9},{6,10},{7,11},{8,4},{9,5},{10,6},{11,7},{12,16},{13,17... | collective-permute-start | bytes 688136 | tf_op jit(solution)/shard_map/ppermute | solution.py:279
  41.6 3.3 %collective-permute-done.2.last_far_ref = bf16[2,2,112,256]{3,2,1,0:T(8,128)(2,1)S(1)} collective-permute-done((bf16[2,2,112,256]{3,2,1,0:T(8,128)(2,1)S(1)}, bf16[2,2,112,256]{3,2,1,0:T(8,128)(2,1)S(1)}, u32[]{:S(2)}, u32[]{:S(2)}) %collective-permute-start.2) | collective-permute-done | bytes 229408 | tf_op jit(solution)/shard_map/ppermute | solution.py:279
  45.0 1.2 %shard_map.76 = bf16[8,2,32,128]{3,2,1,0:T(8,128)(2,1)S(1)} custom-call(s32[24]{0:T(128)S(1)} %pad.4.scal, f32[1]{0:T(128)S(6)} %copy.8.size_ref, bf16[8,2,112,128]{3,2,1,0:T(8,128)(2,1)S(1)} %all-to-all-done.1.got_ref, bf16[8,2,112,256]{3,2,1,0:T(8,128)(2,1)S(1)} %bitcast.28, bf16[2,2,112,256]{3,2,1,0:T(8,128)(2,1)S(1)} %collective-permute-done.1.rest_0_.near_far_ref, ...), custom_call_target="tpu_custom_call" | custom-call | tf_op jit(solution)/shard_map/pallas_call | solution.py:211
  46.2 12.3 %all_to_all.40 = bf16[16,32,128]{2,1,0:T(8,128)(2,1)S(1)} all-to-all(bf16[16,32,128]{2,1,0:T(8,128)(2,1)S(1)} %bitcast.42), channel_id=1, replica_groups={{60,0,124,64,188,128,252,192,316,256,380,320,444,384,508,448},{61,1,125..., dimensions={0} | all-to-all | bytes 262144 | tf_op jit(solution)/shard_map/all_to_all | solution.py:251
  58.7 9.2 %all_to_all.41 = bf16[16,32,128]{2,1,0:T(8,128)(2,1)S(1)} all-to-all(bf16[16,32,128]{2,1,0:T(8,128)(2,1)S(1)} %bitcast.40), channel_id=1, replica_groups={{60,0,124,64,188,128,252,192,316,256,380,320,444,384,508,448},{61,1,125..., dimensions={0} | all-to-all | bytes 262144 | tf_op jit(solution)/shard_map/all_to_all | solution.py:251
  67.9 1.1 shard_map.78
  69.1 14.9 %all_to_all.42.got_ref = bf16[8,2,112,128]{3,2,1,0:T(8,128)(2,1)S(1)} all-to-all(bf16[8,2,112,128]{3,2,1,0:T(8,128)(2,1)S(1)} %shard_map.78), channel_id=1, replica_groups={{0,1,2,3,4,5,6,7},{8,9,10,11,12,13,14,15},{16,17,18,19,20,21,22,23},{24..., dimensions={0} | all-to-all | bytes 917504 | tf_op jit(solution)/shard_map/all_to_all | solution.py:247
  84.0 1.5 %shard_map.79 = bf16[8,2,112,128]{3,2,1,0:T(8,128)(2,1)S(1)} custom-call(s32[24]{0:T(128)S(1)} %pad.4.scal, bf16[8,2,112,128]{3,2,1,0:T(8,128)(2,1)S(1)} %all_to_all.42.got_ref, bf16[8,2,112,256]{3,2,1,0:T(8,128)(2,1)S(1)} %bitcast.32, bf16[256,128]{1,0:T(8,128)(2,1)S(1)} %bitcast.44), custom_call_target="tpu_custom_call" | custom-call | tf_op jit(solution)/shard_map/pallas_call | solution.py:211
  85.5 11.7 %all_to_all.43.got_ref = bf16[8,2,112,128]{3,2,1,0:T(8,128)(2,1)S(1)} all-to-all(bf16[8,2,112,128]{3,2,1,0:T(8,128)(2,1)S(1)} %shard_map.79), channel_id=1, replica_groups={{0,1,2,3,4,5,6,7},{8,9,10,11,12,13,14,15},{16,17,18,19,20,21,22,23},{24..., dimensions={0} | all-to-all | bytes 917504 | tf_op jit(solution)/shard_map/all_to_all | solution.py:247
  97.1 1.2 %shard_map.80 = bf16[8,2,32,128]{3,2,1,0:T(8,128)(2,1)S(1)} custom-call(s32[24]{0:T(128)S(1)} %pad.4.scal, f32[1]{0:T(128)S(6)} %copy.8.size_ref, bf16[8,2,112,128]{3,2,1,0:T(8,128)(2,1)S(1)} %all_to_all.43.got_ref, bf16[8,2,112,256]{3,2,1,0:T(8,128)(2,1)S(1)} %bitcast.30, bf16[2,2,112,256]{3,2,1,0:T(8,128)(2,1)S(1)} %collective-permute-done.1.rest_0_.near_far_ref, ...), custom_call_target="tpu_custom_call" | custom-call | tf_op jit(solution)/shard_map/pallas_call | solution.py:211
  98.4 14.9 %all_to_all.44 = bf16[16,32,128]{2,1,0:T(8,128)(2,1)S(1)} all-to-all(bf16[16,32,128]{2,1,0:T(8,128)(2,1)S(1)} %bitcast.41), channel_id=1, replica_groups={{60,0,124,64,188,128,252,192,316,256,380,320,444,384,508,448},{61,1,125..., dimensions={0} | all-to-all | bytes 262144 | tf_op jit(solution)/shard_map/all_to_all | solution.py:251
  113.5 8.0 %all_to_all.45 = bf16[8,32,128]{2,1,0:T(8,128)(2,1)S(1)} all-to-all(bf16[8,32,128]{2,1,0:T(8,128)(2,1)S(1)} %bitcast.45), channel_id=1, replica_groups=mesh['freq'=8,'tile'=64] {'freq'}, dimensions={0} | all-to-all | bytes 131072 | tf_op jit(solution)/shard_map/all_to_all | solution.py:318
  121.5 0.7 bitcast_convert_fusion
  (32 shorter events, 1.6 us)
Async XLA Ops:
  0.0 10.8 %copy-start = (bf16[1,8,2,112,256]{4,3,2,1,0:T(8,128)(2,1)S(1)}, bf16[1,8,2,112,256]{4,3,2,1,0:T(8,128)(2,1)}, u32[]{:S(2)}) copy-start(bf16[1,8,2,112,256]{4,3,2,1,0:T(8,128)(2,1)} %param.9) | copy-start | bytes 2752516
  3.6 7.2 %collective-permute-start = (bf16[4,112,128]{2,1,0:T(8,128)(2,1)}, bf16[4,112,128]{2,1,0:T(8,128)(2,1)S(1)}, u32[]{:S(2)}, u32[]{:S(2)}) collective-permute-start(bf16[4,112,128]{2,1,0:T(8,128)(2,1)} %get-tuple-element.12), channel_id=1, source_target_pairs={{4,8},{5,9},{6,10},{7,11},{8,4},{9,5},{10,6},{11,7},{12,16},{13,17... | collective-permute-start | bytes 344072 | tf_op jit(solution)/shard_map/ppermute | solution.py:278
  7.5 0.7 copy-start.5
  7.6 0.7 copy-start.4
  8.2 2.7 %copy-start.2 = (f32[1,256,128]{2,1,0:T(8,128)S(1)}, f32[1,256,128]{2,1,0:T(8,128)}, u32[]{:S(2)}) copy-start(f32[1,256,128]{2,1,0:T(8,128)} %param.7) | copy-start | bytes 393220
  10.8 17.4 %copy-start.1 = (bf16[1,8,2,112,256]{4,3,2,1,0:T(8,128)(2,1)S(1)}, bf16[1,8,2,112,256]{4,3,2,1,0:T(8,128)(2,1)}, u32[]{:S(2)}) copy-start(bf16[1,8,2,112,256]{4,3,2,1,0:T(8,128)(2,1)} %param.10) | copy-start | bytes 2752516
  12.6 6.1 %copy-start.7 = (bf16[2,2,112,256]{3,2,1,0:T(8,128)(2,1)S(1)}, bf16[2,2,112,256]{3,2,1,0:T(8,128)(2,1)}, u32[]{:S(2)}) copy-start(bf16[2,2,112,256]{3,2,1,0:T(8,128)(2,1)} %get-tuple-element.16) | copy-start | bytes 688132
  12.6 15.7 %copy-start.3 = (bf16[1,256,128]{2,1,0:T(8,128)(2,1)S(1)}, bf16[1,256,128]{2,1,0:T(8,128)(2,1)}, u32[]{:S(2)}) copy-start(bf16[1,256,128]{2,1,0:T(8,128)(2,1)} %param.8) | copy-start | bytes 196612
  12.6 15.7 %all-to-all-start = ((bf16[8,2,112,128]{3,2,1,0:T(8,128)(2,1)}), bf16[8,2,112,128]{3,2,1,0:T(8,128)(2,1)S(1)}, u32[]{:S(2)}, u32[]{:S(2)}) async-start(bf16[8,2,112,128]{3,2,1,0:T(8,128)(2,1)} %shard_map.74), calls=%async_computation | async-start | bytes 917504 | tf_op jit(solution)/shard_map/all_to_all | solution.py:247
  18.7 9.6 %collective-permute-start.1 = (bf16[2,2,112,256]{3,2,1,0:T(8,128)(2,1)S(1)}, bf16[2,2,112,256]{3,2,1,0:T(8,128)(2,1)S(1)}, u32[]{:S(2)}, u32[]{:S(2)}) collective-permute-start(bf16[2,2,112,256]{3,2,1,0:T(8,128)(2,1)S(1)} %copy-done.7), channel_id=1, source_target_pairs={{4,8},{5,9},{6,10},{7,11},{8,4},{9,5},{10,6},{11,7},{12,16},{13,17... | collective-permute-start | bytes 688136 | tf_op jit(solution)/shard_map/ppermute | solution.py:279
  30.6 6.1 %copy-start.6 = (bf16[2,2,112,256]{3,2,1,0:T(8,128)(2,1)S(1)}, bf16[2,2,112,256]{3,2,1,0:T(8,128)(2,1)}, u32[]{:S(2)}) copy-start(bf16[2,2,112,256]{3,2,1,0:T(8,128)(2,1)} %get-tuple-element.17) | copy-start | bytes 688132
  30.6 14.4 %all-to-all-start.1 = ((bf16[8,2,112,128]{3,2,1,0:T(8,128)(2,1)}), bf16[8,2,112,128]{3,2,1,0:T(8,128)(2,1)S(1)}, u32[]{:S(2)}, u32[]{:S(2)}) async-start(bf16[8,2,112,128]{3,2,1,0:T(8,128)(2,1)} %shard_map.75), calls=%async_computation.1 | async-start | bytes 917504 | tf_op jit(solution)/shard_map/all_to_all | solution.py:247
  36.7 8.3 %collective-permute-start.2 = (bf16[2,2,112,256]{3,2,1,0:T(8,128)(2,1)S(1)}, bf16[2,2,112,256]{3,2,1,0:T(8,128)(2,1)S(1)}, u32[]{:S(2)}, u32[]{:S(2)}) collective-permute-start(bf16[2,2,112,256]{3,2,1,0:T(8,128)(2,1)S(1)} %copy-done.6), channel_id=1, source_target_pairs={{4,8},{5,9},{6,10},{7,11},{8,4},{9,5},{10,6},{11,7},{12,16},{13,17... | collective-permute-start | bytes 688136 | tf_op jit(solution)/shard_map/ppermute | solution.py:279

commit v7 on v6

--- a/solution.py
+++ b/solution.py
@@ -13,7 +13,7 @@
 WIDE = 4
 VMEM_BYTES = 24 * 2**20
 FIRST_VMEM_BYTES = 62 * 2**20
-COL, ODD, OWN, FAR, ROW, SCALARS = 0, 1, 2, 10, 14, 24
+COL, ODD, SEAT, INNER, OWN, FAR, ROW, SCALARS = 0, 1, 2, 3, 4, 12, 16, 24
 
 
 def gate_matrix(window, count):
@@ -73,13 +73,13 @@
     return column, same, near
 
 
-def beyond_kernel(scal, v_ref, x_ref, out_ref, low_ref, high_ref, x_here, arrived):
+def beyond_kernel(v_ref, x_ref, out_ref, v_here, x_here, arrived):
     half = out_ref.shape[0]
-    each = half // 2
+    odd = 1 - (lax.axis_index("tile") // WIDE) % 2
     copies = [pltpu.make_async_copy(x_ref, x_here, arrived.at[half])]
     for i in range(half):
-        there = (low_ref, high_ref)[i // each].at[i % each]
-        copies.append(pltpu.make_async_copy(v_ref.at[half * scal[ODD] + i], there, arrived.at[i]))
+        tile = v_ref.at[half * odd + i]
+        copies.append(pltpu.make_async_copy(tile, v_here.at[i], arrived.at[i]))
     for copy in copies:
         copy.start()
     copies[0].wait()
@@ -87,19 +87,18 @@
     x_turn = turn_bf(x)
     for i in range(half):
         copies[1 + i].wait()
-        tile = (low_ref, high_ref)[i // each]
-        piece = dot(tile[i % each, 0], x) + dot(tile[i % each, 1], x_turn)
+        piece = dot(v_here[i, 0], x) + dot(v_here[i, 1], x_turn)
         out_ref[i] = piece.astype(jnp.bfloat16)
 
 
 def own_coefs(scal, v_ref, x, out_ref):
     slots = v_ref.shape[0]
     half = slots // 2
-    col, odd = scal[COL], scal[ODD]
+    col, odd, seat = scal[COL], scal[ODD], scal[SEAT]
     x_turn = turn_bf(x)
     for s in range(slots):
         column, same, _ = outward(col, s, odd)
-        place = column + half * jnp.where(same, odd, 1 - odd)
+        place = column + half * jnp.where(same, seat, 1 - seat)
         out_ref[place, 0] = keep(dot(v_ref[s, 0], x) + dot(v_ref[s, 1], x_turn), scal[OWN + s])
 
 
@@ -132,7 +131,7 @@
     out_ref = rest[-1]
     slots = u_ref.shape[0]
     half = slots // 2
-    col, odd = scal[COL], scal[ODD]
+    col, odd, seat = scal[COL], scal[ODD], scal[SEAT]
     real = jnp.zeros(data_ref.shape, jnp.float32)
     imag = jnp.zeros(data_ref.shape, jnp.float32)
     for s in range(slots):
@@ -140,7 +139,7 @@
         way = (col + slots - s) >> 2
         near = jnp.where(odd == 1, way == 0, way == 2)
         relay = jnp.logical_not(jnp.logical_or(near, way == 1)).astype(jnp.int32)
-        piece = got_ref[column + half * jnp.where(near, 1 - odd, odd), relay]
+        piece = got_ref[column + half * jnp.where(near, 1 - seat, seat), relay]
         real += left_dot(u_ref[s, 0], piece)
         imag += left_dot(u_ref[s, 1], piece)
     image = real + turn(imag)
@@ -150,7 +149,7 @@
         column = (col + slots - s) & 3
         same = ((col + slots - s) >> 2) == 1
         piece = keep(dot(u_ref[s, 0], resid) - dot(u_ref[s, 1], resid_turn), scal[ROW + s])
-        place = column + half * jnp.where(same, odd, 1 - odd)
+        place = column + half * jnp.where(same, seat, 1 - seat)
         out_ref[place, 0] = piece
         out_ref[(place + half) & (slots - 1), 1] = piece
 
@@ -161,14 +160,15 @@
     far_refs = (near_far_ref, last_far_ref)
     slots, _, levels, _ = v_ref.shape
     half = slots // 2
-    col, odd = scal[COL], scal[ODD]
+    col, odd, seat = scal[COL], scal[ODD], scal[SEAT]
     parts, _, part, width = out_ref.shape
     shape = (parts * part, width)
     real = jnp.zeros(shape, jnp.float32)
     imag = jnp.zeros(shape, jnp.float32)
     for s in range(slots):
         column, same, near = outward(col, s, odd)
-        piece = got_ref[column + half * jnp.where(same, odd, 1 - odd), 0]
+        piece = got_ref[column + half * jnp.where(same, seat, 1 - seat), 0]
+        near = jnp.logical_and(near, scal[INNER] == 1)
         piece = keep(piece, jnp.where(jnp.logical_or(same, near), levels, 0))
         real += left_dot(v_ref[s, 0], piece)
         imag += left_dot(v_ref[s, 1], piece)
@@ -177,7 +177,7 @@
     for i in range(half):
         column = (col + i) & 3
         valid = (col + i < half).astype(jnp.int32) == odd
-        piece = keep(got_ref[column + half * odd, 1], jnp.where(valid, levels, 0))
+        piece = keep(got_ref[column + half * seat, 1], jnp.where(valid, levels, 0))
         far_real += left_dot(far_factor(far_refs, i, 0), piece)
         far_imag += left_dot(far_factor(far_refs, i, 1), piece)
     x = x_ref[...] if first else side_of(x_ref, 1 - odd).astype(jnp.float32)
@@ -226,25 +226,38 @@
     half = slots // 2
     rows_z = ntile // WIDE
     col = myself % WIDE
-    odd = (myself // WIDE) % 2
-    groups = [[slots * k + i for i in range(slots)] for k in range(ntile // slots)]
+    odd = 1 - (myself // WIDE) % 2
+    inner = [
+        [f * ntile + slots * k - WIDE + i for i in range(slots)]
+        for f in range(nfreq)
+        for k in range(1, rows_z // 2)
+    ]
+    outer = [
+        [(f + j) * ntile + z * WIDE + y for j in range(2) for y in range(WIDE)]
+        for f in range(0, nfreq, 2)
+        for z in (0, rows_z - 1)
+    ]
+    edge = jnp.logical_or(myself < WIDE, myself >= ntile - WIDE)
+    seat = jnp.where(edge, lax.axis_index("freq") % 2, odd)
     swaps = [
-        (z * WIDE + y, (z + 1 if z % 2 else z - 1) * WIDE + y)
-        for z in range(1, rows_z - 1)
+        (z * WIDE + y, (z - 1 if z % 2 else z + 1) * WIDE + y)
+        for z in range(rows_z)
         for y in range(WIDE)
     ]
     pairs = [
         [
-            f * ntile + (z % rows_z) * WIDE + y
+            f * ntile + z * WIDE + y
             for f in range(nfreq)
-            for z in (2 * k - 1, 2 * k)
+            for z in (2 * k, 2 * k + 1)
         ]
         for k in range(rows_z // 2)
         for y in range(WIDE)
     ]
 
     def spread(pieces):
-        return lax.all_to_all(pieces, "tile", 0, 0, tiled=True, axis_index_groups=groups)
+        return lax.all_to_all(
+            pieces, ("freq", "tile"), 0, 0, tiled=True, axis_index_groups=inner + outer
+        )
 
     def among_pair(pieces):
         flat = pieces.reshape(2 * nfreq, -1, pieces.shape[-1])
@@ -258,32 +271,35 @@
     part = rows // nfreq
     v, u, observed = col_factors[0], row_factors[0], data[0]
 
-    where = jnp.stack([col, odd])
-    vmem = pl.BlockSpec(memory_space=pltpu.VMEM)
+    where = jnp.stack([col, odd, seat, 1 - edge.astype(jnp.int32)])
     hbm = pl.BlockSpec(memory_space=pltpu.HBM)
-    relay, *fars = pl.pallas_call(
+    relay = pl.pallas_call(
         beyond_kernel,
-        out_shape=[
-            jax.ShapeDtypeStruct(shape, jnp.bfloat16)
-            for shape in [(half, levels, width)] + [(half // 2, 2, levels, rows)] * 2
-        ],
-        in_specs=[pl.BlockSpec(memory_space=pltpu.SMEM), hbm, hbm],
-        out_specs=[vmem] * 3,
+        out_shape=jax.ShapeDtypeStruct((half, levels, width), jnp.bfloat16),
+        in_specs=[hbm, hbm],
+        out_specs=pl.BlockSpec(memory_space=pltpu.VMEM),
         scratch_shapes=[
+            pltpu.VMEM((half, 2, levels, rows), jnp.bfloat16),
             pltpu.VMEM((rows, width), jnp.float32),
             pltpu.SemaphoreType.DMA((half + 1,)),
         ],
         compiler_params=pltpu.CompilerParams(vmem_limit_bytes=FIRST_VMEM_BYTES),
-    )(where, v, model)
+    )(v, model)
     relay = lax.ppermute(relay, "tile", swaps)
-    fars = [lax.ppermute(far, "tile", swaps) for far in fars]
+    fars = [
+        lax.dynamic_slice_in_dim(v, half * odd + i, half // 2, 0) for i in (0, half // 2)
+    ]
 
     table = ranks[0]
     slot_ids = jnp.arange(slots, dtype=jnp.int32)
     opposite = jnp.clip(myself + jnp.where(odd == 1, WIDE, -WIDE), 0, ntile - 1)
     far_ranks = lax.dynamic_slice(table, (opposite, half * (1 - odd)), (1, half))[0]
     own_ranks = lax.dynamic_index_in_dim(table, myself, 0, keepdims=False)
-    anchors = jnp.clip(myself + half - slot_ids, 0, ntile - 1)
+    receivers = myself + slot_ids - half
+    outside = (col + slot_ids) // WIDE == 2 * odd
+    exists = (receivers >= 0) & (receivers < ntile)
+    own_ranks = jnp.where(exists & jnp.logical_not(outside), own_ranks, 0)
+    anchors = myself + half - slot_ids
     holder = jnp.arange(ntile, dtype=jnp.int32)[:, None] == anchors[None, :]
     row_ranks = jnp.sum(jnp.where(holder, table, 0), axis=0)
     scal = jnp.concatenate([where, own_ranks, far_ranks, row_ranks])
@@ -293,7 +309,10 @@
     gate_re = jnp.concatenate([gate_re, gate_re], axis=-1)
     gate_im = jnp.concatenate([gate_im, gate_im], axis=-1)
 
-    relay, scal, gate_re, gate_im = lax.optimization_barrier((relay, scal, gate_re, gate_im))
+    relay, fars, scal, gate_re, gate_im = lax.optimization_barrier(
+        (relay, fars, scal, gate_re, gate_im)
+    )
+    fars = [lax.ppermute(far, "tile", swaps) for far in fars]
     tiles = (slots, 2, levels, width)
     for step in range(ITERS):
         first = step == 0

time: 123 us -> 120 us (0.976)
  the two profiles are of different devices: /device:TPU:32 before, /device:TPU:64 now
where the time goes in v7:
time: 120 us; the launch traced here: 119 us
  blocking collectives  69.4 us (58%)
  starting transfers between devices  25.1 us (21%)
  Pallas kernels  12 us (10%)
  waiting for transfers between devices  8.83 us (7%)
  local copies, waits for them, and re-layouts  1.65 us (1%)
  other arithmetic  1.36 us (1%)
    all_to_all x3, blocking collectives, among_pair(): lax.all_to_all(flat, ('freq', 'tile'), 0, 0, tiled=True, axis_index_group...  37.2 us
    all_to_all x2, blocking collectives, spread(): lax.all_to_all(pieces, ('freq', 'tile'), 0, 0, tiled=True, axis_index_gro...  24.2 us
    all_to_all x2, starting transfers between devices, spread(): lax.all_to_all(pieces, ('freq', 'tile'), 0, 0, tiled=True, axis_index_gro...  12.8 us
    pallas_call x8, Pallas kernels, kernel_call(): pl.pallas_call(body, out_shape=jax.ShapeDtypeStruct(shape, jnp.bfloat16),...  9.56 us
    ppermute x2, starting transfers between devices, on_device(): fars = [lax.ppermute(far, 'tile', swaps) for far in fars]  8.43 us
    all_to_all x1, blocking collectives, on_device(): model = lax.all_to_all(mixed[:, 0], 'freq', 0, 0, tiled=True)  8.04 us
    ppermute x2, waiting for transfers between devices, on_device(): fars = [lax.ppermute(far, 'tile', swaps) for far in fars]  8.01 us
    ppermute x1, starting transfers between devices, on_device(): relay = lax.ppermute(relay, 'tile', swaps)  3.82 us
  transfers between devices with their start and end apart: 5, of which 3 were waited for; matrix products, arithmetic and copies ran while one was open for 1% of the time, Pallas kernels for 0%

profile of v7, /device:TPU:64, one launch (start us, length us, event | category | flops | bytes accessed | tf_op | source)
XLA Modules:
  0.0 119.3 jit_solution(5956931523342407631)
XLA Ops:
  0.0 2.4 %shard_map.73 = bf16[4,112,128]{2,1,0:T(8,128)(2,1)} custom-call(bf16[8,2,112,256]{3,2,1,0:T(8,128)(2,1)} %bitcast.32, f32[256,128]{1,0:T(8,128)} %bitcast.39), custom_call_target="tpu_custom_call" | custom-call | tf_op jit(solution)/shard_map/pallas_call | solution.py:276
  2.5 3.8 %collective-permute-start = (bf16[4,112,128]{2,1,0:T(8,128)(2,1)}, bf16[4,112,128]{2,1,0:T(8,128)(2,1)S(1)}, u32[]{:S(2)}, u32[]{:S(2)}) collective-permute-start(bf16[4,112,128]{2,1,0:T(8,128)(2,1)} %shard_map.73), channel_id=1, source_target_pairs={{0,4},{1,5},{2,6},{3,7},{4,0},{5,1},{6,2},{7,3},{8,12},{9,13},{10,... | collective-permute-start | bytes 344072 | tf_op jit(solution)/shard_map/ppermute | solution.py:288
  6.5 0.7 copy-done.4
  7.5 0.5 copy-done.5
  8.8 0.8 collective-permute-done.relay_ref
  9.6 1.8 %shard_map.74 = bf16[8,2,112,128]{3,2,1,0:T(8,128)(2,1)} custom-call(s32[24]{0:T(128)S(1)} %concatenate.9.scal, bf16[8,2,112,256]{3,2,1,0:T(8,128)(2,1)S(1)} %bitcast.33, f32[256,128]{1,0:T(8,128)S(1)} %bitcast.40, bf16[4,112,128]{2,1,0:T(8,128)(2,1)S(1)} %collective-permute-done.relay_ref), custom_call_target="tpu_custom_call" | custom-call | tf_op jit(solution)/shard_map/pallas_call | solution.py:211
  11.4 6.8 %all-to-all-start = ((bf16[8,2,112,128]{3,2,1,0:T(8,128)(2,1)}), bf16[8,2,112,128]{3,2,1,0:T(8,128)(2,1)S(1)}, u32[]{:S(2)}, u32[]{:S(2)}) async-start(bf16[8,2,112,128]{3,2,1,0:T(8,128)(2,1)} %shard_map.74), calls=%async_computation | async-start | bytes 917504 | tf_op jit(solution)/shard_map/all_to_all | solution.py:258
  18.2 4.2 %collective-permute-start.1 = (bf16[2,2,112,256]{3,2,1,0:T(8,128)(2,1)S(1)}, bf16[2,2,112,256]{3,2,1,0:T(8,128)(2,1)S(1)}, u32[]{:S(2)}, u32[]{:S(2)}) collective-permute-start(bf16[2,2,112,256]{3,2,1,0:T(8,128)(2,1)S(1)} %get-tuple-element.14), channel_id=1, source_target_pairs={{0,4},{1,5},{2,6},{3,7},{4,0},{5,1},{6,2},{7,3},{8,12},{9,13},{10,... | collective-permute-start | bytes 688136 | tf_op jit(solution)/shard_map/ppermute | solution.py:315
  22.4 4.6 %collective-permute-done.1.rest_0_.near_far_ref = bf16[2,2,112,256]{3,2,1,0:T(8,128)(2,1)S(1)} collective-permute-done((bf16[2,2,112,256]{3,2,1,0:T(8,128)(2,1)S(1)}, bf16[2,2,112,256]{3,2,1,0:T(8,128)(2,1)S(1)}, u32[]{:S(2)}, u32[]{:S(2)}) %collective-permute-start.1) | collective-permute-done | bytes 229408 | tf_op jit(solution)/shard_map/ppermute | solution.py:315
  27.0 2.3 %shard_map.75 = bf16[8,2,112,128]{3,2,1,0:T(8,128)(2,1)} custom-call(s32[24]{0:T(128)S(1)} %concatenate.9.scal, bf16[8,2,112,128]{3,2,1,0:T(8,128)(2,1)S(1)} %all-to-all-done.got_ref, bf16[8,2,112,256]{3,2,1,0:T(8,128)(2,1)S(1)} %bitcast.37, bf16[256,128]{1,0:T(8,128)(2,1)S(1)} %bitcast.49, ...), custom_call_target="tpu_custom_call" | custom-call | tf_op jit(solution)/shard_map/pallas_call | solution.py:211
  29.3 6.0 %all-to-all-start.1 = ((bf16[8,2,112,128]{3,2,1,0:T(8,128)(2,1)}), bf16[8,2,112,128]{3,2,1,0:T(8,128)(2,1)S(1)}, u32[]{:S(2)}, u32[]{:S(2)}) async-start(bf16[8,2,112,128]{3,2,1,0:T(8,128)(2,1)} %shard_map.75), calls=%async_computation.1 | async-start | bytes 917504 | tf_op jit(solution)/shard_map/all_to_all | solution.py:258
  35.3 4.3 %collective-permute-start.2 = (bf16[2,2,112,256]{3,2,1,0:T(8,128)(2,1)S(1)}, bf16[2,2,112,256]{3,2,1,0:T(8,128)(2,1)S(1)}, u32[]{:S(2)}, u32[]{:S(2)}) collective-permute-start(bf16[2,2,112,256]{3,2,1,0:T(8,128)(2,1)S(1)} %get-tuple-element.15), channel_id=1, source_target_pairs={{0,4},{1,5},{2,6},{3,7},{4,0},{5,1},{6,2},{7,3},{8,12},{9,13},{10,... | collective-permute-start | bytes 688136 | tf_op jit(solution)/shard_map/ppermute | solution.py:315
  40.3 3.4 %collective-permute-done.2.last_far_ref = bf16[2,2,112,256]{3,2,1,0:T(8,128)(2,1)S(1)} collective-permute-done((bf16[2,2,112,256]{3,2,1,0:T(8,128)(2,1)S(1)}, bf16[2,2,112,256]{3,2,1,0:T(8,128)(2,1)S(1)}, u32[]{:S(2)}, u32[]{:S(2)}) %collective-permute-start.2) | collective-permute-done | bytes 229408 | tf_op jit(solution)/shard_map/ppermute | solution.py:315
  43.6 1.2 %shard_map.76 = bf16[8,2,32,128]{3,2,1,0:T(8,128)(2,1)S(1)} custom-call(s32[24]{0:T(128)S(1)} %concatenate.9.scal, f32[1]{0:T(128)S(6)} %copy.8.size_ref, bf16[8,2,112,128]{3,2,1,0:T(8,128)(2,1)S(1)} %all-to-all-done.1.got_ref, bf16[8,2,112,256]{3,2,1,0:T(8,128)(2,1)S(1)} %bitcast.34, ...), custom_call_target="tpu_custom_call" | custom-call | tf_op jit(solution)/shard_map/pallas_call | solution.py:211
  44.9 13.5 %all_to_all.40 = bf16[16,32,128]{2,1,0:T(8,128)(2,1)S(1)} all-to-all(bf16[16,32,128]{2,1,0:T(8,128)(2,1)S(1)} %bitcast.48), channel_id=1, replica_groups={{0,4,64,68,128,132,192,196,256,260,320,324,384,388,448,452},{1,5,65,69,..., dimensions={0} | all-to-all | bytes 262144 | tf_op jit(solution)/shard_map/all_to_all | solution.py:264
  58.6 9.2 %all_to_all.41 = bf16[16,32,128]{2,1,0:T(8,128)(2,1)S(1)} all-to-all(bf16[16,32,128]{2,1,0:T(8,128)(2,1)S(1)} %bitcast.46), channel_id=1, replica_groups={{0,4,64,68,128,132,192,196,256,260,320,324,384,388,448,452},{1,5,65,69,..., dimensions={0} | all-to-all | bytes 262144 | tf_op jit(solution)/shard_map/all_to_all | solution.py:264
  67.8 1.1 shard_map.78
  68.9 13.0 %all_to_all.42.got_ref = bf16[8,2,112,128]{3,2,1,0:T(8,128)(2,1)S(1)} all-to-all(bf16[8,2,112,128]{3,2,1,0:T(8,128)(2,1)S(1)} %shard_map.78), channel_id=1, replica_groups={{4,5,6,7,8,9,10,11},{12,13,14,15,16,17,18,19},{20,21,22,23,24,25,26,27}..., dimensions={0} | all-to-all | bytes 917504 | tf_op jit(solution)/shard_map/all_to_all | solution.py:258
  81.9 1.5 %shard_map.79 = bf16[8,2,112,128]{3,2,1,0:T(8,128)(2,1)S(1)} custom-call(s32[24]{0:T(128)S(1)} %concatenate.9.scal, bf16[8,2,112,128]{3,2,1,0:T(8,128)(2,1)S(1)} %all_to_all.42.got_ref, bf16[8,2,112,256]{3,2,1,0:T(8,128)(2,1)S(1)} %bitcast.38, bf16[256,128]{1,0:T(8,128)(2,1)S(1)} %bitcast.50), custom_call_target="tpu_custom_call" | custom-call | tf_op jit(solution)/shard_map/pallas_call | solution.py:211
  83.4 11.2 %all_to_all.43.got_ref = bf16[8,2,112,128]{3,2,1,0:T(8,128)(2,1)S(1)} all-to-all(bf16[8,2,112,128]{3,2,1,0:T(8,128)(2,1)S(1)} %shard_map.79), channel_id=1, replica_groups={{4,5,6,7,8,9,10,11},{12,13,14,15,16,17,18,19},{20,21,22,23,24,25,26,27}..., dimensions={0} | all-to-all | bytes 917504 | tf_op jit(solution)/shard_map/all_to_all | solution.py:258
  94.7 1.2 %shard_map.80 = bf16[8,2,32,128]{3,2,1,0:T(8,128)(2,1)S(1)} custom-call(s32[24]{0:T(128)S(1)} %concatenate.9.scal, f32[1]{0:T(128)S(6)} %copy.8.size_ref, bf16[8,2,112,128]{3,2,1,0:T(8,128)(2,1)S(1)} %all_to_all.43.got_ref, bf16[8,2,112,256]{3,2,1,0:T(8,128)(2,1)S(1)} %bitcast.36, bf16[2,2,112,256]{3,2,1,0:T(8,128)(2,1)S(1)} %collective-permute-done.1.rest_0_.near_far_ref, ...), custom_call_target="tpu_custom_call" | custom-call | tf_op jit(solution)/shard_map/pallas_call | solution.py:211
  95.9 14.4 %all_to_all.44 = bf16[16,32,128]{2,1,0:T(8,128)(2,1)S(1)} all-to-all(bf16[16,32,128]{2,1,0:T(8,128)(2,1)S(1)} %bitcast.47), channel_id=1, replica_groups={{0,4,64,68,128,132,192,196,256,260,320,324,384,388,448,452},{1,5,65,69,..., dimensions={0} | all-to-all | bytes 262144 | tf_op jit(solution)/shard_map/all_to_all | solution.py:264
  110.5 8.0 %all_to_all.45 = bf16[8,32,128]{2,1,0:T(8,128)(2,1)S(1)} all-to-all(bf16[8,32,128]{2,1,0:T(8,128)(2,1)S(1)} %bitcast.51), channel_id=1, replica_groups=mesh['freq'=8,'tile'=64] {'freq'}, dimensions={0} | all-to-all | bytes 131072 | tf_op jit(solution)/shard_map/all_to_all | solution.py:337
  118.6 0.7 bitcast_convert_fusion
  (28 shorter events, 1.6 us)
Async XLA Ops:
  0.0 8.0 %copy-start = (bf16[1,8,2,112,256]{4,3,2,1,0:T(8,128)(2,1)S(1)}, bf16[1,8,2,112,256]{4,3,2,1,0:T(8,128)(2,1)}, u32[]{:S(2)}) copy-start(bf16[1,8,2,112,256]{4,3,2,1,0:T(8,128)(2,1)} %param.9) | copy-start | bytes 2752516
  2.5 7.2 %collective-permute-start = (bf16[4,112,128]{2,1,0:T(8,128)(2,1)}, bf16[4,112,128]{2,1,0:T(8,128)(2,1)S(1)}, u32[]{:S(2)}, u32[]{:S(2)}) collective-permute-start(bf16[4,112,128]{2,1,0:T(8,128)(2,1)} %shard_map.73), channel_id=1, source_target_pairs={{0,4},{1,5},{2,6},{3,7},{4,0},{5,1},{6,2},{7,3},{8,12},{9,13},{10,... | collective-permute-start | bytes 344072 | tf_op jit(solution)/shard_map/ppermute | solution.py:288
  6.4 0.7 copy-start.4
  7.3 0.7 copy-start.5
  8.1 1.6 %copy-start.2 = (f32[1,256,128]{2,1,0:T(8,128)S(1)}, f32[1,256,128]{2,1,0:T(8,128)}, u32[]{:S(2)}) copy-start(f32[1,256,128]{2,1,0:T(8,128)} %param.7) | copy-start | bytes 393220
  9.6 17.4 %copy-start.1 = (bf16[1,8,2,112,256]{4,3,2,1,0:T(8,128)(2,1)S(1)}, bf16[1,8,2,112,256]{4,3,2,1,0:T(8,128)(2,1)}, u32[]{:S(2)}) copy-start(bf16[1,8,2,112,256]{4,3,2,1,0:T(8,128)(2,1)} %param.10) | copy-start | bytes 2752516
  11.4 15.6 %copy-start.3 = (bf16[1,256,128]{2,1,0:T(8,128)(2,1)S(1)}, bf16[1,256,128]{2,1,0:T(8,128)(2,1)}, u32[]{:S(2)}) copy-start(bf16[1,256,128]{2,1,0:T(8,128)(2,1)} %param.8) | copy-start | bytes 196612
  11.4 15.6 %all-to-all-start = ((bf16[8,2,112,128]{3,2,1,0:T(8,128)(2,1)}), bf16[8,2,112,128]{3,2,1,0:T(8,128)(2,1)S(1)}, u32[]{:S(2)}, u32[]{:S(2)}) async-start(bf16[8,2,112,128]{3,2,1,0:T(8,128)(2,1)} %shard_map.74), calls=%async_computation | async-start | bytes 917504 | tf_op jit(solution)/shard_map/all_to_all | solution.py:258
  18.2 8.8 %collective-permute-start.1 = (bf16[2,2,112,256]{3,2,1,0:T(8,128)(2,1)S(1)}, bf16[2,2,112,256]{3,2,1,0:T(8,128)(2,1)S(1)}, u32[]{:S(2)}, u32[]{:S(2)}) collective-permute-start(bf16[2,2,112,256]{3,2,1,0:T(8,128)(2,1)S(1)} %get-tuple-element.14), channel_id=1, source_target_pairs={{0,4},{1,5},{2,6},{3,7},{4,0},{5,1},{6,2},{7,3},{8,12},{9,13},{10,... | collective-permute-start | bytes 688136 | tf_op jit(solution)/shard_map/ppermute | solution.py:315
  29.3 14.3 %all-to-all-start.1 = ((bf16[8,2,112,128]{3,2,1,0:T(8,128)(2,1)}), bf16[8,2,112,128]{3,2,1,0:T(8,128)(2,1)S(1)}, u32[]{:S(2)}, u32[]{:S(2)}) async-start(bf16[8,2,112,128]{3,2,1,0:T(8,128)(2,1)} %shard_map.75), calls=%async_computation.1 | async-start | bytes 917504 | tf_op jit(solution)/shard_map/all_to_all | solution.py:258
  35.3 8.3 %collective-permute-start.2 = (bf16[2,2,112,256]{3,2,1,0:T(8,128)(2,1)S(1)}, bf16[2,2,112,256]{3,2,1,0:T(8,128)(2,1)S(1)}, u32[]{:S(2)}, u32[]{:S(2)}) collective-permute-start(bf16[2,2,112,256]{3,2,1,0:T(8,128)(2,1)S(1)} %get-tuple-element.15), channel_id=1, source_target_pairs={{0,4},{1,5},{2,6},{3,7},{4,0},{5,1},{6,2},{7,3},{8,12},{9,13},{10,... | collective-permute-start | bytes 688136 | tf_op jit(solution)/shard_map/ppermute | solution.py:315

commit v8 on v7

--- a/solution.py
+++ b/solution.py
@@ -12,7 +12,7 @@
 ITERS = 2
 WIDE = 4
 VMEM_BYTES = 24 * 2**20
-FIRST_VMEM_BYTES = 62 * 2**20
+FIRST_VMEM_BYTES = 215 * 2**18
 COL, ODD, SEAT, INNER, OWN, FAR, ROW, SCALARS = 0, 1, 2, 3, 4, 12, 16, 24
 
 
@@ -51,6 +51,10 @@
     return lax.dot_general(a, b, (((0,), (0,)), ((), ())), preferred_element_type=jnp.float32)
 
 
+def stacked(ref, which):
+    return jnp.concatenate([ref[s, which] for s in range(ref.shape[0])], axis=0)
+
+
 def keep(value, rank):
     row = lax.broadcasted_iota(jnp.int32, value.shape, 0)
     return jnp.where(row < rank, value.astype(jnp.float32), 0.0).astype(jnp.bfloat16)
@@ -128,21 +132,18 @@
 
 
 def resid_kernel(scal, got_ref, u_ref, data_ref, *rest):
-    out_ref = rest[-1]
+    out_ref, placed = rest[-2:]
     slots = u_ref.shape[0]
     half = slots // 2
     col, odd, seat = scal[COL], scal[ODD], scal[SEAT]
-    real = jnp.zeros(data_ref.shape, jnp.float32)
-    imag = jnp.zeros(data_ref.shape, jnp.float32)
     for s in range(slots):
         column = (col + slots - s) & 3
         way = (col + slots - s) >> 2
         near = jnp.where(odd == 1, way == 0, way == 2)
         relay = jnp.logical_not(jnp.logical_or(near, way == 1)).astype(jnp.int32)
-        piece = got_ref[column + half * jnp.where(near, 1 - seat, seat), relay]
-        real += left_dot(u_ref[s, 0], piece)
-        imag += left_dot(u_ref[s, 1], piece)
-    image = real + turn(imag)
+        placed[s] = got_ref[column + half * jnp.where(near, 1 - seat, seat), relay]
+    values = placed[...].reshape(-1, placed.shape[-1])
+    image = left_dot(stacked(u_ref, 0), values) + turn(left_dot(stacked(u_ref, 1), values))
     resid = (image - data_ref[...].astype(jnp.float32)).astype(jnp.bfloat16)
     resid_turn = turn_bf(resid)
     for s in range(slots):
@@ -155,7 +156,7 @@
 
 
 def grad_kernel(
-    scal, size_ref, got_ref, v_ref, near_far_ref, last_far_ref, x_ref, out_ref, *, first
+    scal, size_ref, got_ref, v_ref, near_far_ref, last_far_ref, x_ref, out_ref, landed, *, first
 ):
     far_refs = (near_far_ref, last_far_ref)
     slots, _, levels, _ = v_ref.shape
@@ -163,15 +164,14 @@
     col, odd, seat = scal[COL], scal[ODD], scal[SEAT]
     parts, _, part, width = out_ref.shape
     shape = (parts * part, width)
-    real = jnp.zeros(shape, jnp.float32)
-    imag = jnp.zeros(shape, jnp.float32)
     for s in range(slots):
         column, same, near = outward(col, s, odd)
         piece = got_ref[column + half * jnp.where(same, seat, 1 - seat), 0]
         near = jnp.logical_and(near, scal[INNER] == 1)
-        piece = keep(piece, jnp.where(jnp.logical_or(same, near), levels, 0))
-        real += left_dot(v_ref[s, 0], piece)
-        imag += left_dot(v_ref[s, 1], piece)
+        landed[s] = keep(piece, jnp.where(jnp.logical_or(same, near), levels, 0))
+    values = landed[...].reshape(-1, width)
+    real = left_dot(stacked(v_ref, 0), values)
+    imag = left_dot(stacked(v_ref, 1), values)
     far_real = jnp.zeros(shape, jnp.float32)
     far_imag = jnp.zeros(shape, jnp.float32)
     for i in range(half):
@@ -205,7 +205,7 @@
             out_ref[f, side] = total
 
 
-def kernel_call(body, shape, scalars, *operands):
+def kernel_call(body, shape, scalars, *operands, scratch=()):
     smem = pl.BlockSpec(memory_space=pltpu.SMEM)
     vmem = pl.BlockSpec(memory_space=pltpu.VMEM)
     return pl.pallas_call(
@@ -213,6 +213,7 @@
         out_shape=jax.ShapeDtypeStruct(shape, jnp.bfloat16),
         in_specs=[smem] * len(scalars) + [vmem] * len(operands),
         out_specs=vmem,
+        scratch_shapes=[pltpu.VMEM(held, jnp.bfloat16) for held in scratch],
         compiler_params=pltpu.CompilerParams(vmem_limit_bytes=VMEM_BYTES),
     )(*scalars, *operands)
 
@@ -285,6 +286,7 @@
         ],
         compiler_params=pltpu.CompilerParams(vmem_limit_bytes=FIRST_VMEM_BYTES),
     )(v, model)
+    v, relay = lax.optimization_barrier((v, relay))
     relay = lax.ppermute(relay, "tile", swaps)
     fars = [
         lax.dynamic_slice_in_dim(v, half * odd + i, half // 2, 0) for i in (0, half // 2)
@@ -314,14 +316,18 @@
     )
     fars = [lax.ppermute(far, "tile", swaps) for far in fars]
     tiles = (slots, 2, levels, width)
+    pieces = [(slots, levels, width)]
     for step in range(ITERS):
         first = step == 0
         if first:
             coef = kernel_call(first_coef_kernel, tiles, [scal], v, model, relay)
-            back = kernel_call(resid_kernel, tiles, [scal], spread(coef), u, observed, fars[0])
+            early = (fars[0],)
         else:
             coef = kernel_call(coef_kernel, tiles, [scal], v, *fars, model)
-            back = kernel_call(resid_kernel, tiles, [scal], spread(coef), u, observed)
+            early = ()
+        back = kernel_call(
+            resid_kernel, tiles, [scal], spread(coef), u, observed, *early, scratch=pieces
+        )
         z = kernel_call(
             functools.partial(grad_kernel, first=first),
             (nfreq, 2, part, width),
@@ -330,6 +336,7 @@
             v,
             *fars,
             model,
+            scratch=pieces,
         )
         z = among_pair(z)
         if step == ITERS - 1:

time: 120 us -> 119 us (level)
  no operation moved by 1% of the time
where the time goes in v8:
time: 119 us; the launch traced here: 118 us
  blocking collectives  69.4 us (58%)
  starting transfers between devices  25.1 us (21%)
  Pallas kernels  11.1 us (9%)
  waiting for transfers between devices  8.62 us (7%)
  local copies, waits for them, and re-layouts  1.65 us (1%)
  other arithmetic  1.36 us (1%)
    all_to_all x3, blocking collectives, among_pair(): lax.all_to_all(flat, ('freq', 'tile'), 0, 0, tiled=True, axis_index_group...  37.2 us
    all_to_all x2, blocking collectives, spread(): lax.all_to_all(pieces, ('freq', 'tile'), 0, 0, tiled=True, axis_index_gro...  24.2 us
    all_to_all x2, starting transfers between devices, spread(): lax.all_to_all(pieces, ('freq', 'tile'), 0, 0, tiled=True, axis_index_gro...  12.8 us
    pallas_call x8, Pallas kernels, kernel_call(): pl.pallas_call(body, out_shape=jax.ShapeDtypeStruct(shape, jnp.bfloat16),...  9.34 us
    ppermute x2, starting transfers between devices, on_device(): fars = [lax.ppermute(far, 'tile', swaps) for far in fars]  8.43 us
    all_to_all x1, blocking collectives, on_device(): model = lax.all_to_all(mixed[:, 0], 'freq', 0, 0, tiled=True)  8.04 us
    ppermute x2, waiting for transfers between devices, on_device(): fars = [lax.ppermute(far, 'tile', swaps) for far in fars]  8.01 us
    ppermute x1, starting transfers between devices, on_device(): relay = lax.ppermute(relay, 'tile', swaps)  3.82 us
  transfers between devices with their start and end apart: 5, of which 3 were waited for; matrix products, arithmetic and copies ran while one was open for 1% of the time, Pallas kernels for 0%

profile of v8, /device:TPU:64, one launch (start us, length us, event | category | flops | bytes accessed | tf_op | source)
XLA Modules:
  0.0 118.2 jit_solution(1908861335793685432)
XLA Ops:
  0.0 1.8 %shard_map.73 = bf16[4,112,128]{2,1,0:T(8,128)(2,1)S(1)} custom-call(bf16[8,2,112,256]{3,2,1,0:T(8,128)(2,1)} %bitcast.28, f32[256,128]{1,0:T(8,128)} %bitcast.36), custom_call_target="tpu_custom_call" | custom-call | tf_op jit(solution)/shard_map/pallas_call | solution.py:277
  1.8 3.8 %collective-permute-start = (bf16[4,112,128]{2,1,0:T(8,128)(2,1)S(1)}, bf16[4,112,128]{2,1,0:T(8,128)(2,1)S(1)}, u32[]{:S(2)}, u32[]{:S(2)}) collective-permute-start(bf16[4,112,128]{2,1,0:T(8,128)(2,1)S(1)} %shard_map.73), channel_id=1, source_target_pairs={{0,4},{1,5},{2,6},{3,7},{4,0},{5,1},{6,2},{7,3},{8,12},{9,13},{10,... | collective-permute-start | bytes 344072 | tf_op jit(solution)/shard_map/ppermute | solution.py:290
  5.8 0.7 copy-done.4
  6.8 0.5 copy-done.5
  8.2 0.6 collective-permute-done.relay_ref
  8.8 1.8 %shard_map.74 = bf16[8,2,112,128]{3,2,1,0:T(8,128)(2,1)} custom-call(s32[24]{0:T(128)S(1)} %concatenate.9.scal, bf16[8,2,112,256]{3,2,1,0:T(8,128)(2,1)S(1)} %bitcast.30, f32[256,128]{1,0:T(8,128)S(1)} %bitcast.37, bf16[4,112,128]{2,1,0:T(8,128)(2,1)S(1)} %collective-permute-done.relay_ref), custom_call_target="tpu_custom_call" | custom-call | tf_op jit(solution)/shard_map/pallas_call | solution.py:211
  10.6 6.8 %all-to-all-start = ((bf16[8,2,112,128]{3,2,1,0:T(8,128)(2,1)}), bf16[8,2,112,128]{3,2,1,0:T(8,128)(2,1)S(1)}, u32[]{:S(2)}, u32[]{:S(2)}) async-start(bf16[8,2,112,128]{3,2,1,0:T(8,128)(2,1)} %shard_map.74), calls=%async_computation | async-start | bytes 917504 | tf_op jit(solution)/shard_map/all_to_all | solution.py:259
  17.4 4.1 %collective-permute-start.1 = (bf16[2,2,112,256]{3,2,1,0:T(8,128)(2,1)S(1)}, bf16[2,2,112,256]{3,2,1,0:T(8,128)(2,1)S(1)}, u32[]{:S(2)}, u32[]{:S(2)}) collective-permute-start(bf16[2,2,112,256]{3,2,1,0:T(8,128)(2,1)S(1)} %get-tuple-element.18), channel_id=1, source_target_pairs={{0,4},{1,5},{2,6},{3,7},{4,0},{5,1},{6,2},{7,3},{8,12},{9,13},{10,... | collective-permute-start | bytes 688136 | tf_op jit(solution)/shard_map/ppermute | solution.py:317
  21.5 4.6 %collective-permute-done.1.rest_0_.near_far_ref = bf16[2,2,112,256]{3,2,1,0:T(8,128)(2,1)S(1)} collective-permute-done((bf16[2,2,112,256]{3,2,1,0:T(8,128)(2,1)S(1)}, bf16[2,2,112,256]{3,2,1,0:T(8,128)(2,1)S(1)}, u32[]{:S(2)}, u32[]{:S(2)}) %collective-permute-start.1) | collective-permute-done | bytes 229408 | tf_op jit(solution)/shard_map/ppermute | solution.py:317
  26.2 2.2 %shard_map.75 = bf16[8,2,112,128]{3,2,1,0:T(8,128)(2,1)} custom-call(s32[24]{0:T(128)S(1)} %concatenate.9.scal, bf16[8,2,112,128]{3,2,1,0:T(8,128)(2,1)S(1)} %all-to-all-done.got_ref, bf16[8,2,112,256]{3,2,1,0:T(8,128)(2,1)S(1)} %bitcast.34, bf16[256,128]{1,0:T(8,128)(2,1)S(1)} %bitcast.46, ...), custom_call_target="tpu_custom_call" | custom-call | tf_op jit(solution)/shard_map/pallas_call | solution.py:211
  28.4 6.0 %all-to-all-start.1 = ((bf16[8,2,112,128]{3,2,1,0:T(8,128)(2,1)}), bf16[8,2,112,128]{3,2,1,0:T(8,128)(2,1)S(1)}, u32[]{:S(2)}, u32[]{:S(2)}) async-start(bf16[8,2,112,128]{3,2,1,0:T(8,128)(2,1)} %shard_map.75), calls=%async_computation.1 | async-start | bytes 917504 | tf_op jit(solution)/shard_map/all_to_all | solution.py:259
  34.4 4.3 %collective-permute-start.2 = (bf16[2,2,112,256]{3,2,1,0:T(8,128)(2,1)S(1)}, bf16[2,2,112,256]{3,2,1,0:T(8,128)(2,1)S(1)}, u32[]{:S(2)}, u32[]{:S(2)}) collective-permute-start(bf16[2,2,112,256]{3,2,1,0:T(8,128)(2,1)S(1)} %get-tuple-element.19), channel_id=1, source_target_pairs={{0,4},{1,5},{2,6},{3,7},{4,0},{5,1},{6,2},{7,3},{8,12},{9,13},{10,... | collective-permute-start | bytes 688136 | tf_op jit(solution)/shard_map/ppermute | solution.py:317
  39.3 3.4 %collective-permute-done.2.last_far_ref = bf16[2,2,112,256]{3,2,1,0:T(8,128)(2,1)S(1)} collective-permute-done((bf16[2,2,112,256]{3,2,1,0:T(8,128)(2,1)S(1)}, bf16[2,2,112,256]{3,2,1,0:T(8,128)(2,1)S(1)}, u32[]{:S(2)}, u32[]{:S(2)}) %collective-permute-start.2) | collective-permute-done | bytes 229408 | tf_op jit(solution)/shard_map/ppermute | solution.py:317
  42.7 1.2 %shard_map.76 = bf16[8,2,32,128]{3,2,1,0:T(8,128)(2,1)S(1)} custom-call(s32[24]{0:T(128)S(1)} %concatenate.9.scal, f32[1]{0:T(128)S(6)} %copy.8.size_ref, bf16[8,2,112,128]{3,2,1,0:T(8,128)(2,1)S(1)} %all-to-all-done.1.got_ref, bf16[8,2,112,256]{3,2,1,0:T(8,128)(2,1)S(1)} %bitcast.31, ...), custom_call_target="tpu_custom_call" | custom-call | tf_op jit(solution)/shard_map/pallas_call | solution.py:211
  43.9 13.6 %all_to_all.40 = bf16[16,32,128]{2,1,0:T(8,128)(2,1)S(1)} all-to-all(bf16[16,32,128]{2,1,0:T(8,128)(2,1)S(1)} %bitcast.45), channel_id=1, replica_groups={{0,4,64,68,128,132,192,196,256,260,320,324,384,388,448,452},{1,5,65,69,..., dimensions={0} | all-to-all | bytes 262144 | tf_op jit(solution)/shard_map/all_to_all | solution.py:265
  57.7 9.2 %all_to_all.41 = bf16[16,32,128]{2,1,0:T(8,128)(2,1)S(1)} all-to-all(bf16[16,32,128]{2,1,0:T(8,128)(2,1)S(1)} %bitcast.43), channel_id=1, replica_groups={{0,4,64,68,128,132,192,196,256,260,320,324,384,388,448,452},{1,5,65,69,..., dimensions={0} | all-to-all | bytes 262144 | tf_op jit(solution)/shard_map/all_to_all | solution.py:265
  66.9 1.1 shard_map.78
  68.0 13.0 %all_to_all.42.got_ref = bf16[8,2,112,128]{3,2,1,0:T(8,128)(2,1)S(1)} all-to-all(bf16[8,2,112,128]{3,2,1,0:T(8,128)(2,1)S(1)} %shard_map.78), channel_id=1, replica_groups={{4,5,6,7,8,9,10,11},{12,13,14,15,16,17,18,19},{20,21,22,23,24,25,26,27}..., dimensions={0} | all-to-all | bytes 917504 | tf_op jit(solution)/shard_map/all_to_all | solution.py:259
  81.0 1.5 %shard_map.79 = bf16[8,2,112,128]{3,2,1,0:T(8,128)(2,1)S(1)} custom-call(s32[24]{0:T(128)S(1)} %concatenate.9.scal, bf16[8,2,112,128]{3,2,1,0:T(8,128)(2,1)S(1)} %all_to_all.42.got_ref, bf16[8,2,112,256]{3,2,1,0:T(8,128)(2,1)S(1)} %bitcast.35, bf16[256,128]{1,0:T(8,128)(2,1)S(1)} %bitcast.47), custom_call_target="tpu_custom_call" | custom-call | tf_op jit(solution)/shard_map/pallas_call | solution.py:211
  82.4 11.2 %all_to_all.43.got_ref = bf16[8,2,112,128]{3,2,1,0:T(8,128)(2,1)S(1)} all-to-all(bf16[8,2,112,128]{3,2,1,0:T(8,128)(2,1)S(1)} %shard_map.79), channel_id=1, replica_groups={{4,5,6,7,8,9,10,11},{12,13,14,15,16,17,18,19},{20,21,22,23,24,25,26,27}..., dimensions={0} | all-to-all | bytes 917504 | tf_op jit(solution)/shard_map/all_to_all | solution.py:259
  93.6 1.2 %shard_map.80 = bf16[8,2,32,128]{3,2,1,0:T(8,128)(2,1)S(1)} custom-call(s32[24]{0:T(128)S(1)} %concatenate.9.scal, f32[1]{0:T(128)S(6)} %copy.8.size_ref, bf16[8,2,112,128]{3,2,1,0:T(8,128)(2,1)S(1)} %all_to_all.43.got_ref, bf16[8,2,112,256]{3,2,1,0:T(8,128)(2,1)S(1)} %bitcast.33, bf16[2,2,112,256]{3,2,1,0:T(8,128)(2,1)S(1)} %collective-permute-done.1.rest_0_.near_far_ref, ...), custom_call_target="tpu_custom_call" | custom-call | tf_op jit(solution)/shard_map/pallas_call | solution.py:211
  94.8 14.5 %all_to_all.44 = bf16[16,32,128]{2,1,0:T(8,128)(2,1)S(1)} all-to-all(bf16[16,32,128]{2,1,0:T(8,128)(2,1)S(1)} %bitcast.44), channel_id=1, replica_groups={{0,4,64,68,128,132,192,196,256,260,320,324,384,388,448,452},{1,5,65,69,..., dimensions={0} | all-to-all | bytes 262144 | tf_op jit(solution)/shard_map/all_to_all | solution.py:265
  109.5 8.0 %all_to_all.45 = bf16[8,32,128]{2,1,0:T(8,128)(2,1)S(1)} all-to-all(bf16[8,32,128]{2,1,0:T(8,128)(2,1)S(1)} %bitcast.48), channel_id=1, replica_groups=mesh['freq'=8,'tile'=64] {'freq'}, dimensions={0} | all-to-all | bytes 131072 | tf_op jit(solution)/shard_map/all_to_all | solution.py:344
  117.5 0.7 bitcast_convert_fusion
  (28 shorter events, 1.6 us)
Async XLA Ops:
  0.0 7.4 %copy-start = (bf16[1,8,2,112,256]{4,3,2,1,0:T(8,128)(2,1)S(1)}, bf16[1,8,2,112,256]{4,3,2,1,0:T(8,128)(2,1)}, u32[]{:S(2)}) copy-start(bf16[1,8,2,112,256]{4,3,2,1,0:T(8,128)(2,1)} %param.9) | copy-start | bytes 2752516
  1.8 7.0 %collective-permute-start = (bf16[4,112,128]{2,1,0:T(8,128)(2,1)S(1)}, bf16[4,112,128]{2,1,0:T(8,128)(2,1)S(1)}, u32[]{:S(2)}, u32[]{:S(2)}) collective-permute-start(bf16[4,112,128]{2,1,0:T(8,128)(2,1)S(1)} %shard_map.73), channel_id=1, source_target_pairs={{0,4},{1,5},{2,6},{3,7},{4,0},{5,1},{6,2},{7,3},{8,12},{9,13},{10,... | collective-permute-start | bytes 344072 | tf_op jit(solution)/shard_map/ppermute | solution.py:290
  5.8 0.7 copy-start.4
  6.6 0.7 copy-start.5
  7.4 1.3 %copy-start.2 = (f32[1,256,128]{2,1,0:T(8,128)S(1)}, f32[1,256,128]{2,1,0:T(8,128)}, u32[]{:S(2)}) copy-start(f32[1,256,128]{2,1,0:T(8,128)} %param.7) | copy-start | bytes 393220
  8.8 17.4 %copy-start.1 = (bf16[1,8,2,112,256]{4,3,2,1,0:T(8,128)(2,1)S(1)}, bf16[1,8,2,112,256]{4,3,2,1,0:T(8,128)(2,1)}, u32[]{:S(2)}) copy-start(bf16[1,8,2,112,256]{4,3,2,1,0:T(8,128)(2,1)} %param.10) | copy-start | bytes 2752516
  10.6 15.6 %copy-start.3 = (bf16[1,256,128]{2,1,0:T(8,128)(2,1)S(1)}, bf16[1,256,128]{2,1,0:T(8,128)(2,1)}, u32[]{:S(2)}) copy-start(bf16[1,256,128]{2,1,0:T(8,128)(2,1)} %param.8) | copy-start | bytes 196612
  10.6 15.6 %all-to-all-start = ((bf16[8,2,112,128]{3,2,1,0:T(8,128)(2,1)}), bf16[8,2,112,128]{3,2,1,0:T(8,128)(2,1)S(1)}, u32[]{:S(2)}, u32[]{:S(2)}) async-start(bf16[8,2,112,128]{3,2,1,0:T(8,128)(2,1)} %shard_map.74), calls=%async_computation | async-start | bytes 917504 | tf_op jit(solution)/shard_map/all_to_all | solution.py:259
  17.4 8.8 %collective-permute-start.1 = (bf16[2,2,112,256]{3,2,1,0:T(8,128)(2,1)S(1)}, bf16[2,2,112,256]{3,2,1,0:T(8,128)(2,1)S(1)}, u32[]{:S(2)}, u32[]{:S(2)}) collective-permute-start(bf16[2,2,112,256]{3,2,1,0:T(8,128)(2,1)S(1)} %get-tuple-element.18), channel_id=1, source_target_pairs={{0,4},{1,5},{2,6},{3,7},{4,0},{5,1},{6,2},{7,3},{8,12},{9,13},{10,... | collective-permute-start | bytes 688136 | tf_op jit(solution)/shard_map/ppermute | solution.py:317
  28.4 14.3 %all-to-all-start.1 = ((bf16[8,2,112,128]{3,2,1,0:T(8,128)(2,1)}), bf16[8,2,112,128]{3,2,1,0:T(8,128)(2,1)S(1)}, u32[]{:S(2)}, u32[]{:S(2)}) async-start(bf16[8,2,112,128]{3,2,1,0:T(8,128)(2,1)} %shard_map.75), calls=%async_computation.1 | async-start | bytes 917504 | tf_op jit(solution)/shard_map/all_to_all | solution.py:259
  34.4 8.3 %collective-permute-start.2 = (bf16[2,2,112,256]{3,2,1,0:T(8,128)(2,1)S(1)}, bf16[2,2,112,256]{3,2,1,0:T(8,128)(2,1)S(1)}, u32[]{:S(2)}, u32[]{:S(2)}) collective-permute-start(bf16[2,2,112,256]{3,2,1,0:T(8,128)(2,1)S(1)} %get-tuple-element.19), channel_id=1, source_target_pairs={{0,4},{1,5},{2,6},{3,7},{4,0},{5,1},{6,2},{7,3},{8,12},{9,13},{10,... | collective-permute-start | bytes 688136 | tf_op jit(solution)/shard_map/ppermute | solution.py:317

commit v9 on v8

--- a/solution.py
+++ b/solution.py
@@ -200,17 +200,17 @@
         total = jnp.zeros_like(z[0])
         for g in range(count):
             total += re_ref[f, g : g + 1, :] * z[g] + im_ref[f, g : g + 1, :] * z_turn[g]
-        total = total.astype(jnp.bfloat16)
+        total = total.astype(out_ref.dtype)
         for side in range(out_ref.shape[1]):
             out_ref[f, side] = total
 
 
-def kernel_call(body, shape, scalars, *operands, scratch=()):
+def kernel_call(body, shape, scalars, *operands, scratch=(), dtype=jnp.bfloat16):
     smem = pl.BlockSpec(memory_space=pltpu.SMEM)
     vmem = pl.BlockSpec(memory_space=pltpu.VMEM)
     return pl.pallas_call(
         body,
-        out_shape=jax.ShapeDtypeStruct(shape, jnp.bfloat16),
+        out_shape=jax.ShapeDtypeStruct(shape, dtype),
         in_specs=[smem] * len(scalars) + [vmem] * len(operands),
         out_specs=vmem,
         scratch_shapes=[pltpu.VMEM(held, jnp.bfloat16) for held in scratch],
@@ -340,7 +340,15 @@
         )
         z = among_pair(z)
         if step == ITERS - 1:
-            mixed = kernel_call(mix_kernel, (nfreq, 1, part, width), [], gate_re, gate_im, z)
+            mixed = kernel_call(
+                mix_kernel,
+                (nfreq, 1, part, width),
+                [],
+                gate_re,
+                gate_im,
+                z,
+                dtype=jnp.float32,
+            )
             model = lax.all_to_all(mixed[:, 0], "freq", 0, 0, tiled=True)
         else:
             mixed = kernel_call(mix_kernel, z.shape, [], gate_re, gate_im, z)

time: 119 us -> 119 us (level)
  no operation moved by 1% of the time
where the time goes in v9:
time: 119 us
  blocking collectives  70 us (59%)
  starting transfers between devices  25.1 us (21%)
  Pallas kernels  11.1 us (9%)
  waiting for transfers between devices  8.62 us (7%)
  local copies, waits for them, and re-layouts  2.31 us (2%)
    all_to_all x3, blocking collectives, among_pair(): lax.all_to_all(flat, ('freq', 'tile'), 0, 0, tiled=True, axis_index_group...  37.2 us
    all_to_all x2, blocking collectives, spread(): lax.all_to_all(pieces, ('freq', 'tile'), 0, 0, tiled=True, axis_index_gro...  24.2 us
    all_to_all x2, starting transfers between devices, spread(): lax.all_to_all(pieces, ('freq', 'tile'), 0, 0, tiled=True, axis_index_gro...  12.8 us
    pallas_call x8, Pallas kernels, kernel_call(): pl.pallas_call(body, out_shape=jax.ShapeDtypeStruct(shape, dtype), in_spe...  9.34 us
    all_to_all x1, blocking collectives, on_device(): model = lax.all_to_all(mixed[:, 0], 'freq', 0, 0, tiled=True)  8.56 us
    ppermute x2, starting transfers between devices, on_device(): fars = [lax.ppermute(far, 'tile', swaps) for far in fars]  8.43 us
    ppermute x2, waiting for transfers between devices, on_device(): fars = [lax.ppermute(far, 'tile', swaps) for far in fars]  8.01 us
    ppermute x1, starting transfers between devices, on_device(): relay = lax.ppermute(relay, 'tile', swaps)  3.82 us
  transfers between devices with their start and end apart: 5, of which 3 were waited for; matrix products, arithmetic and copies ran while one was open for 1% of the time, Pallas kernels for 0%

profile of v9, /device:TPU:64, one launch (start us, length us, event | category | flops | bytes accessed | tf_op | source)
XLA Modules:
  0.0 118.7 jit_solution(17240106241109031174)
XLA Ops:
  0.0 1.8 %shard_map.73 = bf16[4,112,128]{2,1,0:T(8,128)(2,1)S(1)} custom-call(bf16[8,2,112,256]{3,2,1,0:T(8,128)(2,1)} %bitcast.25, f32[256,128]{1,0:T(8,128)} %bitcast.33), custom_call_target="tpu_custom_call" | custom-call | tf_op jit(solution)/shard_map/pallas_call | solution.py:277
  1.8 3.8 %collective-permute-start = (bf16[4,112,128]{2,1,0:T(8,128)(2,1)S(1)}, bf16[4,112,128]{2,1,0:T(8,128)(2,1)S(1)}, u32[]{:S(2)}, u32[]{:S(2)}) collective-permute-start(bf16[4,112,128]{2,1,0:T(8,128)(2,1)S(1)} %shard_map.73), channel_id=1, source_target_pairs={{0,4},{1,5},{2,6},{3,7},{4,0},{5,1},{6,2},{7,3},{8,12},{9,13},{10,... | collective-permute-start | bytes 344072 | tf_op jit(solution)/shard_map/ppermute | solution.py:290
  5.8 0.7 copy-done.4
  6.8 0.5 copy-done.5
  8.2 0.6 collective-permute-done.relay_ref
  8.8 1.8 %shard_map.74 = bf16[8,2,112,128]{3,2,1,0:T(8,128)(2,1)} custom-call(s32[24]{0:T(128)S(1)} %concatenate.9.scal, bf16[8,2,112,256]{3,2,1,0:T(8,128)(2,1)S(1)} %bitcast.27, f32[256,128]{1,0:T(8,128)S(1)} %bitcast.34, bf16[4,112,128]{2,1,0:T(8,128)(2,1)S(1)} %collective-permute-done.relay_ref), custom_call_target="tpu_custom_call" | custom-call | tf_op jit(solution)/shard_map/pallas_call | solution.py:211
  10.6 6.8 %all-to-all-start = ((bf16[8,2,112,128]{3,2,1,0:T(8,128)(2,1)}), bf16[8,2,112,128]{3,2,1,0:T(8,128)(2,1)S(1)}, u32[]{:S(2)}, u32[]{:S(2)}) async-start(bf16[8,2,112,128]{3,2,1,0:T(8,128)(2,1)} %shard_map.74), calls=%async_computation | async-start | bytes 917504 | tf_op jit(solution)/shard_map/all_to_all | solution.py:259
  17.4 4.1 %collective-permute-start.1 = (bf16[2,2,112,256]{3,2,1,0:T(8,128)(2,1)S(1)}, bf16[2,2,112,256]{3,2,1,0:T(8,128)(2,1)S(1)}, u32[]{:S(2)}, u32[]{:S(2)}) collective-permute-start(bf16[2,2,112,256]{3,2,1,0:T(8,128)(2,1)S(1)} %get-tuple-element.18), channel_id=1, source_target_pairs={{0,4},{1,5},{2,6},{3,7},{4,0},{5,1},{6,2},{7,3},{8,12},{9,13},{10,... | collective-permute-start | bytes 688136 | tf_op jit(solution)/shard_map/ppermute | solution.py:317
  21.5 4.6 %collective-permute-done.1.rest_0_.near_far_ref = bf16[2,2,112,256]{3,2,1,0:T(8,128)(2,1)S(1)} collective-permute-done((bf16[2,2,112,256]{3,2,1,0:T(8,128)(2,1)S(1)}, bf16[2,2,112,256]{3,2,1,0:T(8,128)(2,1)S(1)}, u32[]{:S(2)}, u32[]{:S(2)}) %collective-permute-start.1) | collective-permute-done | bytes 229408 | tf_op jit(solution)/shard_map/ppermute | solution.py:317
  26.2 2.2 %shard_map.75 = bf16[8,2,112,128]{3,2,1,0:T(8,128)(2,1)} custom-call(s32[24]{0:T(128)S(1)} %concatenate.9.scal, bf16[8,2,112,128]{3,2,1,0:T(8,128)(2,1)S(1)} %all-to-all-done.got_ref, bf16[8,2,112,256]{3,2,1,0:T(8,128)(2,1)S(1)} %bitcast.31, bf16[256,128]{1,0:T(8,128)(2,1)S(1)} %bitcast.44, ...), custom_call_target="tpu_custom_call" | custom-call | tf_op jit(solution)/shard_map/pallas_call | solution.py:211
  28.4 6.0 %all-to-all-start.1 = ((bf16[8,2,112,128]{3,2,1,0:T(8,128)(2,1)}), bf16[8,2,112,128]{3,2,1,0:T(8,128)(2,1)S(1)}, u32[]{:S(2)}, u32[]{:S(2)}) async-start(bf16[8,2,112,128]{3,2,1,0:T(8,128)(2,1)} %shard_map.75), calls=%async_computation.1 | async-start | bytes 917504 | tf_op jit(solution)/shard_map/all_to_all | solution.py:259
  34.4 4.3 %collective-permute-start.2 = (bf16[2,2,112,256]{3,2,1,0:T(8,128)(2,1)S(1)}, bf16[2,2,112,256]{3,2,1,0:T(8,128)(2,1)S(1)}, u32[]{:S(2)}, u32[]{:S(2)}) collective-permute-start(bf16[2,2,112,256]{3,2,1,0:T(8,128)(2,1)S(1)} %get-tuple-element.19), channel_id=1, source_target_pairs={{0,4},{1,5},{2,6},{3,7},{4,0},{5,1},{6,2},{7,3},{8,12},{9,13},{10,... | collective-permute-start | bytes 688136 | tf_op jit(solution)/shard_map/ppermute | solution.py:317
  39.3 3.4 %collective-permute-done.2.last_far_ref = bf16[2,2,112,256]{3,2,1,0:T(8,128)(2,1)S(1)} collective-permute-done((bf16[2,2,112,256]{3,2,1,0:T(8,128)(2,1)S(1)}, bf16[2,2,112,256]{3,2,1,0:T(8,128)(2,1)S(1)}, u32[]{:S(2)}, u32[]{:S(2)}) %collective-permute-start.2) | collective-permute-done | bytes 229408 | tf_op jit(solution)/shard_map/ppermute | solution.py:317
  42.7 1.2 %shard_map.76 = bf16[8,2,32,128]{3,2,1,0:T(8,128)(2,1)S(1)} custom-call(s32[24]{0:T(128)S(1)} %concatenate.9.scal, f32[1]{0:T(128)S(6)} %copy.9.size_ref, bf16[8,2,112,128]{3,2,1,0:T(8,128)(2,1)S(1)} %all-to-all-done.1.got_ref, bf16[8,2,112,256]{3,2,1,0:T(8,128)(2,1)S(1)} %bitcast.28, ...), custom_call_target="tpu_custom_call" | custom-call | tf_op jit(solution)/shard_map/pallas_call | solution.py:211
  43.9 13.6 %all_to_all.40 = bf16[16,32,128]{2,1,0:T(8,128)(2,1)S(1)} all-to-all(bf16[16,32,128]{2,1,0:T(8,128)(2,1)S(1)} %bitcast.43), channel_id=1, replica_groups={{0,4,64,68,128,132,192,196,256,260,320,324,384,388,448,452},{1,5,65,69,..., dimensions={0} | all-to-all | bytes 262144 | tf_op jit(solution)/shard_map/all_to_all | solution.py:265
  57.7 9.2 %all_to_all.41 = bf16[16,32,128]{2,1,0:T(8,128)(2,1)S(1)} all-to-all(bf16[16,32,128]{2,1,0:T(8,128)(2,1)S(1)} %bitcast.41), channel_id=1, replica_groups={{0,4,64,68,128,132,192,196,256,260,320,324,384,388,448,452},{1,5,65,69,..., dimensions={0} | all-to-all | bytes 262144 | tf_op jit(solution)/shard_map/all_to_all | solution.py:265
  66.9 1.1 shard_map.78
  68.0 13.0 %all_to_all.42.got_ref = bf16[8,2,112,128]{3,2,1,0:T(8,128)(2,1)S(1)} all-to-all(bf16[8,2,112,128]{3,2,1,0:T(8,128)(2,1)S(1)} %shard_map.78), channel_id=1, replica_groups={{4,5,6,7,8,9,10,11},{12,13,14,15,16,17,18,19},{20,21,22,23,24,25,26,27}..., dimensions={0} | all-to-all | bytes 917504 | tf_op jit(solution)/shard_map/all_to_all | solution.py:259
  81.0 1.5 %shard_map.79 = bf16[8,2,112,128]{3,2,1,0:T(8,128)(2,1)S(1)} custom-call(s32[24]{0:T(128)S(1)} %concatenate.9.scal, bf16[8,2,112,128]{3,2,1,0:T(8,128)(2,1)S(1)} %all_to_all.42.got_ref, bf16[8,2,112,256]{3,2,1,0:T(8,128)(2,1)S(1)} %bitcast.32, bf16[256,128]{1,0:T(8,128)(2,1)S(1)} %bitcast.45), custom_call_target="tpu_custom_call" | custom-call | tf_op jit(solution)/shard_map/pallas_call | solution.py:211
  82.4 11.2 %all_to_all.43.got_ref = bf16[8,2,112,128]{3,2,1,0:T(8,128)(2,1)S(1)} all-to-all(bf16[8,2,112,128]{3,2,1,0:T(8,128)(2,1)S(1)} %shard_map.79), channel_id=1, replica_groups={{4,5,6,7,8,9,10,11},{12,13,14,15,16,17,18,19},{20,21,22,23,24,25,26,27}..., dimensions={0} | all-to-all | bytes 917504 | tf_op jit(solution)/shard_map/all_to_all | solution.py:259
  93.6 1.2 %shard_map.80 = bf16[8,2,32,128]{3,2,1,0:T(8,128)(2,1)S(1)} custom-call(s32[24]{0:T(128)S(1)} %concatenate.9.scal, f32[1]{0:T(128)S(6)} %copy.9.size_ref, bf16[8,2,112,128]{3,2,1,0:T(8,128)(2,1)S(1)} %all_to_all.43.got_ref, bf16[8,2,112,256]{3,2,1,0:T(8,128)(2,1)S(1)} %bitcast.30, bf16[2,2,112,256]{3,2,1,0:T(8,128)(2,1)S(1)} %collective-permute-done.1.rest_0_.near_far_ref, ...), custom_call_target="tpu_custom_call" | custom-call | tf_op jit(solution)/shard_map/pallas_call | solution.py:211
  94.8 14.5 %all_to_all.44 = bf16[16,32,128]{2,1,0:T(8,128)(2,1)S(1)} all-to-all(bf16[16,32,128]{2,1,0:T(8,128)(2,1)S(1)} %bitcast.42), channel_id=1, replica_groups={{0,4,64,68,128,132,192,196,256,260,320,324,384,388,448,452},{1,5,65,69,..., dimensions={0} | all-to-all | bytes 262144 | tf_op jit(solution)/shard_map/all_to_all | solution.py:265
  109.5 8.6 %all_to_all.45 = f32[8,32,128]{2,1,0:T(8,128)S(1)} all-to-all(f32[8,32,128]{2,1,0:T(8,128)S(1)} %bitcast.39), channel_id=1, replica_groups=mesh['freq'=8,'tile'=64] {'freq'}, dimensions={0} | all-to-all | bytes 262144 | tf_op jit(solution)/shard_map/all_to_all | solution.py:352
  118.1 0.7 copy.10
  (28 shorter events, 1.6 us)
Async XLA Ops:
  0.0 7.4 %copy-start = (bf16[1,8,2,112,256]{4,3,2,1,0:T(8,128)(2,1)S(1)}, bf16[1,8,2,112,256]{4,3,2,1,0:T(8,128)(2,1)}, u32[]{:S(2)}) copy-start(bf16[1,8,2,112,256]{4,3,2,1,0:T(8,128)(2,1)} %param.9) | copy-start | bytes 2752516
  1.8 7.0 %collective-permute-start = (bf16[4,112,128]{2,1,0:T(8,128)(2,1)S(1)}, bf16[4,112,128]{2,1,0:T(8,128)(2,1)S(1)}, u32[]{:S(2)}, u32[]{:S(2)}) collective-permute-start(bf16[4,112,128]{2,1,0:T(8,128)(2,1)S(1)} %shard_map.73), channel_id=1, source_target_pairs={{0,4},{1,5},{2,6},{3,7},{4,0},{5,1},{6,2},{7,3},{8,12},{9,13},{10,... | collective-permute-start | bytes 344072 | tf_op jit(solution)/shard_map/ppermute | solution.py:290
  5.8 0.7 copy-start.4
  6.6 0.7 copy-start.5
  7.4 1.3 %copy-start.2 = (f32[1,256,128]{2,1,0:T(8,128)S(1)}, f32[1,256,128]{2,1,0:T(8,128)}, u32[]{:S(2)}) copy-start(f32[1,256,128]{2,1,0:T(8,128)} %param.7) | copy-start | bytes 393220
  8.8 17.4 %copy-start.1 = (bf16[1,8,2,112,256]{4,3,2,1,0:T(8,128)(2,1)S(1)}, bf16[1,8,2,112,256]{4,3,2,1,0:T(8,128)(2,1)}, u32[]{:S(2)}) copy-start(bf16[1,8,2,112,256]{4,3,2,1,0:T(8,128)(2,1)} %param.10) | copy-start | bytes 2752516
  10.6 15.6 %copy-start.3 = (bf16[1,256,128]{2,1,0:T(8,128)(2,1)S(1)}, bf16[1,256,128]{2,1,0:T(8,128)(2,1)}, u32[]{:S(2)}) copy-start(bf16[1,256,128]{2,1,0:T(8,128)(2,1)} %param.8) | copy-start | bytes 196612
  10.6 15.6 %all-to-all-start = ((bf16[8,2,112,128]{3,2,1,0:T(8,128)(2,1)}), bf16[8,2,112,128]{3,2,1,0:T(8,128)(2,1)S(1)}, u32[]{:S(2)}, u32[]{:S(2)}) async-start(bf16[8,2,112,128]{3,2,1,0:T(8,128)(2,1)} %shard_map.74), calls=%async_computation | async-start | bytes 917504 | tf_op jit(solution)/shard_map/all_to_all | solution.py:259
  17.4 8.8 %collective-permute-start.1 = (bf16[2,2,112,256]{3,2,1,0:T(8,128)(2,1)S(1)}, bf16[2,2,112,256]{3,2,1,0:T(8,128)(2,1)S(1)}, u32[]{:S(2)}, u32[]{:S(2)}) collective-permute-start(bf16[2,2,112,256]{3,2,1,0:T(8,128)(2,1)S(1)} %get-tuple-element.18), channel_id=1, source_target_pairs={{0,4},{1,5},{2,6},{3,7},{4,0},{5,1},{6,2},{7,3},{8,12},{9,13},{10,... | collective-permute-start | bytes 688136 | tf_op jit(solution)/shard_map/ppermute | solution.py:317
  28.4 14.3 %all-to-all-start.1 = ((bf16[8,2,112,128]{3,2,1,0:T(8,128)(2,1)}), bf16[8,2,112,128]{3,2,1,0:T(8,128)(2,1)S(1)}, u32[]{:S(2)}, u32[]{:S(2)}) async-start(bf16[8,2,112,128]{3,2,1,0:T(8,128)(2,1)} %shard_map.75), calls=%async_computation.1 | async-start | bytes 917504 | tf_op jit(solution)/shard_map/all_to_all | solution.py:259
  34.4 8.3 %collective-permute-start.2 = (bf16[2,2,112,256]{3,2,1,0:T(8,128)(2,1)S(1)}, bf16[2,2,112,256]{3,2,1,0:T(8,128)(2,1)S(1)}, u32[]{:S(2)}, u32[]{:S(2)}) collective-permute-start(bf16[2,2,112,256]{3,2,1,0:T(8,128)(2,1)S(1)} %get-tuple-element.19), channel_id=1, source_target_pairs={{0,4},{1,5},{2,6},{3,7},{4,0},{5,1},{6,2},{7,3},{8,12},{9,13},{10,... | collective-permute-start | bytes 688136 | tf_op jit(solution)/shard_map/ppermute | solution.py:317
